TPU v7x, 32 devices: a whole 2x2x4 slice. The times are simulated.
32 devices in a mesh: dp: 16 (over z, x, core), tensor: 2 (over y).
Axes of the slice: x: 2, y: 2, z: 4, core: 2. Of those that a mesh axis runs over, the one named last changes fastest.
Arguments:
- short_tokens: bfloat16 [128, 64, 768], P('dp'), may hold values from -6 to 6
- long_tokens: bfloat16 [128, 256, 768], P('dp'), may hold values from -6 to 6
- short_cotangent: bfloat16 [128, 64, 768], P('dp'), may hold values from -6 to 6
- long_cotangent: bfloat16 [128, 256, 768], P('dp'), may hold values from -6 to 6
- short_lengths: int32 [128], P('dp'), may hold values from 1 to 64, 6144 in all
- long_lengths: int32 [128], P('dp'), may hold values from 1 to 256, 24576 in all
- queries: bfloat16 [256, 768], P('dp'), may hold values from -0.4375 to 0.4375
- positives: int32 [256], P('dp'), may hold values from 0 to 255, each once
- step_count: int32 [1], replicated, may hold values from 2 to 20
- mixing_weight: float32 [768, 3, 768], P('dp', None, 'tensor'), may hold values from -0.21875 to 0.21875
- mixing_moment: float32 [768, 3, 768], P('dp', None, 'tensor'), may hold values from -0.005859375 to 0.005859375
- mixing_square: float32 [768, 3, 768], P('dp', None, 'tensor'), may hold values from 4.709503e-08 to 1.8838011e-07
- mixing_average: float32 [768, 3, 768], P('dp', None, 'tensor'), may hold values from -0.21875 to 0.21875
- merging_weight: float32 [768, 768], P('tensor', 'dp'), may hold values from -1.75 to 1.75
- merging_moment: float32 [768, 768], P('tensor', 'dp'), may hold values from -0.005859375 to 0.005859375
- merging_square: float32 [768, 768], P('tensor', 'dp'), may hold values from 4.709503e-08 to 1.8838011e-07
- merging_average: float32 [768, 768], P('tensor', 'dp'), may hold values from -1.75 to 1.75
- expand_weight: float32 [768, 3072], P('dp', 'tensor'), may hold values from -0.21875 to 0.21875
- expand_moment: float32 [768, 3072], P('dp', 'tensor'), may hold values from -0.005859375 to 0.005859375
- expand_square: float32 [768, 3072], P('dp', 'tensor'), may hold values from 4.709503e-08 to 1.8838011e-07
- expand_average: float32 [768, 3072], P('dp', 'tensor'), may hold values from -0.21875 to 0.21875
- shrink_weight: float32 [3072, 768], P('tensor', 'dp'), may hold values from -0.109375 to 0.109375
- shrink_moment: float32 [3072, 768], P('tensor', 'dp'), may hold values from -0.005859375 to 0.005859375
- shrink_square: float32 [3072, 768], P('tensor', 'dp'), may hold values from 4.709503e-08 to 1.8838011e-07
- shrink_average: float32 [3072, 768], P('tensor', 'dp'), may hold values from -0.109375 to 0.109375
- scales_weight: float32 [6, 768], replicated, may hold values from -0.75 to 1.5
- scales_moment: float32 [6, 768], replicated, may hold values from -0.0234375 to 0.0234375
- scales_square: float32 [6, 768], replicated, may hold values from 7.5352045e-07 to 3.0140818e-06
- scales_average: float32 [6, 768], replicated, may hold values from -0.75 to 1.5
- offsets_weight: float32 [4608], P('tensor'), may hold values from -3 to 3
- offsets_moment: float32 [4608], P('tensor'), may hold values from -0.0234375 to 0.0234375
- offsets_square: float32 [4608], P('tensor'), may hold values from 7.5352045e-07 to 3.0140818e-06
- offsets_average: float32 [4608], P('tensor'), may hold values from -3 to 3
Outputs:
- short_output: bfloat16 [128, 64, 768], P('dp')
- long_output: bfloat16 [128, 256, 768], P('dp')
- short_gradient: float32 [128, 64, 768], P('dp')
- long_gradient: float32 [128, 256, 768], P('dp')
- query_gradient: float32 [256, 768], P('dp')
- contrast_loss: float32 [1], replicated
- gradient_norm: float32 [1], replicated
- mixing_master: float32 [768, 3, 768], P('dp', None, 'tensor')
- mixing_first: float32 [768, 3, 768], P('dp', None, 'tensor')
- mixing_second: float32 [768, 3, 768], P('dp', None, 'tensor')
- mixing_smooth: float32 [768, 3, 768], P('dp', None, 'tensor')
- merging_master: float32 [768, 768], P('tensor', 'dp')
- merging_first: float32 [768, 768], P('tensor', 'dp')
- merging_second: float32 [768, 768], P('tensor', 'dp')
- merging_smooth: float32 [768, 768], P('tensor', 'dp')
- expand_master: float32 [768, 3072], P('dp', 'tensor')
- expand_first: float32 [768, 3072], P('dp', 'tensor')
- expand_second: float32 [768, 3072], P('dp', 'tensor')
- expand_smooth: float32 [768, 3072], P('dp', 'tensor')
- shrink_master: float32 [3072, 768], P('tensor', 'dp')
- shrink_first: float32 [3072, 768], P('tensor', 'dp')
- shrink_second: float32 [3072, 768], P('tensor', 'dp')
- shrink_smooth: float32 [3072, 768], P('tensor', 'dp')
- scales_master: float32 [6, 768], replicated
- scales_first: float32 [6, 768], replicated
- scales_second: float32 [6, 768], replicated
- scales_smooth: float32 [6, 768], replicated
- offsets_master: float32 [4608], P('tensor')
- offsets_first: float32 [4608], P('tensor')
- offsets_second: float32 [4608], P('tensor')
- offsets_smooth: float32 [4608], P('tensor')
Inputs may be any that keep to these rules, and one draw needn't show every extreme that they name: `short_lengths`: at least one short passage has all 64 tokens valid. `long_lengths`: at least one long passage has all 256 tokens valid. `positives`: each passage is the positive of exactly one query.
All inputs are finite; a program needn't handle non-finite values. No bound on the sum of `short_lengths` or of `long_lengths` on one device may be relied on, other than what follows from the above.
Results may differ from a plain program's by a relative error of at most 0.013.
The roundings to bfloat16 on the way count: a program that leaves them out, or rounds other values in their place, can miss the bound.
Values may be sent and summed in bfloat16 or wider, within the bound.
A program may use at most 256 MiB of HBM per device.

v0:
```python
import math

import jax
import jax.numpy as jnp
from jax import lax
from jax.sharding import PartitionSpec as P

D = 768
FF = 3072
HEAD_DIM = 64


norm_eps = 1e-05
score_scale = 0.125
masked_value = -1e30
first_decay = 0.5
second_decay = 0.75
smooth_decay = 0.75
decay_weight = 0.01
adam_eps = 1e-08
clip_limit = 1.0
inverse_root_two = 0.7071067811865476
inverse_root_tau = 0.3989422804014327


def layer_stats(resid):
    centre = resid - jnp.mean(resid, axis=-1, keepdims=True)
    rstd = lax.rsqrt(jnp.mean(centre * centre, axis=-1, keepdims=True) + norm_eps)
    return (centre * rstd, rstd)


def layer_back(gradient, normed, rstd, gain):
    scaled = gradient * gain
    return rstd * (
        scaled
        - jnp.mean(scaled, axis=-1, keepdims=True)
        - normed * jnp.mean(scaled * normed, axis=-1, keepdims=True)
    )


def gelu_slope(upward):
    cumulative = 0.5 * (1.0 + lax.erf(upward * inverse_root_two))
    density = jnp.exp(-0.5 * upward * upward) * inverse_root_tau
    return cumulative + upward * density


def key_scores(queries_part, keys_part, lengths):
    product = (
        jnp.einsum("bqhd,bkhd->bhqk", queries_part, keys_part, preferred_element_type=jnp.float32)
        * score_scale
    )
    visible = lax.broadcasted_iota(jnp.int32, product.shape, 3) < lengths[:, None, None, None]
    return jnp.where(visible, product, masked_value)


def attend_forward(queries_part, keys_part, values_part, lengths):
    scores = key_scores(queries_part, keys_part, lengths)
    highest = jnp.max(scores, axis=-1, keepdims=True)
    powered = jnp.exp(scores - highest)
    summed = jnp.sum(powered, axis=-1, keepdims=True)
    weights = (powered / summed).astype(jnp.bfloat16)
    context = jnp.einsum(
        "bhqk,bkhd->bqhd", weights, values_part, preferred_element_type=jnp.float32
    )
    return (context.astype(jnp.bfloat16), highest + jnp.log(summed))


def attend_back(queries_part, keys_part, values_part, lengths, logsum, context_back):
    scores = key_scores(queries_part, keys_part, lengths)
    weights = jnp.exp(scores - logsum)
    value_back = jnp.einsum(
        "bhqk,bqhd->bkhd",
        weights.astype(jnp.bfloat16),
        context_back,
        preferred_element_type=jnp.float32,
    )
    weight_back = jnp.einsum(
        "bqhd,bkhd->bhqk", context_back, values_part, preferred_element_type=jnp.float32
    )
    score_back = weights * (weight_back - jnp.sum(weights * weight_back, axis=-1, keepdims=True))
    score_low = (score_back * score_scale).astype(jnp.bfloat16)
    query_back = jnp.einsum(
        "bhqk,bkhd->bqhd", score_low, keys_part, preferred_element_type=jnp.float32
    )
    key_back = jnp.einsum(
        "bhqk,bqhd->bkhd", score_low, queries_part, preferred_element_type=jnp.float32
    )
    return (query_back, key_back, value_back)


def split_heads(rows, first, count, span):
    return rows[first : first + count * span].reshape(count, span, -1, HEAD_DIM)


def tensor_total(partial_rows):
    return lax.psum(partial_rows, "tensor")


def shards(
    short_tokens,
    long_tokens,
    short_cotangent,
    long_cotangent,
    short_lengths,
    long_lengths,
    queries,
    positives,
    step_count,
    mixing_weight,
    mixing_moment,
    mixing_square,
    mixing_average,
    merging_weight,
    merging_moment,
    merging_square,
    merging_average,
    expand_weight,
    expand_moment,
    expand_square,
    expand_average,
    shrink_weight,
    shrink_moment,
    shrink_square,
    shrink_average,
    scales_weight,
    scales_moment,
    scales_square,
    scales_average,
    offsets_weight,
    offsets_moment,
    offsets_square,
    offsets_average,
):
    mixing_full, merging_full, expand_full, shrink_full = (
        lax.all_gather(mixing_weight.astype(jnp.bfloat16), "dp", axis=0, tiled=True),
        lax.all_gather(merging_weight.astype(jnp.bfloat16), "dp", axis=1, tiled=True),
        lax.all_gather(expand_weight.astype(jnp.bfloat16), "dp", axis=0, tiled=True),
        lax.all_gather(shrink_weight.astype(jnp.bfloat16), "dp", axis=1, tiled=True),
    )
    short_count = short_tokens.shape[0]
    short_span = short_tokens.shape[1]
    long_count = long_tokens.shape[0]
    long_span = long_tokens.shape[1]
    short_rows = short_count * short_span
    local_width = mixing_full.shape[2]
    tensor_count = lax.axis_size("tensor")
    data_count = lax.axis_size("dp")
    tensor_place = lax.axis_index("tensor")
    inputs = jnp.concatenate(
        [short_tokens.reshape(short_rows, D), long_tokens.reshape(-1, D)], axis=0
    )
    inputs_float = inputs.astype(jnp.float32)
    projected = jnp.dot(
        inputs, mixing_full.reshape(D, 3 * local_width), preferred_element_type=jnp.float32
    ).reshape(-1, 3, local_width)
    query_bias = offsets_weight[:local_width]
    value_bias = offsets_weight[local_width : 2 * local_width]
    upward_bias = offsets_weight[2 * local_width :]
    queries_all = (projected[:, 0] + query_bias).astype(jnp.bfloat16)
    keys_all = projected[:, 1].astype(jnp.bfloat16)
    values_all = (projected[:, 2] + value_bias).astype(jnp.bfloat16)
    short_query = split_heads(queries_all, 0, short_count, short_span)
    short_key = split_heads(keys_all, 0, short_count, short_span)
    short_value = split_heads(values_all, 0, short_count, short_span)
    long_query = split_heads(queries_all, short_rows, long_count, long_span)
    long_key = split_heads(keys_all, short_rows, long_count, long_span)
    long_value = split_heads(values_all, short_rows, long_count, long_span)
    short_context, short_logsum = attend_forward(short_query, short_key, short_value, short_lengths)
    long_context, long_logsum = attend_forward(long_query, long_key, long_value, long_lengths)
    context = jnp.concatenate(
        [short_context.reshape(short_rows, local_width), long_context.reshape(-1, local_width)],
        axis=0,
    )
    attention_part = jnp.dot(context, merging_full, preferred_element_type=jnp.float32)
    resid_first = inputs_float + tensor_total(attention_part) + scales_weight[4]
    normed_first, rstd_first = layer_stats(resid_first)
    hidden = normed_first * scales_weight[0] + scales_weight[1]
    hidden_low = hidden.astype(jnp.bfloat16)
    upward = jnp.dot(hidden_low, expand_full, preferred_element_type=jnp.float32) + upward_bias
    activated = jax.nn.gelu(upward, approximate=False).astype(jnp.bfloat16)
    down_part = jnp.dot(activated, shrink_full, preferred_element_type=jnp.float32)
    downward = tensor_total(down_part) + scales_weight[5]
    normed_second, rstd_second = layer_stats(hidden + downward)
    result_local = (normed_second * scales_weight[2] + scales_weight[3]).astype(jnp.bfloat16)
    short_output = result_local[:short_rows].reshape(short_tokens.shape)
    long_output = result_local[short_rows:].reshape(long_tokens.shape)
    leading = jnp.concatenate([short_output[:, 0], long_output[:, 0]], axis=0)
    passages_all = lax.all_gather(leading, "dp", axis=0, tiled=True)
    logits = jnp.einsum("qd,pd->qp", queries, passages_all, preferred_element_type=jnp.float32)
    chosen = (lax.broadcasted_iota(jnp.int32, logits.shape, 1) == positives[:, None]).astype(
        jnp.float32
    )
    highest = jnp.max(logits, axis=1, keepdims=True)
    powered = jnp.exp(logits - highest)
    summed = jnp.sum(powered, axis=1, keepdims=True)
    loss_part = jnp.sum(highest[:, 0] + jnp.log(summed[:, 0]) - jnp.sum(logits * chosen, axis=1))
    logit_back = (powered / summed - chosen).astype(jnp.bfloat16)
    query_gradient = jnp.einsum(
        "qp,pd->qd", logit_back, passages_all, preferred_element_type=jnp.float32
    )
    passage_back = lax.psum_scatter(
        jnp.einsum("qp,qd->pd", logit_back, queries, preferred_element_type=jnp.float32),
        "dp",
        scatter_dimension=0,
        tiled=True,
    )
    short_back = short_cotangent.astype(jnp.float32).at[:, 0].add(passage_back[:short_count])
    long_back = long_cotangent.astype(jnp.float32).at[:, 0].add(passage_back[short_count:])
    result_back = jnp.concatenate(
        [short_back.reshape(short_rows, D), long_back.reshape(-1, D)], axis=0
    )
    gain_second = jnp.sum(result_back * normed_second, axis=0)
    shift_second = jnp.sum(result_back, axis=0)
    second_back = layer_back(result_back, normed_second, rstd_second, scales_weight[2])
    down_bias = jnp.sum(second_back, axis=0)
    down_low = second_back.astype(jnp.bfloat16)
    shrink_grad = jnp.einsum("tf,td->fd", activated, down_low, preferred_element_type=jnp.float32)
    upward_back = jnp.einsum(
        "td,fd->tf", down_low, shrink_full, preferred_element_type=jnp.float32
    ) * gelu_slope(upward)
    up_bias = jnp.sum(upward_back, axis=0)
    upward_low = upward_back.astype(jnp.bfloat16)
    expand_grad = jnp.einsum(
        "td,tf->df", hidden_low, upward_low, preferred_element_type=jnp.float32
    )
    feed_part = jnp.einsum("tf,df->td", upward_low, expand_full, preferred_element_type=jnp.float32)
    hidden_back = second_back + tensor_total(feed_part)
    gain_first = jnp.sum(hidden_back * normed_first, axis=0)
    shift_first = jnp.sum(hidden_back, axis=0)
    first_back = layer_back(hidden_back, normed_first, rstd_first, scales_weight[0])
    out_bias = jnp.sum(first_back, axis=0)
    first_low = first_back.astype(jnp.bfloat16)
    merging_grad = jnp.einsum("tc,td->cd", context, first_low, preferred_element_type=jnp.float32)
    context_back = jnp.einsum(
        "td,cd->tc", first_low, merging_full, preferred_element_type=jnp.float32
    ).astype(jnp.bfloat16)
    short_qback, short_kback, short_vback = attend_back(
        short_query,
        short_key,
        short_value,
        short_lengths,
        short_logsum,
        split_heads(context_back, 0, short_count, short_span),
    )
    long_qback, long_kback, long_vback = attend_back(
        long_query,
        long_key,
        long_value,
        long_lengths,
        long_logsum,
        split_heads(context_back, short_rows, long_count, long_span),
    )
    query_back = jnp.concatenate(
        [short_qback.reshape(short_rows, local_width), long_qback.reshape(-1, local_width)], axis=0
    )
    key_back = jnp.concatenate(
        [short_kback.reshape(short_rows, local_width), long_kback.reshape(-1, local_width)], axis=0
    )
    value_back = jnp.concatenate(
        [short_vback.reshape(short_rows, local_width), long_vback.reshape(-1, local_width)], axis=0
    )
    projected_back = jnp.stack([query_back, key_back, value_back], axis=1).astype(jnp.bfloat16)
    mixing_grad = jnp.einsum(
        "td,tcf->dcf", inputs, projected_back, preferred_element_type=jnp.float32
    )
    input_part = jnp.einsum(
        "tcf,dcf->td", projected_back, mixing_full, preferred_element_type=jnp.float32
    )
    input_back = first_back + tensor_total(input_part)
    short_gradient = input_back[:short_rows].reshape(short_tokens.shape)
    long_gradient = input_back[short_rows:].reshape(long_tokens.shape)
    scales_grad = jnp.stack(
        [gain_first, shift_first, gain_second, shift_second, out_bias, down_bias]
    )
    scales_term = scales_grad / tensor_count
    offsets_grad = jnp.concatenate(
        [jnp.sum(query_back, axis=0), jnp.sum(value_back, axis=0), up_bias]
    )
    own_slot = (lax.broadcasted_iota(jnp.int32, (tensor_count, 1), 0) == tensor_place).astype(
        jnp.float32
    )
    offsets_slots = own_slot * offsets_grad[None, :]
    reduced = (
        lax.psum_scatter(mixing_grad, "dp", scatter_dimension=0, tiled=True),
        lax.psum_scatter(merging_grad, "dp", scatter_dimension=1, tiled=True),
        lax.psum_scatter(expand_grad, "dp", scatter_dimension=0, tiled=True),
        lax.psum_scatter(shrink_grad, "dp", scatter_dimension=1, tiled=True),
    )
    scales_sum, offsets_total = lax.psum((scales_term, offsets_slots), ("dp", "tensor"))
    offsets_sum = jnp.sum(offsets_total * own_slot, axis=0)
    squares = jnp.sum(reduced[0] * reduced[0]) + jnp.sum(reduced[1] * reduced[1])
    squares = squares + jnp.sum(reduced[2] * reduced[2]) + jnp.sum(reduced[3] * reduced[3])
    squares = (
        squares
        + (jnp.sum(scales_sum * scales_sum) / tensor_count + jnp.sum(offsets_sum * offsets_sum))
        / data_count
    )
    squares_all, loss_all = lax.psum((squares, loss_part / tensor_count), ("dp", "tensor"))
    norm_value = jnp.sqrt(squares_all)
    factor = clip_limit / jnp.maximum(norm_value, clip_limit)
    steps_float = step_count[0].astype(jnp.float32)
    first_fix = 1.0 - jnp.power(first_decay, steps_float)
    second_fix = 1.0 - jnp.power(second_decay, steps_float)

    def update(weight, moment, square, average, gradient, rate):
        clipped = gradient * factor
        first = first_decay * moment + (1.0 - first_decay) * clipped
        second = second_decay * square + (1.0 - second_decay) * clipped * clipped
        master = weight - rate * (
            first / first_fix / (jnp.sqrt(second / second_fix) + adam_eps) + decay_weight * weight
        )
        smooth = smooth_decay * average + (1.0 - smooth_decay) * master
        return (master, first, second, smooth)

    mixing_new = update(
        mixing_weight, mixing_moment, mixing_square, mixing_average, reduced[0], 1.0 / math.sqrt(D)
    )
    merging_new = update(
        merging_weight,
        merging_moment,
        merging_square,
        merging_average,
        reduced[1],
        8.0 / math.sqrt(D),
    )
    expand_new = update(
        expand_weight, expand_moment, expand_square, expand_average, reduced[2], 1.0 / math.sqrt(D)
    )
    shrink_new = update(
        shrink_weight, shrink_moment, shrink_square, shrink_average, reduced[3], 1.0 / math.sqrt(FF)
    )
    scales_new = update(
        scales_weight, scales_moment, scales_square, scales_average, scales_sum, 0.3
    )
    offsets_new = update(
        offsets_weight, offsets_moment, offsets_square, offsets_average, offsets_sum, 0.3
    )
    contrast_loss = (loss_all / passages_all.shape[0]).reshape(1)
    gradient_norm = norm_value.reshape(1)
    return (
        (
            short_output,
            long_output,
            short_gradient,
            long_gradient,
            query_gradient,
            contrast_loss,
            gradient_norm,
        )
        + mixing_new
        + merging_new
        + expand_new
        + shrink_new
        + scales_new
        + offsets_new
    )


def solution(mesh):
    placed = (
        P("dp", None, None),
        P("dp", None, None),
        P("dp", None, None),
        P("dp", None, None),
        P("dp"),
        P("dp"),
        P("dp", None),
        P("dp"),
        P(),
        P("dp", None, "tensor"),
        P("dp", None, "tensor"),
        P("dp", None, "tensor"),
        P("dp", None, "tensor"),
        P("tensor", "dp"),
        P("tensor", "dp"),
        P("tensor", "dp"),
        P("tensor", "dp"),
        P("dp", "tensor"),
        P("dp", "tensor"),
        P("dp", "tensor"),
        P("dp", "tensor"),
        P("tensor", "dp"),
        P("tensor", "dp"),
        P("tensor", "dp"),
        P("tensor", "dp"),
        P(),
        P(),
        P(),
        P(),
        P("tensor"),
        P("tensor"),
        P("tensor"),
        P("tensor"),
    )
    return jax.shard_map(
        shards,
        mesh=mesh,
        in_specs=placed,
        out_specs=(
            P("dp", None, None),
            P("dp", None, None),
            P("dp", None, None),
            P("dp", None, None),
            P("dp", None),
            P(),
            P(),
            P("dp", None, "tensor"),
            P("dp", None, "tensor"),
            P("dp", None, "tensor"),
            P("dp", None, "tensor"),
            P("tensor", "dp"),
            P("tensor", "dp"),
            P("tensor", "dp"),
            P("tensor", "dp"),
            P("dp", "tensor"),
            P("dp", "tensor"),
            P("dp", "tensor"),
            P("dp", "tensor"),
            P("tensor", "dp"),
            P("tensor", "dp"),
            P("tensor", "dp"),
            P("tensor", "dp"),
            P(),
            P(),
            P(),
            P(),
            P("tensor"),
            P("tensor"),
            P("tensor"),
            P("tensor"),
        ),
        check_vma=False,
    )
```

profile of v0, /device:TPU:0, one launch (start us, length us, event | category | flops | bytes accessed | tf_op | source)
XLA Modules:
  0.0 1412.0 jit_solution(9783435549638099572)
XLA Ops:
  10.6 26.3 %all_gather.16 = bf16[384,768]{0,1:T(8,128)(2,1)} all-gather(bf16[384,48]{0,1:T(8,128)(2,1)S(1)} %convert_element_type.109), channel_id=1, replica_groups=mesh['dp'=16,'tensor'=2] {'dp'}, dimensions={1}, use_global_device_ids=true | all-gather | bytes 626688 | tf_op jit(solution)/shard_map/all_gather | solution.py:136
  36.9 17.6 %all-gather.4.cloned.1.call-done = bf16[768,3,384]{2,0,1:T(8,128)(2,1)} async-done(((bf16[48,3,384]{2,0,1:T(8,128)(2,1)}), bf16[768,3,384]{2,0,1:T(8,128)(2,1)}) %all-gather.4.cloned.1.call-update) | async-done | bytes 1769488 | tf_op jit(solution)/shard_map/all_gather | solution.py:135
  57.1 7.5 fusion.151
  117.7 183.6 %all-reduce.7.cloned.1.call-done = f32[2560,768]{1,0:T(8,128)} async-done(((f32[2560,768]{1,0:T(8,128)}), f32[2560,768]{1,0:T(8,128)}) %all-reduce.7.cloned.1.call-update) | async-done | bytes 7864336 | tf_op jit(solution)/shard_map/psum | solution.py:96
  310.5 36.2 %all-gather.6.cloned.1.call-done = bf16[768,1536]{1,0:T(8,128)(2,1)} async-done(((bf16[48,1536]{1,0:T(8,128)(2,1)}), bf16[768,1536]{1,0:T(8,128)(2,1)}) %all-gather.6.cloned.1.call-update) | async-done | bytes 2359312 | tf_op jit(solution)/shard_map/all_gather | solution.py:137
  346.8 44.2 %fusion.4 = (bf16[2560,1536]{1,0:T(8,128)(2,1)}, f32[2560,1536]{1,0:T(8,128)}) fusion(f32[1536]{0:T(1024)S(1)} %slice.146, bf16[768,1536]{1,0:T(8,128)(2,1)} %all-gather.6.cloned.1.call-done, f32[2560,768]{1,0:T(8,128)} %copy-done.2, f32[768]{0:T(1024)S(1)} %get-tuple-element.64, f32[768]{0:T(1024)S(1)} %get-tuple-element.65, f32[2560]{0:T(1024)S(1)} %add_rsqrt_fusion.1, ...), kind=kOutput, calls=%fused_computation.6 | convolution fusion | flops 6309150720 | bytes 33849344 | tf_op jit(solution)/shard_map/dot_general | solution.py:179
  390.9 11.3 fusion.161
  402.3 186.1 %all-reduce.9.cloned.1.call-done = f32[2560,768]{1,0:T(8,128)} async-done(((f32[2560,768]{1,0:T(8,128)}), f32[2560,768]{1,0:T(8,128)}) %all-reduce.9.cloned.1.call-update) | async-done | bytes 7864336 | tf_op jit(solution)/shard_map/psum | solution.py:96
  588.4 7.6 fusion.148
  601.5 22.4 %all_gather.19 = bf16[256,768]{1,0:T(8,128)(2,1)S(1)} all-gather(bf16[16,768]{1,0:T(8,128)(2,1)S(1)} %pad_maximum_fusion.7), channel_id=1, replica_groups=mesh['dp'=16,'tensor'=2] {'dp'}, dimensions={0}, use_global_device_ids=true | all-gather | bytes 417792 | tf_op jit(solution)/shard_map/all_gather | solution.py:188
  627.6 6.5 copy_convert_fusion
  634.1 46.0 %reduce-scatter.6.cloned.1.call-done = f32[16,768]{1,0:T(8,128)} async-done(((f32[256,768]{1,0:T(8,128)}), f32[16,768]{1,0:T(8,128)}) %reduce-scatter.6.cloned.1.call-update) | async-done | bytes 49168 | tf_op jit(solution)/shard_map/reduce_scatter | solution.py:201
  682.1 5.6 copy.168
  697.1 16.6 %fusion.159 = (f32[1536]{0:T(1024)}, bf16[2560,1536]{1,0:T(8,128)(2,1)S(1)}) fusion(f32[2560,1536]{1,0:T(8,128)} %get-tuple-element.120, f32[1536]{0:T(1024)S(1)} %slice.146, bf16[1536,768]{0,1:T(8,128)(2,1)S(1)} %copy-done.55, f32[2560,768]{1,0:T(8,128)S(1)} %get-tuple-element.99), kind=kOutput, calls=%fused_computation.245 | convolution fusion | flops 6088948224 | bytes 33828864 | tf_op jit(solution)/shard_map/td,fd->tf/dot_general | solution.py:218
  716.8 8.6 fusion.49
  725.5 12.5 fusion.54
  738.1 12.7 fusion.47
  751.1 160.7 %all-reduce.11.cloned.1.call-done = f32[2560,768]{1,0:T(8,128)} async-done(((f32[2560,768]{1,0:T(8,128)}), f32[2560,768]{1,0:T(8,128)}) %all-reduce.11.cloned.1.call-update) | async-done | bytes 7864336 | tf_op jit(solution)/shard_map/psum | solution.py:96
  911.8 11.0 multiply_reduce_fusion.2
  922.8 6.2 fusion.147
  953.5 8.3 bitcast_convert_fusion
  966.9 6.4 fusion.80
  973.4 20.8 %bitcast_convert_fusion.1 = (bf16[8,256,6,64]{1,3,2,0:T(8,128)(2,1)S(1)}, f32[8,6,64,256]{3,2,1,0:T(8,128)}) fusion(f32[8,6,256,256]{2,3,1,0:T(8,128)} %fusion.80, f32[8,6,256,256]{2,3,1,0:T(8,128)} %copy-done.5, f32[8,6,256]{2,1,0:T(8,128)S(1)} %log_add_fusion, bf16[8,256,6,64]{1,0,3,2:T(8,128)(2,1)} %bitcast.195), kind=kOutput, calls=%fused_computation.85 | convolution fusion | flops 425472256 | bytes 31506432 | tf_op jit(solution)/shard_map/bhqk,bkhd->bqhd/dot_general | solution.py:82
  996.7 22.1 %fusion.72 = bf16[8,256,6,64]{1,3,2,0:T(8,128)(2,1)} fusion(f32[8,6,256,256]{2,3,1,0:T(8,128)} %fusion.80, f32[8,6,256,256]{2,3,1,0:T(8,128)} %copy-done.5, f32[8,6,256]{2,1,0:T(8,128)S(1)} %log_add_fusion, bf16[8,256,6,64]{1,0,3,2:T(8,128)(2,1)} %bitcast.193), kind=kOutput, calls=%fused_computation.114 | convolution fusion | flops 425472256 | bytes 28360704 | tf_op jit(solution)/shard_map/bhqk,bqhd->bkhd/dot_general | solution.py:85
  1018.9 7.2 fusion.51
  1044.3 10.6 fusion.43
  1054.9 9.8 convolution_bitcast_fusion
  1089.3 40.7 %all-reduce.1 = (f32[6,768]{1,0:T(8,128)S(1)}, f32[2,2304]{1,0:T(2,128)S(1)}) all-reduce(f32[6,768]{1,0:T(8,128)S(1)} %broadcast_multiply_fusion, f32[2,2304]{1,0:T(2,128)S(1)} %broadcast_multiply_fusion.1), channel_id=1, replica_groups=mesh['dp'=16,'tensor'=2] {'dp','tensor'}, use_global_device_ids=true, to_apply=%region_39.40 | all-reduce | flops 9216 | bytes 73728 | tf_op jit(solution)/shard_map/psum | solution.py:289
  1134.7 67.2 %reduce-scatter.8.cloned.1.call-done = f32[48,3,384]{2,0,1:T(8,128)} async-done(((f32[768,3,384]{2,0,1:T(8,128)}), f32[48,3,384]{2,0,1:T(8,128)}) %reduce-scatter.8.cloned.1.call-update) | async-done | bytes 221200 | tf_op jit(solution)/shard_map/reduce_scatter | solution.py:284
  1208.1 40.1 %all-reduce = (f32[]{:T(128)}, f32[]{:T(128)}) all-reduce(f32[]{:T(128)S(6)} %div.161, f32[]{:T(128)S(6)} %add.321), channel_id=1, replica_groups=mesh['dp'=16,'tensor'=2] {'dp','tensor'}, use_global_device_ids=true, to_apply=%region_23.24 | all-reduce | flops 2 | bytes 16 | tf_op jit(solution)/shard_map/psum | solution.py:298
  1260.2 131.7 %all-reduce.13.cloned.1.call-done = f32[2560,768]{1,0:T(8,128)} async-done(((f32[2560,768]{1,0:T(8,128)}), f32[2560,768]{1,0:T(8,128)}) %all-reduce.13.cloned.1.call-update) | async-done | bytes 7864336 | tf_op jit(solution)/shard_map/psum | solution.py:96
  1391.9 6.5 add.315
  (284 shorter events, 187.0 us)
Async XLA Ops:
  7.2 617.5 %copy-start = (bf16[16,768]{1,0:T(8,128)(2,1)S(1)}, bf16[16,768]{1,0:T(8,128)(2,1)}, u32[]{:S(2)}) copy-start(bf16[16,768]{1,0:T(8,128)(2,1)} %param.43) | copy-start | bytes 73732
  7.2 47.3 %all-gather.4.cloned.1.call-start = ((), (), s32[]{:S(2)}) async-start(), calls=%async_computation.5 | async-start | bytes 1880064 | tf_op jit(solution)/shard_map/all_gather | solution.py:135
  8.9 292.4 %all-reduce.7.cloned.1.call-start = ((), (), s32[]{:S(2)}) async-start(), calls=%async_computation.6 | async-start | bytes 15728640 | tf_op jit(solution)/shard_map/psum | solution.py:96
  72.8 31.4 %copy-start.10 = (bf16[48,8,8,256]{3,2,1,0:T(8,128)(2,1)}, bf16[48,8,8,256]{3,2,1,0:T(8,128)(2,1)S(1)}, u32[]{:S(2)}) copy-start(bf16[48,8,8,256]{3,2,1,0:T(8,128)(2,1)S(1)} %copy.224) | copy-start | bytes 4718596
  74.6 14.1 copy-start.56
  109.6 191.7 %copy-start.19 = (bf16[8,256,768]{2,1,0:T(8,128)(2,1)S(1)}, bf16[8,256,768]{2,1,0:T(8,128)(2,1)}, u32[]{:S(2)}) copy-start(bf16[8,256,768]{2,1,0:T(8,128)(2,1)} %param.38) | copy-start | bytes 9437188
  115.1 231.7 %all-gather.6.cloned.1.call-start = ((), (), s32[]{:S(2)}) async-start(), calls=%async_computation.7 | async-start | bytes 2506752 | tf_op jit(solution)/shard_map/all_gather | solution.py:137
  115.8 275.1 %all-gather.8.cloned.1.call-start = ((), (), s32[]{:S(2)}) async-start(), calls=%async_computation.8 | async-start | bytes 2506752 | tf_op jit(solution)/shard_map/all_gather | solution.py:138
  117.5 470.8 %all-reduce.9.cloned.1.call-start = ((), (), s32[]{:S(2)}) async-start(), calls=%async_computation.9 | async-start | bytes 15728640 | tf_op jit(solution)/shard_map/psum | solution.py:96
  402.3 277.9 %reduce-scatter.6.cloned.1.call-start = ((), (), s32[]{:S(2)}) async-start(), calls=%async_computation.10 | async-start | bytes 835584 | tf_op jit(solution)/shard_map/reduce_scatter | solution.py:201
  597.9 27.2 %copy-start.53 = (s32[16]{0:T(128)S(1)}, s32[16]{0:T(128)}, u32[]{:S(2)}) copy-start(s32[16]{0:T(128)} %param.44) | copy-start | bytes 196
  599.5 27.6 %copy-start.28 = (bf16[8,64,768]{2,1,0:T(8,128)(2,1)S(1)}, bf16[8,64,768]{2,1,0:T(8,128)(2,1)}, u32[]{:S(2)}) copy-start(bf16[8,64,768]{2,1,0:T(8,128)(2,1)} %param.39) | copy-start | bytes 2359300
  599.6 25.5 %copy-start.26 = (bf16[512,768]{1,0:T(8,128)(2,1)}, bf16[512,768]{1,0:T(8,128)(2,1)S(1)}, u32[]{:S(2)}) copy-start(bf16[512,768]{1,0:T(8,128)(2,1)S(1)} %slice.170) | copy-start | bytes 2359300
  625.1 56.9 %copy-start.48 = (f32[16]{0:T(128)}, f32[16]{0:T(128)S(1)}, u32[]{:S(2)}) copy-start(f32[16]{0:T(128)S(1)} %get-tuple-element.121) | copy-start | bytes 196
  625.8 56.2 %copy-start.50 = (f32[16]{0:T(128)}, f32[16]{0:T(128)S(1)}, u32[]{:S(2)}) copy-start(f32[16]{0:T(128)S(1)} %get-tuple-element.69) | copy-start | bytes 196
  627.1 284.7 %all-reduce.11.cloned.1.call-start = ((), (), s32[]{:S(2)}) async-start(), calls=%async_computation.11 | async-start | bytes 15728640 | tf_op jit(solution)/shard_map/psum | solution.py:96
  697.1 16.6 %copy-start.6 = (f32[2560,768]{1,0:T(8,128)}, f32[2560,768]{1,0:T(8,128)S(1)}, u32[]{:S(2)}) copy-start(f32[2560,768]{1,0:T(8,128)S(1)} %get-tuple-element.99) | copy-start | bytes 23592964
  697.1 19.7 %copy-start.54 = (bf16[768,1536]{1,0:T(8,128)(2,1)S(1)}, bf16[768,1536]{1,0:T(8,128)(2,1)}, u32[]{:S(2)}) copy-start(bf16[768,1536]{1,0:T(8,128)(2,1)} %all-gather.6.cloned.1.call-done) | copy-start | bytes 7077892
  725.5 349.3 %reduce-scatter.14.cloned.1.call-start = ((), (), s32[]{:S(2)}) async-start(), calls=%async_computation.16 | async-start | bytes 5013504 | tf_op jit(solution)/shard_map/reduce_scatter | solution.py:287
  738.0 338.4 %reduce-scatter.12.cloned.1.call-start = ((), (), s32[]{:S(2)}) async-start(), calls=%async_computation.15 | async-start | bytes 5013504 | tf_op jit(solution)/shard_map/reduce_scatter | solution.py:286
  750.8 382.5 %reduce-scatter.10.cloned.1.call-start = ((), (), s32[]{:S(2)}) async-start(), calls=%async_computation.14 | async-start | bytes 1253376 | tf_op jit(solution)/shard_map/reduce_scatter | solution.py:285
  1026.1 175.8 %reduce-scatter.8.cloned.1.call-start = ((), (), s32[]{:S(2)}) async-start(), calls=%async_computation.13 | async-start | bytes 3760128 | tf_op jit(solution)/shard_map/reduce_scatter | solution.py:284
  1054.9 337.0 %all-reduce.13.cloned.1.call-start = ((), (), s32[]{:S(2)}) async-start(), calls=%async_computation.12 | async-start | bytes 15728640 | tf_op jit(solution)/shard_map/psum | solution.py:96
  1067.5 15.2 %copy-start.9 = (f32[8,6,64,256]{3,2,1,0:T(8,128)S(1)}, f32[8,6,64,256]{3,2,1,0:T(8,128)}, u32[]{:S(2)}) copy-start(f32[8,6,64,256]{3,2,1,0:T(8,128)} %get-tuple-element.124) | copy-start | bytes 9437188
  1067.5 138.6 %copy-start.38 = (f32[256,16]{0,1:T(8,128)S(1)}, f32[256,16]{0,1:T(8,128)}, u32[]{:S(2)}) copy-start(f32[256,16]{0,1:T(8,128)} %copy-done.37) | copy-start | bytes 49156
  1067.5 182.0 %copy-start.45 = (f32[2304]{0:T(1024)S(1)}, f32[2304]{0:T(1024)}, u32[]{:S(2)}) copy-start(f32[2304]{0:T(1024)} %param.66) | copy-start | bytes 27652
  1067.6 184.9 %copy-start.29 = (f32[384,48]{0,1:T(8,128)S(1)}, f32[384,48]{0,1:T(8,128)}, u32[]{:S(2)}) copy-start(f32[384,48]{0,1:T(8,128)} %param.50) | copy-start | bytes 221188
  1071.6 184.9 %copy-start.24 = (f32[48,1536]{1,0:T(8,128)S(1)}, f32[48,1536]{1,0:T(8,128)}, u32[]{:S(2)}) copy-start(f32[48,1536]{1,0:T(8,128)} %param.54) | copy-start | bytes 884740
  1083.0 173.5 %copy-start.25 = (f32[48,1536]{1,0:T(8,128)S(1)}, f32[48,1536]{1,0:T(8,128)}, u32[]{:S(2)}) copy-start(f32[48,1536]{1,0:T(8,128)} %reduce-scatter.12.cloned.1.call-done) | copy-start | bytes 884740
  1083.0 173.5 %copy-start.30 = (f32[48,1536]{1,0:T(8,128)S(1)}, f32[48,1536]{1,0:T(8,128)}, u32[]{:S(2)}) copy-start(f32[48,1536]{1,0:T(8,128)} %param.57) | copy-start | bytes 884740
  1083.0 173.5 %copy-start.31 = (f32[48,1536]{1,0:T(8,128)S(1)}, f32[48,1536]{1,0:T(8,128)}, u32[]{:S(2)}) copy-start(f32[48,1536]{1,0:T(8,128)} %param.56) | copy-start | bytes 884740
  1083.0 173.5 %copy-start.32 = (f32[48,1536]{1,0:T(8,128)S(1)}, f32[48,1536]{1,0:T(8,128)}, u32[]{:S(2)}) copy-start(f32[48,1536]{1,0:T(8,128)} %param.55) | copy-start | bytes 884740
  (41 other events, 214.7 us)
Sparse Core Ops, SparseCore 0:
  10.9 43.4 all-gather.3
  115.2 186.0 all-reduce.6
  304.4 42.3 all-gather.5
  349.8 41.1 all-gather.7
  402.4 185.9 all-reduce.8
  627.2 52.8 reduce-scatter.5
  725.6 186.1 all-reduce.10
  915.7 75.5 reduce-scatter.13
  995.6 74.6 reduce-scatter.11
  1073.7 57.3 reduce-scatter.9
  1134.9 66.9 reduce-scatter.7
  1204.3 187.5 all-reduce.12
where the time goes:
time: 1420 us; the launch traced here: 1410 us
  waiting for transfers between devices  829 us (58%)
  matrix products  236 us (17%)
  blocking collectives  129 us (9%)
  other arithmetic  106 us (7%)
  local copies, waits for them, and re-layouts  84.9 us (6%)
  between operations  24.5 us (2%)
    psum x4, waiting for transfers between devices, tensor_total(): return lax.psum(partial_rows, 'tensor')  662 us
    reduce_scatter x1, waiting for transfers between devices, shards(): lax.psum_scatter(mixing_grad, 'dp', scatter_dimension=0, tiled=True)  67.2 us
    reduce_scatter x1, waiting for transfers between devices, shards(): lax.psum_scatter(jnp.einsum('qp,qd->pd', logit_back, queries, preferred_e...  46 us
    dot_general x1, matrix products, shards(): jnp.dot(hidden_low, expand_full, preferred_element_type=jnp.float32)  44.2 us
    psum x1, blocking collectives, shards(): lax.psum((scales_term, offsets_slots), ('dp', 'tensor'))  40.7 us
    psum x1, blocking collectives, shards(): lax.psum((squares, loss_part / tensor_count), ('dp', 'tensor'))  40.1 us
    all_gather x1, waiting for transfers between devices, shards(): lax.all_gather(expand_weight.astype(jnp.bfloat16), 'dp', axis=0, tiled=True)  36.2 us
  transfers between devices with their start and end apart: 12, of which 8 were waited for; matrix products, arithmetic and copies ran while one was open for 20% of the time, Pallas kernels for 0%

commit v1 on v0

v1 whole, which is shorter than its diff:
```python
import functools
import math

import jax
import jax.numpy as jnp
from jax import lax
from jax.experimental import pallas as pl
from jax.experimental.pallas import tpu as pltpu
from jax.sharding import PartitionSpec as P

D = 768
FF = 3072
HEAD_DIM = 64
PAIR = 2 * HEAD_DIM
MESH = pl.DeviceIdType.MESH

norm_eps = 1e-05
score_scale = 0.125
masked_value = -1e30
first_decay = 0.5
second_decay = 0.75
smooth_decay = 0.75
decay_weight = 0.01
adam_eps = 1e-08
clip_limit = 1.0
inverse_root_two = 0.7071067811865476
inverse_root_tau = 0.3989422804014327
big_vmem = 56 * 1024 * 1024


def dot_nn(a, b):
    return lax.dot_general(a, b, (((1,), (0,)), ((), ())), preferred_element_type=jnp.float32)


def dot_nt(a, b):
    return lax.dot_general(a, b, (((1,), (1,)), ((), ())), preferred_element_type=jnp.float32)


def dot_tn(a, b):
    return lax.dot_general(a, b, (((0,), (0,)), ((), ())), preferred_element_type=jnp.float32)


def layer_stats(resid):
    centre = resid - jnp.mean(resid, axis=-1, keepdims=True)
    rstd = lax.rsqrt(jnp.mean(centre * centre, axis=-1, keepdims=True) + norm_eps)
    return (centre * rstd, rstd)


def layer_back(gradient, normed, rstd, gain):
    scaled = gradient * gain
    return rstd * (
        scaled
        - jnp.mean(scaled, axis=-1, keepdims=True)
        - normed * jnp.mean(scaled * normed, axis=-1, keepdims=True)
    )


def visible_keys(spans, step, rows, piece, key_axis):
    shape = (rows, 1) if key_axis == 0 else (1, rows)
    place = lax.broadcasted_iota(jnp.int32, shape, key_axis)
    segment = place // piece
    limit = jnp.zeros(shape, jnp.int32)
    for index in range(rows // piece):
        limit = jnp.where(segment == index, spans[step, index], limit)
    key_valid = (place % piece) < limit
    first = lax.broadcasted_iota(jnp.int32, (rows, rows), 0) // piece
    second = lax.broadcasted_iota(jnp.int32, (rows, rows), 1) // piece
    return jnp.logical_and(jnp.logical_or(first == second, step > 0), key_valid)


def own_lanes(value, which):
    lane = lax.broadcasted_iota(jnp.int32, value.shape, 1)
    return jnp.where((lane // HEAD_DIM) == which, value, jnp.zeros_like(value))


def join_lanes(low, high):
    lane = lax.broadcasted_iota(jnp.int32, low.shape, 1)
    return jnp.where(lane < HEAD_DIM, low, high)


def attend_forward_kernel(piece, spans, x_ref, w_ref, bias_ref, qkv_ref, ctx_ref):
    step = pl.program_id(0)
    rows = x_ref.shape[0]
    width = w_ref.shape[2] // 3
    visible = visible_keys(spans, step, rows, piece, 1)
    for half in range(w_ref.shape[0]):
        base = half * 3 * width
        projected = dot_nn(x_ref[...], w_ref[half]) + bias_ref[:, base : base + 3 * width]
        qkv_ref[:, base : base + 3 * width] = projected.astype(jnp.bfloat16)
        for pair in range(width // PAIR):
            at = base + pair * PAIR
            q = qkv_ref[:, at : at + PAIR] * jnp.bfloat16(score_scale)
            k = qkv_ref[:, at + width : at + width + PAIR]
            v = qkv_ref[:, at + 2 * width : at + 2 * width + PAIR]
            parts = []
            for which in range(2):
                scores = jnp.where(visible, dot_nt(own_lanes(q, which), k), masked_value)
                powered = jnp.exp(scores - jnp.max(scores, axis=-1, keepdims=True))
                weights = powered * (1.0 / jnp.sum(powered, axis=-1, keepdims=True))
                parts.append(dot_nn(weights.astype(jnp.bfloat16), v))
            at = half * width + pair * PAIR
            ctx_ref[:, at : at + PAIR] = join_lanes(*parts).astype(jnp.bfloat16)


def feed_forward_kernel(
    ctx_ref, x_ref, mt_ref, e_ref, st_ref, scales_ref, bu_ref,
    out_ref, hb_ref, g_ref, slope_ref, n1_ref, r1_ref, n2_ref, r2_ref,
):
    width = mt_ref.shape[2]
    wide = e_ref.shape[2]
    attention = scales_ref[4:5, :]
    for half in range(mt_ref.shape[0]):
        attention = attention + dot_nt(
            ctx_ref[:, half * width : (half + 1) * width], mt_ref[half]
        )
    normed, rstd = layer_stats(x_ref[...].astype(jnp.float32) + attention)
    n1_ref[...] = normed
    r1_ref[...] = rstd
    hidden = normed * scales_ref[0:1, :] + scales_ref[1:2, :]
    hidden_low = hidden.astype(jnp.bfloat16)
    hb_ref[...] = hidden_low
    downward = scales_ref[5:6, :]
    for half in range(e_ref.shape[0]):
        at = half * wide
        upward = dot_nn(hidden_low, e_ref[half]) + bu_ref[:, at : at + wide]
        cumulative = 0.5 * (1.0 + lax.erf(upward * inverse_root_two))
        density = jnp.exp(-0.5 * upward * upward) * inverse_root_tau
        activated = (upward * cumulative).astype(jnp.bfloat16)
        g_ref[:, at : at + wide] = activated
        slope_ref[:, at : at + wide] = (cumulative + upward * density).astype(jnp.bfloat16)
        downward = downward + dot_nt(activated, st_ref[half])
    normed, rstd = layer_stats(hidden + downward)
    n2_ref[...] = normed
    r2_ref[...] = rstd
    out_ref[...] = (normed * scales_ref[2:3, :] + scales_ref[3:4, :]).astype(jnp.bfloat16)


def add_row(ref, index, value):
    ref[index : index + 1, :] += jnp.sum(value, axis=0, keepdims=True)


def feed_back_kernel(
    piece, cot_ref, lead_ref, n1_ref, r1_ref, n2_ref, r2_ref, slope_ref, mt_ref, e_ref, st_ref, scales_ref,
    dz_ref, dub_ref, da_ref, dr1_ref, dctx_ref, vec_ref, up_ref,
):
    @pl.when(pl.program_id(0) == 0)
    def _():
        vec_ref[...] = jnp.zeros_like(vec_ref)
        up_ref[...] = jnp.zeros_like(up_ref)

    width = mt_ref.shape[2]
    wide = e_ref.shape[2]
    dout = cot_ref[...].astype(jnp.float32)
    row = lax.broadcasted_iota(jnp.int32, dout.shape, 0)
    for index in range(dout.shape[0] // piece):
        dout = dout + jnp.where(row == index * piece, lead_ref[0, index : index + 1, :], 0.0)
    normed = n2_ref[...]
    add_row(vec_ref, 2, dout * normed)
    add_row(vec_ref, 3, dout)
    second = layer_back(dout, normed, r2_ref[...], scales_ref[2:3, :])
    add_row(vec_ref, 5, second)
    low = second.astype(jnp.bfloat16)
    dz_ref[...] = low
    hidden_back = second
    for half in range(e_ref.shape[0]):
        at = half * wide
        upward = dot_nn(low, st_ref[half]) * slope_ref[:, at : at + wide].astype(jnp.float32)
        up_ref[0:1, at : at + wide] += jnp.sum(upward, axis=0, keepdims=True)
        upward_low = upward.astype(jnp.bfloat16)
        dub_ref[:, at : at + wide] = upward_low
        hidden_back = hidden_back + dot_nt(upward_low, e_ref[half])
    normed = n1_ref[...]
    add_row(vec_ref, 0, hidden_back * normed)
    add_row(vec_ref, 1, hidden_back)
    first = layer_back(hidden_back, normed, r1_ref[...], scales_ref[0:1, :])
    add_row(vec_ref, 4, first)
    dr1_ref[...] = first
    low = first.astype(jnp.bfloat16)
    da_ref[...] = low
    for half in range(mt_ref.shape[0]):
        dctx_ref[:, half * width : (half + 1) * width] = dot_nn(low, mt_ref[half]).astype(
            jnp.bfloat16
        )


def attend_back_kernel(
    piece, spans, qkv_ref, dctx_ref, dr1_ref, w_ref, dproj_ref, dx_ref, low_ref, bias_ref
):
    step = pl.program_id(0)

    @pl.when(step == 0)
    def _():
        bias_ref[...] = jnp.zeros_like(bias_ref)

    rows = qkv_ref.shape[0]
    width = w_ref.shape[2] // 3
    visible = visible_keys(spans, step, rows, piece, 0)
    total = dr1_ref[...]
    for half in range(w_ref.shape[0]):
        base = half * 3 * width
        for pair in range(width // PAIR):
            at = base + pair * PAIR
            q = qkv_ref[:, at : at + PAIR]
            k = qkv_ref[:, at + width : at + width + PAIR]
            v = qkv_ref[:, at + 2 * width : at + 2 * width + PAIR]
            near = half * width + pair * PAIR
            back = dctx_ref[:, near : near + PAIR]
            parts = []
            for which in range(2):
                scores = dot_nt(own_lanes(k, which) * jnp.bfloat16(score_scale), q)
                scores = jnp.where(visible, scores, masked_value)
                powered = jnp.exp(scores - jnp.max(scores, axis=0, keepdims=True))
                weights = powered * (1.0 / jnp.sum(powered, axis=0, keepdims=True))
                weight_back = dot_nt(own_lanes(v, which), back)
                score_back = weights * (
                    weight_back - jnp.sum(weights * weight_back, axis=0, keepdims=True)
                )
                score_low = (score_back * score_scale).astype(jnp.bfloat16)
                parts.append(
                    (
                        dot_tn(score_low, k),
                        dot_nn(score_low, q),
                        dot_nn(weights.astype(jnp.bfloat16), back),
                    )
                )
            for part in range(3):
                value = join_lanes(parts[0][part], parts[1][part])
                spot = at + part * width
                if part != 1:
                    bias_ref[0:1, spot : spot + PAIR] += jnp.sum(value, axis=0, keepdims=True)
                dproj_ref[:, spot : spot + PAIR] = value.astype(jnp.bfloat16)
        total = total + dot_nt(dproj_ref[:, base : base + 3 * width], w_ref[half])
    dx_ref[...] = total
    low_ref[...] = total.astype(jnp.bfloat16)


def weight_grad_kernel(left_ref, right_ref, out_ref, turned_ref):
    @pl.when(pl.program_id(0) == 0)
    def _():
        turned_ref[...] = left_ref[...].T

    out_ref[0] = dot_nn(turned_ref[...], right_ref[...]).astype(jnp.bfloat16)


def weight_grad(left, right, groups, tile):
    rows, depth = left.shape
    columns = right.shape[1]
    per = columns // groups // tile
    return pl.pallas_call(
        weight_grad_kernel,
        grid=(columns // tile,),
        in_specs=[
            pl.BlockSpec((rows, depth), lambda i: (0, 0), pipeline_mode=pl.Buffered(1)),
            pl.BlockSpec((rows, tile), lambda i: (0, i)),
        ],
        out_specs=pl.BlockSpec((1, depth, tile), lambda i: (i // per, 0, i % per)),
        out_shape=jax.ShapeDtypeStruct((groups, depth, columns // groups), jnp.bfloat16),
        scratch_shapes=[pltpu.VMEM((depth, rows), jnp.bfloat16)],
        compiler_params=pltpu.CompilerParams(vmem_limit_bytes=big_vmem),
        cost_estimate=pl.CostEstimate(
            flops=2 * rows * depth * columns,
            bytes_accessed=2 * (rows * depth + rows * columns + depth * columns),
            transcendentals=0,
        ),
        name="weight_grad",
    )(left, right)


def contrast_kernel(
    count, own, halves, cls_ref, q_ref, pos_ref, qg_ref, lead_ref, loss_ref,
    all_ref, part_ref, got_ref, stat_ref, term_ref,
    sem_a, sem_b, sem_c, sem_d, sem_e, sem_f, sem_g, sem_h,
):
    me = lax.axis_index("dp")
    half = lax.axis_index("tensor")
    other = 1 - half
    barrier = pltpu.get_barrier_semaphore()

    @pl.loop(1, count)
    def _(gap):
        pl.semaphore_signal(
            barrier, inc=1, device_id=(lax.rem(me + gap, count), half), device_id_type=MESH
        )

    pl.semaphore_signal(barrier, inc=1, device_id=(me, other), device_id_type=MESH)
    pl.semaphore_wait(barrier, count)

    def push(source, target, sends, lands, gap):
        peer = lax.rem(me + gap, count)
        return pltpu.make_async_remote_copy(
            src_ref=source(peer),
            dst_ref=target.at[me],
            send_sem=sends.at[gap],
            recv_sem=lands.at[me],
            device_id=(peer, half),
            device_id_type=MESH,
        )

    def landed(source, target, sends, lands, gap):
        origin = lax.rem(me + count - gap, count)
        return pltpu.make_async_remote_copy(
            src_ref=target.at[origin],
            dst_ref=target.at[origin],
            send_sem=sends.at[gap],
            recv_sem=lands.at[origin],
            device_id=(origin, half),
            device_id_type=MESH,
        )

    def whole(peer):
        return cls_ref

    @pl.loop(1, count)
    def _(gap):
        push(whole, all_ref, sem_a, sem_b, gap).start()

    all_ref[me] = cls_ref[...]

    @pl.loop(1, count)
    def _(gap):
        landed(whole, all_ref, sem_a, sem_b, gap).wait_recv()

    passages = all_ref[...].reshape(count * own, D).astype(jnp.bfloat16)
    queries = q_ref[...]
    logits = dot_nt(queries, passages)
    column = lax.broadcasted_iota(jnp.int32, logits.shape, 1)
    near = column % own
    kind = own // 2
    index = (column // own) * (own * halves) + (near // kind) * (kind * halves)
    index = index + half * kind + near % kind
    chosen = jnp.where(index == pos_ref[...], 1.0, 0.0)
    highest = jnp.max(logits, axis=1, keepdims=True)
    summed = jnp.sum(jnp.exp(logits - highest), axis=1, keepdims=True)
    picked = jnp.sum(logits * chosen, axis=1, keepdims=True)
    lane = lax.broadcasted_iota(jnp.int32, (logits.shape[0], 128), 1)
    stat_ref[half] = jnp.where(lane == 0, highest, jnp.where(lane == 1, summed, picked))

    def swap(ref, send, land):
        return pltpu.make_async_remote_copy(
            src_ref=ref.at[half],
            dst_ref=ref.at[half],
            send_sem=send,
            recv_sem=land,
            device_id=(me, other),
            device_id_type=MESH,
        )

    def swapped(ref, send, land):
        return pltpu.make_async_remote_copy(
            src_ref=ref.at[other],
            dst_ref=ref.at[other],
            send_sem=send,
            recv_sem=land,
            device_id=(me, other),
            device_id_type=MESH,
        )

    swap(stat_ref, sem_e, sem_f).start()
    swapped(stat_ref, sem_e, sem_f).wait_recv()
    low, high = stat_ref[0], stat_ref[1]
    top = jnp.maximum(low[:, 0:1], high[:, 0:1])
    total = low[:, 1:2] * jnp.exp(low[:, 0:1] - top) + high[:, 1:2] * jnp.exp(high[:, 0:1] - top)
    losses = top + jnp.log(total) - (low[:, 2:3] + high[:, 2:3])
    loss_ref[...] = jnp.broadcast_to(jnp.sum(losses, axis=0, keepdims=True), loss_ref.shape)
    logit_back = (jnp.exp(logits - top) / total - chosen).astype(jnp.bfloat16)
    terms = dot_tn(logit_back, queries)
    part_ref[...] = terms.reshape(count, own, D)

    def piece(peer):
        return part_ref.at[peer]

    @pl.loop(1, count)
    def _(gap):
        push(piece, got_ref, sem_c, sem_d, gap).start()

    term_ref[half] = dot_nn(logit_back, passages)
    swap(term_ref, sem_g, sem_h).start()
    got_ref[me] = part_ref[me]
    swapped(term_ref, sem_g, sem_h).wait_recv()
    qg_ref[...] = term_ref[0] + term_ref[1]

    @pl.loop(1, count)
    def _(gap):
        landed(piece, got_ref, sem_c, sem_d, gap).wait_recv()

    lead_ref[...] = jnp.sum(got_ref[...], axis=0)

    @pl.loop(1, count)
    def _(gap):
        push(whole, all_ref, sem_a, sem_b, gap).wait_send()
        push(piece, got_ref, sem_c, sem_d, gap).wait_send()

    swap(stat_ref, sem_e, sem_f).wait_send()
    swap(term_ref, sem_g, sem_h).wait_send()


def contrast(leading, queries, positives):
    count = lax.axis_size("dp")
    halves = lax.axis_size("tensor")
    own = leading.shape[0]
    here = queries.shape[0]
    whole = pl.BlockSpec(memory_space=pltpu.VMEM)
    query_gradient, lead_back, loss = pl.pallas_call(
        functools.partial(contrast_kernel, count, own, halves),
        in_specs=[whole] * 3,
        out_specs=[whole] * 3,
        out_shape=[
            jax.ShapeDtypeStruct((here, D), jnp.float32),
            jax.ShapeDtypeStruct((own, D), jnp.float32),
            jax.ShapeDtypeStruct((8, 128), jnp.float32),
        ],
        scratch_shapes=[
            pltpu.VMEM((count, own, D), jnp.float32),
            pltpu.VMEM((count, own, D), jnp.float32),
            pltpu.VMEM((count, own, D), jnp.float32),
            pltpu.VMEM((halves, here, 128), jnp.float32),
            pltpu.VMEM((halves, here, D), jnp.float32),
            pltpu.SemaphoreType.DMA((count,)),
            pltpu.SemaphoreType.DMA((count,)),
            pltpu.SemaphoreType.DMA((count,)),
            pltpu.SemaphoreType.DMA((count,)),
            pltpu.SemaphoreType.DMA,
            pltpu.SemaphoreType.DMA,
            pltpu.SemaphoreType.DMA,
            pltpu.SemaphoreType.DMA,
        ],
        compiler_params=pltpu.CompilerParams(
            collective_id=1, has_side_effects=True, vmem_limit_bytes=big_vmem
        ),
        name="contrast",
    )(leading.astype(jnp.float32), queries, positives.reshape(here, 1))
    return query_gradient, lead_back, loss[0, 0]


def total_kernel(bits, value_ref, out_ref, slots, send_sem, recv_sem):
    me = lax.axis_index("dp")
    half = lax.axis_index("tensor")

    def partner(stage):
        if stage == bits:
            return (me, 1 - half)
        gap = 1 << stage
        up = 1 - 2 * lax.rem(me // gap, 2)
        return (me + up * gap, half)

    barrier = pltpu.get_barrier_semaphore()
    for stage in range(bits + 1):
        pl.semaphore_signal(barrier, inc=1, device_id=partner(stage), device_id_type=MESH)
    pl.semaphore_wait(barrier, bits + 1)
    out_ref[...] = value_ref[...]
    slots[0] = value_ref[...]
    copies = []
    for stage in range(bits + 1):
        copy = pltpu.make_async_remote_copy(
            src_ref=slots.at[2 * stage],
            dst_ref=slots.at[2 * stage + 1],
            send_sem=send_sem.at[stage],
            recv_sem=recv_sem.at[stage],
            device_id=partner(stage),
            device_id_type=MESH,
        )
        copy.start()
        copies.append(copy)
        copy.wait_recv()
        summed = slots[2 * stage] + slots[2 * stage + 1]
        if stage < bits:
            slots[2 * stage + 2] = summed
        else:
            out_ref[...] = summed
    for copy in copies:
        copy.wait_send()


def all_total(value):
    bits = (lax.axis_size("dp") - 1).bit_length()
    whole = pl.BlockSpec(memory_space=pltpu.VMEM)
    return pl.pallas_call(
        functools.partial(total_kernel, bits),
        in_specs=[whole],
        out_specs=whole,
        out_shape=jax.ShapeDtypeStruct(value.shape, value.dtype),
        scratch_shapes=[
            pltpu.VMEM((2 * bits + 2,) + value.shape, value.dtype),
            pltpu.SemaphoreType.DMA((bits + 1,)),
            pltpu.SemaphoreType.DMA((bits + 1,)),
        ],
        compiler_params=pltpu.CompilerParams(collective_id=2, has_side_effects=True),
        name="all_total",
    )(value)


def tensor_swap(value):
    return lax.ppermute(value, "tensor", [(0, 1), (1, 0)])


def gathered(own):
    return lax.all_gather(own, ("tensor", "dp"), axis=0, tiled=True).reshape(
        lax.axis_size("tensor"), -1, own.shape[1]
    )


def scattered(whole):
    return lax.psum_scatter(
        whole.reshape(-1, whole.shape[2]), ("tensor", "dp"), scatter_dimension=0, tiled=True
    ).astype(jnp.float32)


def row_spec(rows, columns):
    return pl.BlockSpec((rows, columns), lambda i: (i, 0))


def full_spec(shape):
    return pl.BlockSpec(shape, lambda i: (0,) * len(shape), pipeline_mode=pl.Buffered(1))


def shards(
    short_tokens,
    long_tokens,
    short_cotangent,
    long_cotangent,
    short_lengths,
    long_lengths,
    queries,
    positives,
    step_count,
    mixing_weight,
    mixing_moment,
    mixing_square,
    mixing_average,
    merging_weight,
    merging_moment,
    merging_square,
    merging_average,
    expand_weight,
    expand_moment,
    expand_square,
    expand_average,
    shrink_weight,
    shrink_moment,
    shrink_square,
    shrink_average,
    scales_weight,
    scales_moment,
    scales_square,
    scales_average,
    offsets_weight,
    offsets_moment,
    offsets_square,
    offsets_average,
):
    halves = lax.axis_size("tensor")
    place = lax.axis_index("tensor")
    short_span = short_tokens.shape[1]
    long_span = long_tokens.shape[1]
    shorts = short_tokens.shape[0] // halves
    longs = long_tokens.shape[0] // halves
    chunk = long_span
    piece = short_span
    assert shorts * short_span == chunk and shorts == longs
    chunks = longs + 1
    rows = chunks * chunk
    width = mixing_weight.shape[2]
    wide = expand_weight.shape[1]

    def own_half(short_all, long_all):
        return jnp.concatenate(
            [
                lax.dynamic_slice_in_dim(short_all, place * shorts, shorts).reshape(-1, D),
                lax.dynamic_slice_in_dim(long_all, place * longs, longs).reshape(-1, D),
            ],
            axis=0,
        )

    def both_halves(own, other):
        own_first = place == 0
        low = jnp.where(own_first, own, other)
        high = jnp.where(own_first, other, own)
        head = shorts * short_span
        return (
            jnp.concatenate([low[:head], high[:head]]).reshape(short_tokens.shape),
            jnp.concatenate([low[head:], high[head:]]).reshape(long_tokens.shape),
        )

    mixing_full = gathered(mixing_weight.astype(jnp.bfloat16).reshape(-1, 3 * width))
    merging_full = gathered(merging_weight.T.astype(jnp.bfloat16))
    expand_full = gathered(expand_weight.astype(jnp.bfloat16))
    shrink_full = gathered(shrink_weight.T.astype(jnp.bfloat16))
    offsets_other = tensor_swap(offsets_weight)
    offsets_both = jnp.where(
        place == 0,
        jnp.stack([offsets_weight, offsets_other]),
        jnp.stack([offsets_other, offsets_weight]),
    )
    mixing_bias = jnp.concatenate(
        [
            offsets_both[:, :width],
            jnp.zeros((halves, width), jnp.float32),
            offsets_both[:, width : 2 * width],
        ],
        axis=1,
    ).reshape(1, -1)
    upward_bias = offsets_both[:, 2 * width :].reshape(1, -1)
    short_limits = lax.dynamic_slice_in_dim(short_lengths, place * shorts, shorts)
    long_limits = lax.dynamic_slice_in_dim(long_lengths, place * longs, longs)
    spans = jnp.concatenate(
        [
            short_limits[None, :],
            long_limits[:, None] - piece * jnp.arange(chunk // piece, dtype=jnp.int32)[None, :],
        ],
        axis=0,
    )
    inputs = own_half(short_tokens, long_tokens)
    cotangent = own_half(short_cotangent, long_cotangent)
    bf16, f32 = jnp.bfloat16, jnp.float32

    def shaped(columns, dtype):
        return jax.ShapeDtypeStruct((rows, columns), dtype)

    smem = pl.BlockSpec(memory_space=pltpu.SMEM)
    params = pltpu.CompilerParams(vmem_limit_bytes=big_vmem)
    mixing_columns = halves * 3 * width
    scores_flops = 2 * rows * chunk * PAIR * (halves * width // HEAD_DIM)
    qkv, context = pl.pallas_call(
        functools.partial(attend_forward_kernel, piece),
        grid=(chunks,),
        in_specs=[
            smem,
            row_spec(chunk, D),
            full_spec(mixing_full.shape),
            full_spec(mixing_bias.shape),
        ],
        out_specs=[row_spec(chunk, mixing_columns), row_spec(chunk, D)],
        out_shape=[shaped(mixing_columns, bf16), shaped(D, bf16)],
        compiler_params=params,
        cost_estimate=pl.CostEstimate(
            flops=2 * rows * D * mixing_columns + 6 * scores_flops,
            bytes_accessed=16 * 1024 * 1024,
            transcendentals=rows * chunk * 12,
        ),
        name="attend_forward",
    )(spans, inputs, mixing_full, mixing_bias)
    output, hidden_low, activated, slope, normed_first, rstd_first, normed_second, rstd_second = (
        pl.pallas_call(
            feed_forward_kernel,
            grid=(chunks,),
            in_specs=[
                row_spec(chunk, D),
                row_spec(chunk, D),
                full_spec(merging_full.shape),
                full_spec(expand_full.shape),
                full_spec(shrink_full.shape),
                full_spec(scales_weight.shape),
                full_spec(upward_bias.shape),
            ],
            out_specs=[
                row_spec(chunk, D),
                row_spec(chunk, D),
                row_spec(chunk, FF),
                row_spec(chunk, FF),
                row_spec(chunk, D),
                row_spec(chunk, 1),
                row_spec(chunk, D),
                row_spec(chunk, 1),
            ],
            out_shape=[
                shaped(D, bf16),
                shaped(D, bf16),
                shaped(FF, bf16),
                shaped(FF, bf16),
                shaped(D, f32),
                shaped(1, f32),
                shaped(D, f32),
                shaped(1, f32),
            ],
            compiler_params=params,
            cost_estimate=pl.CostEstimate(
                flops=2 * rows * D * (D + 2 * FF),
                bytes_accessed=48 * 1024 * 1024,
                transcendentals=2 * rows * FF,
            ),
            name="feed_forward",
        )(
            context,
            inputs,
            merging_full,
            expand_full,
            shrink_full,
            scales_weight,
            upward_bias,
        )
    )
    output_other = tensor_swap(output)
    leading = jnp.concatenate([output[: shorts * piece : piece], output[chunk::chunk]], axis=0)
    query_gradient, lead_back, loss_part = contrast(leading, queries, positives)
    lead_rows = jnp.zeros((chunks, 8, D), f32)
    lead_rows = lead_rows.at[0, :shorts].set(lead_back[:shorts])
    lead_rows = lead_rows.at[1:, 0].set(lead_back[shorts:])
    down_low, upward_low, first_low, first_back, context_back, vector_grad, upward_grad = (
        pl.pallas_call(
            functools.partial(feed_back_kernel, piece),
            grid=(chunks,),
            in_specs=[
                row_spec(chunk, D),
                pl.BlockSpec((1, 8, D), lambda i: (i, 0, 0)),
                row_spec(chunk, D),
                row_spec(chunk, 1),
                row_spec(chunk, D),
                row_spec(chunk, 1),
                row_spec(chunk, FF),
                full_spec(merging_full.shape),
                full_spec(expand_full.shape),
                full_spec(shrink_full.shape),
                full_spec(scales_weight.shape),
            ],
            out_specs=[
                row_spec(chunk, D),
                row_spec(chunk, FF),
                row_spec(chunk, D),
                row_spec(chunk, D),
                row_spec(chunk, D),
                pl.BlockSpec((8, D), lambda i: (0, 0)),
                pl.BlockSpec((8, FF), lambda i: (0, 0)),
            ],
            out_shape=[
                shaped(D, bf16),
                shaped(FF, bf16),
                shaped(D, bf16),
                shaped(D, f32),
                shaped(D, bf16),
                jax.ShapeDtypeStruct((8, D), f32),
                jax.ShapeDtypeStruct((8, FF), f32),
            ],
            compiler_params=params,
            cost_estimate=pl.CostEstimate(
                flops=2 * rows * D * (D + 2 * FF),
                bytes_accessed=48 * 1024 * 1024,
                transcendentals=0,
            ),
            name="feed_back",
        )(
            cotangent,
            lead_rows,
            normed_first,
            rstd_first,
            normed_second,
            rstd_second,
            slope,
            merging_full,
            expand_full,
            shrink_full,
            scales_weight,
        )
    )
    shrink_sum = scattered(weight_grad(down_low, activated, halves, 512))
    expand_sum = scattered(weight_grad(hidden_low, upward_low, halves, 512))
    merging_sum = scattered(weight_grad(first_low, context, halves, 384))
    projected_back, input_back, input_low, bias_grad = pl.pallas_call(
        functools.partial(attend_back_kernel, piece),
        grid=(chunks,),
        in_specs=[
            smem,
            row_spec(chunk, mixing_columns),
            row_spec(chunk, D),
            row_spec(chunk, D),
            full_spec(mixing_full.shape),
        ],
        out_specs=[
            row_spec(chunk, mixing_columns),
            row_spec(chunk, D),
            row_spec(chunk, D),
            pl.BlockSpec((8, mixing_columns), lambda i: (0, 0)),
        ],
        out_shape=[
            shaped(mixing_columns, bf16),
            shaped(D, f32),
            shaped(D, bf16),
            jax.ShapeDtypeStruct((8, mixing_columns), f32),
        ],
        compiler_params=params,
        cost_estimate=pl.CostEstimate(
            flops=2 * rows * D * mixing_columns + 15 * scores_flops,
            bytes_accessed=24 * 1024 * 1024,
            transcendentals=rows * chunk * 12,
        ),
        name="attend_back",
    )(spans, qkv, context_back, first_back, mixing_full)
    input_other = tensor_swap(input_low)
    mixing_sum = scattered(weight_grad(inputs, projected_back, halves, 384))

    short_output, long_output = both_halves(output, output_other)
    short_gradient, long_gradient = both_halves(input_back, input_other.astype(f32))

    bias_both = bias_grad[0].reshape(halves, 3, width)
    offsets_grad = jnp.concatenate(
        [bias_both[:, 0], bias_both[:, 2], upward_grad[0].reshape(halves, wide)], axis=1
    )
    reduced = (mixing_sum.reshape(mixing_weight.shape), merging_sum.T, expand_sum, shrink_sum.T)
    squares_part = jnp.sum(mixing_sum * mixing_sum) + jnp.sum(merging_sum * merging_sum)
    squares_part = squares_part + jnp.sum(expand_sum * expand_sum)
    squares_part = squares_part + jnp.sum(shrink_sum * shrink_sum)
    lane = lax.broadcasted_iota(jnp.int32, (1, D), 1)
    scalars = jnp.where(lane == 0, squares_part, jnp.where(lane == 1, loss_part, 0.0))
    stacked = jnp.concatenate(
        [vector_grad[:6], offsets_grad.reshape(-1, D), scalars, jnp.zeros((3, D), f32)], axis=0
    )
    summed = all_total(stacked)
    scales_sum = summed[:6]
    offsets_all = summed[6:12].reshape(halves, -1)
    offsets_sum = jnp.where(place == 0, offsets_all[0], offsets_all[1])
    squares_all = summed[12, 0] + jnp.sum(summed[:12] * summed[:12])
    loss_all = summed[12, 1] / halves
    norm_value = jnp.sqrt(squares_all)
    factor = clip_limit / jnp.maximum(norm_value, clip_limit)
    steps_float = step_count[0].astype(jnp.float32)
    first_fix = 1.0 - jnp.power(first_decay, steps_float)
    second_fix = 1.0 - jnp.power(second_decay, steps_float)

    def update(weight, moment, square, average, gradient, rate):
        clipped = gradient * factor
        first = first_decay * moment + (1.0 - first_decay) * clipped
        second = second_decay * square + (1.0 - second_decay) * clipped * clipped
        master = weight - rate * (
            first / first_fix / (jnp.sqrt(second / second_fix) + adam_eps) + decay_weight * weight
        )
        smooth = smooth_decay * average + (1.0 - smooth_decay) * master
        return (master, first, second, smooth)

    mixing_new = update(
        mixing_weight, mixing_moment, mixing_square, mixing_average, reduced[0], 1.0 / math.sqrt(D)
    )
    merging_new = update(
        merging_weight,
        merging_moment,
        merging_square,
        merging_average,
        reduced[1],
        8.0 / math.sqrt(D),
    )
    expand_new = update(
        expand_weight, expand_moment, expand_square, expand_average, reduced[2], 1.0 / math.sqrt(D)
    )
    shrink_new = update(
        shrink_weight, shrink_moment, shrink_square, shrink_average, reduced[3], 1.0 / math.sqrt(FF)
    )
    scales_new = update(
        scales_weight, scales_moment, scales_square, scales_average, scales_sum, 0.3
    )
    offsets_new = update(
        offsets_weight, offsets_moment, offsets_square, offsets_average, offsets_sum, 0.3
    )
    contrast_loss = (loss_all / (queries.shape[0] * lax.axis_size("dp"))).reshape(1)
    gradient_norm = norm_value.reshape(1)
    return (
        (
            short_output,
            long_output,
            short_gradient,
            long_gradient,
            query_gradient,
            contrast_loss,
            gradient_norm,
        )
        + mixing_new
        + merging_new
        + expand_new
        + shrink_new
        + scales_new
        + offsets_new
    )


def solution(mesh):
    placed = (
        P("dp", None, None),
        P("dp", None, None),
        P("dp", None, None),
        P("dp", None, None),
        P("dp"),
        P("dp"),
        P("dp", None),
        P("dp"),
        P(),
        P("dp", None, "tensor"),
        P("dp", None, "tensor"),
        P("dp", None, "tensor"),
        P("dp", None, "tensor"),
        P("tensor", "dp"),
        P("tensor", "dp"),
        P("tensor", "dp"),
        P("tensor", "dp"),
        P("dp", "tensor"),
        P("dp", "tensor"),
        P("dp", "tensor"),
        P("dp", "tensor"),
        P("tensor", "dp"),
        P("tensor", "dp"),
        P("tensor", "dp"),
        P("tensor", "dp"),
        P(),
        P(),
        P(),
        P(),
        P("tensor"),
        P("tensor"),
        P("tensor"),
        P("tensor"),
    )
    return jax.shard_map(
        shards,
        mesh=mesh,
        in_specs=placed,
        out_specs=(
            P("dp", None, None),
            P("dp", None, None),
            P("dp", None, None),
            P("dp", None, None),
            P("dp", None),
            P(),
            P(),
            P("dp", None, "tensor"),
            P("dp", None, "tensor"),
            P("dp", None, "tensor"),
            P("dp", None, "tensor"),
            P("tensor", "dp"),
            P("tensor", "dp"),
            P("tensor", "dp"),
            P("tensor", "dp"),
            P("dp", "tensor"),
            P("dp", "tensor"),
            P("dp", "tensor"),
            P("dp", "tensor"),
            P("tensor", "dp"),
            P("tensor", "dp"),
            P("tensor", "dp"),
            P("tensor", "dp"),
            P(),
            P(),
            P(),
            P(),
            P("tensor"),
            P("tensor"),
            P("tensor"),
            P("tensor"),
        ),
        check_vma=False,
    )
```

time: 1420 us -> 837 us (0.59)
  waiting for transfers between devices: 829 us -> 557 us
  matrix products: 236 us -> 0 us
  Pallas kernels: 0 us -> 189 us
  blocking collectives: 129 us -> 0 us
  local copies, waits for them, and re-layouts: 84.9 us -> 17.2 us
  other arithmetic: 106 us -> 42.7 us
    psum x4 -> x0, waiting for transfers between devices: 662 us -> none  [tensor_total(): return lax.psum(partial_rows, 'tensor')]
    dot_general x27 -> x0, matrix products: 236 us -> none  [the longest x1 44.2 us: shards(): jnp.dot(hidden_low, expand_full, preferred_element_type=jnp.float32)]
    pallas_call x0 -> x10, Pallas kernels: none -> 189 us  [the longest x4 40 us: weight_grad(): pl.pallas_call(weight_grad_kernel, grid=(columns // tile,), in_specs=[pl....]
    reduce_scatter x5 -> x4, waiting for transfers between devices: 113 us -> 284 us  [scattered(): lax.psum_scatter(whole.reshape(-1, whole.shape[2]), ('tensor', 'dp'), sca...]
    all_gather x3 -> x4, waiting for transfers between devices: 53.8 us -> 217 us  [gathered(): lax.all_gather(own, ('tensor', 'dp'), axis=0, tiled=True)]
    psum x2 -> x0, blocking collectives: 80.8 us -> none  [the longest x1 40.7 us: shards(): lax.psum((scales_term, offsets_slots), ('dp', 'tensor'))]
    reduce_sum x28 -> x5, other arithmetic: 65.8 us -> 7.62 us  [the longest x1 1.66 us: shards(): squares_part = squares_part + jnp.sum(shrink_sum * shrink_sum)]
    ppermute x0 -> x3, waiting for transfers between devices: none -> 55.6 us  [tensor_swap(): return lax.ppermute(value, 'tensor', [(0, 1), (1, 0)])]
  transfers between devices with their start and end apart: 12 -> 11, of which waited for: 8 -> 10; matrix products, arithmetic and copies ran while one was open for 20% -> 4% of each run, Pallas kernels for 0% -> 11%
where the time goes in v1:
time: 837 us; the launch traced here: 835 us
  waiting for transfers between devices  557 us (67%)
  Pallas kernels  189 us (23%)
  other arithmetic  42.7 us (5%)
  between operations  22.3 us (3%)
  local copies, waits for them, and re-layouts  17.2 us (2%)
    reduce_scatter x4, waiting for transfers between devices, scattered(): lax.psum_scatter(whole.reshape(-1, whole.shape[2]), ('tensor', 'dp'), sca...  284 us
    all_gather x4, waiting for transfers between devices, gathered(): lax.all_gather(own, ('tensor', 'dp'), axis=0, tiled=True)  217 us
    ppermute x3, waiting for transfers between devices, tensor_swap(): return lax.ppermute(value, 'tensor', [(0, 1), (1, 0)])  55.6 us
    pallas_call x4, Pallas kernels, weight_grad(): pl.pallas_call(weight_grad_kernel, grid=(columns // tile,), in_specs=[pl....  40 us
    pallas_call x1, Pallas kernels, shards(): pl.pallas_call(functools.partial(attend_back_kernel, piece), grid=(chunks...  35.3 us
    pallas_call x1, Pallas kernels, shards(): pl.pallas_call(functools.partial(feed_back_kernel, piece), grid=(chunks,)...  27.4 us
    pallas_call x1, Pallas kernels, shards(): pl.pallas_call(feed_forward_kernel, grid=(chunks,), in_specs=[row_spec(ch...  26.4 us
    pallas_call x1, Pallas kernels, contrast(): pl.pallas_call(functools.partial(contrast_kernel, count, own, halves), in...  23.5 us
  transfers between devices with their start and end apart: 11, of which 10 were waited for; matrix products, arithmetic and copies ran while one was open for 4% of the time, Pallas kernels for 11%

profile of v1, /device:TPU:0, one launch (start us, length us, event | category | flops | bytes accessed | tf_op | source)
XLA Modules:
  0.0 835.1 jit_solution(9654683373863995366)
XLA Ops:
  10.7 1.6 convert_element_type.43
  12.4 1.6 convert_bitcast_fusion
  14.1 3.0 collective-permute-start
  19.1 1.8 constant_dynamic-slice_fusion
  26.4 47.9 %all-gather.5.cloned.1.call-done = bf16[1536,1152]{1,0:T(8,128)(2,1)} async-done(((bf16[48,1152]{1,0:T(8,128)(2,1)}), bf16[1536,1152]{1,0:T(8,128)(2,1)}) %all-gather.5.cloned.1.call-update) | async-done | bytes 3538960 | tf_op jit(solution)/shard_map/all_gather | solution.py:497
  74.3 18.8 %attend_forward.1 = (bf16[1280,2304]{1,0:T(8,128)(2,1)}, bf16[1280,768]{1,0:T(8,128)(2,1)}) custom-call(s32[5,4]{1,0:T(8,128)} %pad_add_fusion.spans, bf16[1280,768]{1,0:T(8,128)(2,1)} %pad_maximum_fusion.2.x_ref.left_ref, bf16[2,768,1152]{2,1,0:T(8,128)(2,1)} %bitcast.105, f32[1,2304]{1,0:T(1,128)} %bitcast.99), custom_call_target="tpu_custom_call" | custom-call | flops 10569646080 | bytes 16777216 | tf_op jit(solution)/shard_map/attend_forward/pallas_call | solution.py:623
  93.0 37.5 %all-gather.7.cloned.1.call-done = bf16[1536,384]{1,0:T(8,128)(2,1)} async-done(((bf16[48,384]{1,0:T(8,128)(2,1)}), bf16[1536,384]{1,0:T(8,128)(2,1)}) %all-gather.7.cloned.1.call-update) | async-done | bytes 1179664 | tf_op jit(solution)/shard_map/all_gather | solution.py:497
  130.5 66.0 %all-gather.9.cloned.1.call-done = bf16[1536,1536]{1,0:T(8,128)(2,1)} async-done(((bf16[48,1536]{1,0:T(8,128)(2,1)}), bf16[1536,1536]{1,0:T(8,128)(2,1)}) %all-gather.9.cloned.1.call-update) | async-done | bytes 4718608 | tf_op jit(solution)/shard_map/all_gather | solution.py:497
  196.6 65.7 %all-gather.11.cloned.1.call-done = bf16[1536,1536]{1,0:T(8,128)(2,1)} async-done(((bf16[48,1536]{1,0:T(8,128)(2,1)}), bf16[1536,1536]{1,0:T(8,128)(2,1)}) %all-gather.11.cloned.1.call-update) | async-done | bytes 4718608 | tf_op jit(solution)/shard_map/all_gather | solution.py:497
  262.3 26.4 %feed_forward.1 = (bf16[1280,768]{1,0:T(8,128)(2,1)}, bf16[1280,768]{1,0:T(8,128)(2,1)}, bf16[1280,3072]{1,0:T(8,128)(2,1)}, bf16[1280,3072]{1,0:T(8,128)(2,1)},...) custom-call(bf16[1280,768]{1,0:T(8,128)(2,1)} %get-tuple-element.79.ctx_ref.right_ref, ...), custom_call_target="tpu_custom_call" | custom-call | flops 13589544960 | bytes 50331648 | tf_op jit(solution)/shard_map/feed_forward/pallas_call | solution.py:643
  291.8 23.5 %contrast.1 = (f32[16,768]{1,0:T(8,128)}, f32[8,768]{1,0:T(8,128)}, f32[8,128]{1,0:T(8,128)}) custom-call(f32[8,768]{1,0:T(8,128)} %maximum_convert_fusion.cls_ref, bf16[16,768]{1,0:T(8,128)(2,1)} %q_ref.1, s32[16,1]{1,0:T(8,128)} %copy.79.pos_ref), custom_call_target="tpu_custom_call" | custom-call | tf_op jit(solution)/shard_map/contrast/pallas_call | solution.py:403
  317.1 27.4 %feed_back.1 = (bf16[1280,768]{1,0:T(8,128)(2,1)}, bf16[1280,3072]{1,0:T(8,128)(2,1)}, bf16[1280,768]{1,0:T(8,128)(2,1)}, f32[1280,768]{1,0:T(8,128)}, bf16[1280...) custom-call(bf16[1280,768]{1,0:T(8,128)(2,1)} %pad_maximum_fusion.3.cot_ref, f32[5,8,768]{2,1,0:T(8,128)} %copy-done.19, ...), custom_call_target="tpu_custom_call" | custom-call | flops 13589544960 | bytes 50331648 | tf_op jit(solution)/shard_map/feed_back/pallas_call | solution.py:699
  344.5 5.6 weight_grad.5
  350.2 35.3 %attend_back.1 = (bf16[1280,2304]{1,0:T(8,128)(2,1)}, f32[1280,768]{1,0:T(8,128)}, bf16[1280,768]{1,0:T(8,128)(2,1)}, f32[8,2304]{1,0:T(8,128)}) custom-call(s32[5,4]{1,0:T(8,128)} %pad_add_fusion.spans, bf16[1280,2304]{1,0:T(8,128)(2,1)} %get-tuple-element.81.qkv_ref, bf16[1280,768]{1,0:T(8,128)(2,1)} %get-tuple-element.88.dctx_ref, ...), custom_call_target="tpu_custom_call" | custom-call | flops 19629342720 | bytes 25165824 | tf_op jit(solution)/shard_map/attend_back/pallas_call | solution.py:757
  385.5 11.1 %weight_grad.4 = bf16[2,768,1152]{2,1,0:T(8,128)(2,1)} custom-call(bf16[1280,768]{1,0:T(8,128)(2,1)} %pad_maximum_fusion.2.x_ref.left_ref, bf16[1280,2304]{1,0:T(8,128)(2,1)} %get-tuple-element.96.right_ref), custom_call_target="tpu_custom_call" | custom-call | flops 4529848320 | bytes 11403264 | tf_op jit(solution)/shard_map/weight_grad/pallas_call | solution.py:249
  396.9 11.6 %weight_grad.6 = bf16[2,768,1536]{2,1,0:T(8,128)(2,1)} custom-call(bf16[1280,768]{1,0:T(8,128)(2,1)} %get-tuple-element.98.left_ref, bf16[1280,3072]{1,0:T(8,128)(2,1)} %get-tuple-element.99.right_ref), custom_call_target="tpu_custom_call" | custom-call | flops 6039797760 | bytes 14548992 | tf_op jit(solution)/shard_map/weight_grad/pallas_call | solution.py:249
  408.6 11.6 %weight_grad.7 = bf16[2,768,1536]{2,1,0:T(8,128)(2,1)} custom-call(bf16[1280,768]{1,0:T(8,128)(2,1)} %get-tuple-element.100.left_ref, bf16[1280,3072]{1,0:T(8,128)(2,1)} %get-tuple-element.101.right_ref), custom_call_target="tpu_custom_call" | custom-call | flops 6039797760 | bytes 14548992 | tf_op jit(solution)/shard_map/weight_grad/pallas_call | solution.py:249
  427.7 22.9 %reduce-scatter.7.cloned.1.call-done = bf16[48,384]{1,0:T(8,128)(2,1)} async-done(((bf16[1536,384]{1,0:T(8,128)(2,1)}), bf16[48,384]{1,0:T(8,128)(2,1)}) %reduce-scatter.7.cloned.1.call-update) | async-done | bytes 36880 | tf_op jit(solution)/shard_map/reduce_scatter | solution.py:503
  452.0 14.6 %collective-permute-done.2 = bf16[1280,768]{1,0:T(8,128)(2,1)} collective-permute-done((bf16[1280,768]{1,0:T(8,128)(2,1)}, bf16[1280,768]{1,0:T(8,128)(2,1)}, u32[]{:S(2)}, u32[]{:S(2)}) %collective-permute-start.2) | collective-permute-done | bytes 1966112 | tf_op jit(solution)/shard_map/ppermute | solution.py:493
  466.6 3.4 convert_select_fusion.1
  470.6 41.0 %collective-permute-done.1 = bf16[1280,768]{1,0:T(8,128)(2,1)} collective-permute-done((bf16[1280,768]{1,0:T(8,128)(2,1)S(1)}, bf16[1280,768]{1,0:T(8,128)(2,1)}, u32[]{:S(2)}, u32[]{:S(2)}) %collective-permute-start.1) | collective-permute-done | bytes 1966112 | tf_op jit(solution)/shard_map/ppermute | solution.py:493
  511.6 1.8 broadcast_select_fusion.1
  515.9 1.9 pad_maximum_fusion.1
  517.7 3.1 pad_maximum_fusion
  520.9 43.1 %reduce-scatter.5.cloned.1.call-done = bf16[48,1152]{1,0:T(8,128)(2,1)} async-done(((bf16[1536,1152]{1,0:T(8,128)(2,1)}), bf16[48,1152]{1,0:T(8,128)(2,1)}) %reduce-scatter.5.cloned.1.call-update) | async-done | bytes 110608 | tf_op jit(solution)/shard_map/reduce_scatter | solution.py:503
  566.8 108.5 %reduce-scatter.9.cloned.1.call-done = bf16[48,1536]{1,0:T(8,128)(2,1)} async-done(((bf16[1536,1536]{1,0:T(8,128)(2,1)}), bf16[48,1536]{1,0:T(8,128)(2,1)}) %reduce-scatter.9.cloned.1.call-update) | async-done | bytes 147472 | tf_op jit(solution)/shard_map/reduce_scatter | solution.py:503
  675.3 1.6 fusion.2
  677.6 110.1 %reduce-scatter.11.cloned.1.call-done = bf16[48,1536]{1,0:T(8,128)(2,1)} async-done(((bf16[1536,1536]{1,0:T(8,128)(2,1)}), bf16[48,1536]{1,0:T(8,128)(2,1)}) %reduce-scatter.11.cloned.1.call-update) | async-done | bytes 147472 | tf_op jit(solution)/shard_map/reduce_scatter | solution.py:503
  787.7 1.7 fusion.3
  792.1 17.8 %all_total.1 = f32[16,768]{1,0:T(8,128)} custom-call(f32[16,768]{1,0:T(8,128)} %maximum_maximum_fusion.value_ref), custom_call_target="tpu_custom_call" | custom-call | tf_op jit(solution)/shard_map/all_total/pallas_call | solution.py:477
  819.3 2.0 multiply_add_fusion.2
  821.3 1.7 multiply_add_fusion.3
  (134 shorter events, 41.2 us)
Async XLA Ops:
  7.2 10.7 %copy-start = (s32[8]{0:T(128)S(1)}, s32[8]{0:T(128)}, u32[]{:S(2)}) copy-start(s32[8]{0:T(128)} %param.41) | copy-start | bytes 100
  7.2 11.9 %copy-start.6 = (bf16[8,256,768]{2,1,0:T(8,128)(2,1)S(1)}, bf16[8,256,768]{2,1,0:T(8,128)(2,1)}, u32[]{:S(2)}) copy-start(bf16[8,256,768]{2,1,0:T(8,128)(2,1)} %param.40) | copy-start | bytes 9437188
  7.2 67.0 %all-gather.5.cloned.1.call-start = ((), (), s32[]{:S(2)}) async-start(), calls=%async_computation.4 | async-start | bytes 3649536 | tf_op jit(solution)/shard_map/all_gather | solution.py:497
  9.1 121.5 %all-gather.7.cloned.1.call-start = ((), (), s32[]{:S(2)}) async-start(), calls=%async_computation.5 | async-start | bytes 1216512 | tf_op jit(solution)/shard_map/all_gather | solution.py:497
  10.6 185.9 %all-gather.9.cloned.1.call-start = ((), (), s32[]{:S(2)}) async-start(), calls=%async_computation.6 | async-start | bytes 4866048 | tf_op jit(solution)/shard_map/all_gather | solution.py:497
  12.4 249.9 %all-gather.11.cloned.1.call-start = ((), (), s32[]{:S(2)}) async-start(), calls=%async_computation.7 | async-start | bytes 4866048 | tf_op jit(solution)/shard_map/all_gather | solution.py:497
  14.1 436.5 %reduce-scatter.7.cloned.1.call-start = ((), (), s32[]{:S(2)}) async-start(), calls=%async_computation.9 | async-start | bytes 1216512 | tf_op jit(solution)/shard_map/reduce_scatter | solution.py:503
  14.1 11.0 %collective-permute-start = (f32[2304]{0:T(1024)}, f32[2304]{0:T(1024)S(1)}, u32[]{:S(2)}, u32[]{:S(2)}) collective-permute-start(f32[2304]{0:T(1024)} %param.66), channel_id=1, source_target_pairs={{0,1},{1,0},{2,3},{3,2},{4,5},{5,4},{6,7},{7,6},{8,9},{9,8},{10,11... | collective-permute-start | bytes 27656 | tf_op jit(solution)/shard_map/ppermute | solution.py:493
  350.2 213.8 %reduce-scatter.5.cloned.1.call-start = ((), (), s32[]{:S(2)}) async-start(), calls=%async_computation.8 | async-start | bytes 3649536 | tf_op jit(solution)/shard_map/reduce_scatter | solution.py:503
  396.7 278.6 %reduce-scatter.9.cloned.1.call-start = ((), (), s32[]{:S(2)}) async-start(), calls=%async_computation.10 | async-start | bytes 4866048 | tf_op jit(solution)/shard_map/reduce_scatter | solution.py:503
  408.6 379.1 %reduce-scatter.11.cloned.1.call-start = ((), (), s32[]{:S(2)}) async-start(), calls=%async_computation.11 | async-start | bytes 4866048 | tf_op jit(solution)/shard_map/reduce_scatter | solution.py:503
  420.3 46.3 %collective-permute-start.2 = (bf16[1280,768]{1,0:T(8,128)(2,1)}, bf16[1280,768]{1,0:T(8,128)(2,1)}, u32[]{:S(2)}, u32[]{:S(2)}) collective-permute-start(bf16[1280,768]{1,0:T(8,128)(2,1)} %get-tuple-element.91), channel_id=1, source_target_pairs={{0,1},{1,0},{2,3},{3,2},{4,5},{5,4},{6,7},{7,6},{8,9},{9,8},{10,11... | collective-permute-start | bytes 5898248 | tf_op jit(solution)/shard_map/ppermute | solution.py:493
  421.8 89.8 %collective-permute-start.1 = (bf16[1280,768]{1,0:T(8,128)(2,1)S(1)}, bf16[1280,768]{1,0:T(8,128)(2,1)}, u32[]{:S(2)}, u32[]{:S(2)}) collective-permute-start(bf16[1280,768]{1,0:T(8,128)(2,1)S(1)} %copy-done.2), channel_id=1, source_target_pairs={{0,1},{1,0},{2,3},{3,2},{4,5},{5,4},{6,7},{7,6},{8,9},{9,8},{10,11... | collective-permute-start | bytes 5898248 | tf_op jit(solution)/shard_map/ppermute | solution.py:493
  517.7 299.3 %copy-start.23 = (f32[2304]{0:T(1024)S(1)}, f32[2304]{0:T(1024)}, u32[]{:S(2)}) copy-start(f32[2304]{0:T(1024)} %param.69) | copy-start | bytes 27652
  517.7 301.6 %copy-start.5 = (f32[48,3,384]{2,0,1:T(8,128)S(1)}, f32[48,3,384]{2,0,1:T(8,128)}, u32[]{:S(2)}) copy-start(f32[48,3,384]{2,0,1:T(8,128)} %param.46) | copy-start | bytes 663556
  517.7 301.6 %copy-start.16 = (f32[48,3,384]{2,0,1:T(8,128)S(1)}, f32[48,3,384]{2,0,1:T(8,128)}, u32[]{:S(2)}) copy-start(f32[48,3,384]{2,0,1:T(8,128)} %param.49) | copy-start | bytes 663556
  517.7 301.6 %copy-start.17 = (f32[48,3,384]{2,0,1:T(8,128)S(1)}, f32[48,3,384]{2,0,1:T(8,128)}, u32[]{:S(2)}) copy-start(f32[48,3,384]{2,0,1:T(8,128)} %param.48) | copy-start | bytes 663556
  520.9 300.4 %copy-start.15 = (f32[384,48]{0,1:T(8,128)S(1)}, f32[384,48]{0,1:T(8,128)}, u32[]{:S(2)}) copy-start(f32[384,48]{0,1:T(8,128)} %param.50) | copy-start | bytes 221188
  520.9 300.4 %copy-start.18 = (bf16[48,384]{1,0:T(8,128)(2,1)S(1)}, bf16[48,384]{1,0:T(8,128)(2,1)}, u32[]{:S(2)}) copy-start(bf16[48,384]{1,0:T(8,128)(2,1)} %reduce-scatter.7.cloned.1.call-done) | copy-start | bytes 110596
  520.9 300.4 %copy-start.20 = (f32[384,48]{0,1:T(8,128)S(1)}, f32[384,48]{0,1:T(8,128)}, u32[]{:S(2)}) copy-start(f32[384,48]{0,1:T(8,128)} %param.53) | copy-start | bytes 221188
  520.9 302.1 %copy-start.3 = (f32[1536,48]{0,1:T(8,128)S(1)}, f32[1536,48]{0,1:T(8,128)}, u32[]{:S(2)}) copy-start(f32[1536,48]{0,1:T(8,128)} %param.58) | copy-start | bytes 884740
  520.9 302.1 %copy-start.9 = (f32[1536,48]{0,1:T(8,128)S(1)}, f32[1536,48]{0,1:T(8,128)}, u32[]{:S(2)}) copy-start(f32[1536,48]{0,1:T(8,128)} %param.61) | copy-start | bytes 884740
  520.9 302.1 %copy-start.10 = (f32[1536,48]{0,1:T(8,128)S(1)}, f32[1536,48]{0,1:T(8,128)}, u32[]{:S(2)}) copy-start(f32[1536,48]{0,1:T(8,128)} %param.60) | copy-start | bytes 884740
  520.9 302.1 %copy-start.11 = (f32[1536,48]{0,1:T(8,128)S(1)}, f32[1536,48]{0,1:T(8,128)}, u32[]{:S(2)}) copy-start(f32[1536,48]{0,1:T(8,128)} %param.59) | copy-start | bytes 884740
  676.9 147.3 %copy-start.4 = (f32[48,1536]{1,0:T(8,128)S(1)}, f32[48,1536]{1,0:T(8,128)}, u32[]{:S(2)}) copy-start(f32[48,1536]{1,0:T(8,128)} %param.54) | copy-start | bytes 884740
  676.9 147.3 %copy-start.7 = (bf16[48,1536]{1,0:T(8,128)(2,1)S(1)}, bf16[48,1536]{1,0:T(8,128)(2,1)}, u32[]{:S(2)}) copy-start(bf16[48,1536]{1,0:T(8,128)(2,1)} %reduce-scatter.9.cloned.1.call-done) | copy-start | bytes 442372
  676.9 147.3 %copy-start.12 = (f32[48,1536]{1,0:T(8,128)S(1)}, f32[48,1536]{1,0:T(8,128)}, u32[]{:S(2)}) copy-start(f32[48,1536]{1,0:T(8,128)} %param.57) | copy-start | bytes 884740
  676.9 147.3 %copy-start.13 = (f32[48,1536]{1,0:T(8,128)S(1)}, f32[48,1536]{1,0:T(8,128)}, u32[]{:S(2)}) copy-start(f32[48,1536]{1,0:T(8,128)} %param.56) | copy-start | bytes 884740
  676.9 147.3 %copy-start.14 = (f32[48,1536]{1,0:T(8,128)S(1)}, f32[48,1536]{1,0:T(8,128)}, u32[]{:S(2)}) copy-start(f32[48,1536]{1,0:T(8,128)} %param.55) | copy-start | bytes 884740
  787.7 35.3 %copy-start.8 = (bf16[48,1536]{1,0:T(8,128)(2,1)S(1)}, bf16[48,1536]{1,0:T(8,128)(2,1)}, u32[]{:S(2)}) copy-start(bf16[48,1536]{1,0:T(8,128)(2,1)} %reduce-scatter.11.cloned.1.call-done) | copy-start | bytes 442372
  819.3 6.7 copy-start.1
  821.3 4.1 copy-start.21
  (4 other events, 9.0 us)
Sparse Core Ops, SparseCore 0:
  11.5 62.7 all-gather.4
  77.7 52.7 all-gather.6
  134.0 62.5 all-gather.8
  199.9 62.3 all-gather.10
  350.3 100.2 reduce-scatter.6
  455.9 108.0 reduce-scatter.4
  569.4 105.7 reduce-scatter.8
  681.7 105.9 reduce-scatter.10

commit v2 on v1

--- a/solution.py
+++ b/solution.py
@@ -78,40 +78,46 @@
     return jnp.where(lane < HEAD_DIM, low, high)
 
 
+def attend_half(half, weight, bias, visible, x_ref, qkv_ref, ctx_ref):
+    width = weight.shape[1] // 3
+    base = half * 3 * width
+    projected = dot_nn(x_ref[...], weight) + bias
+    qkv_ref[:, base : base + 3 * width] = projected.astype(jnp.bfloat16)
+    for pair in range(width // PAIR):
+        at = base + pair * PAIR
+        q = qkv_ref[:, at : at + PAIR] * jnp.bfloat16(score_scale)
+        k = qkv_ref[:, at + width : at + width + PAIR]
+        v = qkv_ref[:, at + 2 * width : at + 2 * width + PAIR]
+        parts = []
+        for which in range(2):
+            scores = jnp.where(visible, dot_nt(own_lanes(q, which), k), masked_value)
+            powered = jnp.exp(scores - jnp.max(scores, axis=-1, keepdims=True))
+            weights = powered * (1.0 / jnp.sum(powered, axis=-1, keepdims=True))
+            parts.append(dot_nn(weights.astype(jnp.bfloat16), v))
+        at = half * width + pair * PAIR
+        ctx_ref[:, at : at + PAIR] = join_lanes(*parts).astype(jnp.bfloat16)
+
+
 def attend_forward_kernel(piece, spans, x_ref, w_ref, bias_ref, qkv_ref, ctx_ref):
     step = pl.program_id(0)
     rows = x_ref.shape[0]
     width = w_ref.shape[2] // 3
     visible = visible_keys(spans, step, rows, piece, 1)
     for half in range(w_ref.shape[0]):
-        base = half * 3 * width
-        projected = dot_nn(x_ref[...], w_ref[half]) + bias_ref[:, base : base + 3 * width]
-        qkv_ref[:, base : base + 3 * width] = projected.astype(jnp.bfloat16)
-        for pair in range(width // PAIR):
-            at = base + pair * PAIR
-            q = qkv_ref[:, at : at + PAIR] * jnp.bfloat16(score_scale)
-            k = qkv_ref[:, at + width : at + width + PAIR]
-            v = qkv_ref[:, at + 2 * width : at + 2 * width + PAIR]
-            parts = []
-            for which in range(2):
-                scores = jnp.where(visible, dot_nt(own_lanes(q, which), k), masked_value)
-                powered = jnp.exp(scores - jnp.max(scores, axis=-1, keepdims=True))
-                weights = powered * (1.0 / jnp.sum(powered, axis=-1, keepdims=True))
-                parts.append(dot_nn(weights.astype(jnp.bfloat16), v))
-            at = half * width + pair * PAIR
-            ctx_ref[:, at : at + PAIR] = join_lanes(*parts).astype(jnp.bfloat16)
+        bias = bias_ref[:, half * 3 * width : (half + 1) * 3 * width]
+        attend_half(half, w_ref[half], bias, visible, x_ref, qkv_ref, ctx_ref)
 
 
 def feed_forward_kernel(
-    ctx_ref, x_ref, mt_ref, e_ref, st_ref, scales_ref, bu_ref,
+    ctx_ref, x_ref, me_ref, st_ref, scales_ref, bu_ref,
     out_ref, hb_ref, g_ref, slope_ref, n1_ref, r1_ref, n2_ref, r2_ref,
 ):
-    width = mt_ref.shape[2]
-    wide = e_ref.shape[2]
+    wide = st_ref.shape[2]
+    width = me_ref.shape[2] - wide
     attention = scales_ref[4:5, :]
-    for half in range(mt_ref.shape[0]):
+    for half in range(me_ref.shape[0]):
         attention = attention + dot_nt(
-            ctx_ref[:, half * width : (half + 1) * width], mt_ref[half]
+            ctx_ref[:, half * width : (half + 1) * width], me_ref[half, :, :width]
         )
     normed, rstd = layer_stats(x_ref[...].astype(jnp.float32) + attention)
     n1_ref[...] = normed
@@ -120,9 +126,9 @@
     hidden_low = hidden.astype(jnp.bfloat16)
     hb_ref[...] = hidden_low
     downward = scales_ref[5:6, :]
-    for half in range(e_ref.shape[0]):
+    for half in range(st_ref.shape[0]):
         at = half * wide
-        upward = dot_nn(hidden_low, e_ref[half]) + bu_ref[:, at : at + wide]
+        upward = dot_nn(hidden_low, me_ref[half, :, width:]) + bu_ref[:, at : at + wide]
         cumulative = 0.5 * (1.0 + lax.erf(upward * inverse_root_two))
         density = jnp.exp(-0.5 * upward * upward) * inverse_root_tau
         activated = (upward * cumulative).astype(jnp.bfloat16)
@@ -140,7 +146,7 @@
 
 
 def feed_back_kernel(
-    piece, cot_ref, lead_ref, n1_ref, r1_ref, n2_ref, r2_ref, slope_ref, mt_ref, e_ref, st_ref, scales_ref,
+    piece, cot_ref, lead_ref, n1_ref, r1_ref, n2_ref, r2_ref, slope_ref, me_ref, st_ref, scales_ref,
     dz_ref, dub_ref, da_ref, dr1_ref, dctx_ref, vec_ref, up_ref,
 ):
     @pl.when(pl.program_id(0) == 0)
@@ -148,8 +154,8 @@
         vec_ref[...] = jnp.zeros_like(vec_ref)
         up_ref[...] = jnp.zeros_like(up_ref)
 
-    width = mt_ref.shape[2]
-    wide = e_ref.shape[2]
+    wide = st_ref.shape[2]
+    width = me_ref.shape[2] - wide
     dout = cot_ref[...].astype(jnp.float32)
     row = lax.broadcasted_iota(jnp.int32, dout.shape, 0)
     for index in range(dout.shape[0] // piece):
@@ -162,13 +168,13 @@
     low = second.astype(jnp.bfloat16)
     dz_ref[...] = low
     hidden_back = second
-    for half in range(e_ref.shape[0]):
+    for half in range(st_ref.shape[0]):
         at = half * wide
         upward = dot_nn(low, st_ref[half]) * slope_ref[:, at : at + wide].astype(jnp.float32)
         up_ref[0:1, at : at + wide] += jnp.sum(upward, axis=0, keepdims=True)
         upward_low = upward.astype(jnp.bfloat16)
         dub_ref[:, at : at + wide] = upward_low
-        hidden_back = hidden_back + dot_nt(upward_low, e_ref[half])
+        hidden_back = hidden_back + dot_nt(upward_low, me_ref[half, :, width:])
     normed = n1_ref[...]
     add_row(vec_ref, 0, hidden_back * normed)
     add_row(vec_ref, 1, hidden_back)
@@ -177,8 +183,8 @@
     dr1_ref[...] = first
     low = first.astype(jnp.bfloat16)
     da_ref[...] = low
-    for half in range(mt_ref.shape[0]):
-        dctx_ref[:, half * width : (half + 1) * width] = dot_nn(low, mt_ref[half]).astype(
+    for half in range(me_ref.shape[0]):
+        dctx_ref[:, half * width : (half + 1) * width] = dot_nn(low, me_ref[half, :, :width]).astype(
             jnp.bfloat16
         )
 
@@ -320,7 +326,7 @@
     def _(gap):
         landed(whole, all_ref, sem_a, sem_b, gap).wait_recv()
 
-    passages = all_ref[...].reshape(count * own, D).astype(jnp.bfloat16)
+    passages = all_ref[...].astype(jnp.float32).reshape(count * own, D).astype(jnp.bfloat16)
     queries = q_ref[...]
     logits = dot_nt(queries, passages)
     column = lax.broadcasted_iota(jnp.int32, logits.shape, 1)
@@ -364,7 +370,7 @@
     loss_ref[...] = jnp.broadcast_to(jnp.sum(losses, axis=0, keepdims=True), loss_ref.shape)
     logit_back = (jnp.exp(logits - top) / total - chosen).astype(jnp.bfloat16)
     terms = dot_tn(logit_back, queries)
-    part_ref[...] = terms.reshape(count, own, D)
+    part_ref[...] = terms.reshape(count, own, D).astype(jnp.bfloat16)
 
     def piece(peer):
         return part_ref.at[peer]
@@ -383,7 +389,7 @@
     def _(gap):
         landed(piece, got_ref, sem_c, sem_d, gap).wait_recv()
 
-    lead_ref[...] = jnp.sum(got_ref[...], axis=0)
+    lead_ref[...] = jnp.sum(got_ref[...].astype(jnp.float32), axis=0)
 
     @pl.loop(1, count)
     def _(gap):
@@ -410,9 +416,9 @@
             jax.ShapeDtypeStruct((8, 128), jnp.float32),
         ],
         scratch_shapes=[
-            pltpu.VMEM((count, own, D), jnp.float32),
-            pltpu.VMEM((count, own, D), jnp.float32),
-            pltpu.VMEM((count, own, D), jnp.float32),
+            pltpu.VMEM((count, own, D), jnp.bfloat16),
+            pltpu.VMEM((count, own, D), jnp.bfloat16),
+            pltpu.VMEM((count, own, D), jnp.bfloat16),
             pltpu.VMEM((halves, here, 128), jnp.float32),
             pltpu.VMEM((halves, here, D), jnp.float32),
             pltpu.SemaphoreType.DMA((count,)),
@@ -428,7 +434,7 @@
             collective_id=1, has_side_effects=True, vmem_limit_bytes=big_vmem
         ),
         name="contrast",
-    )(leading.astype(jnp.float32), queries, positives.reshape(here, 1))
+    )(leading, queries, positives.reshape(here, 1))
     return query_gradient, lead_back, loss[0, 0]
 
 
@@ -503,6 +509,517 @@
     return lax.psum_scatter(
         whole.reshape(-1, whole.shape[2]), ("tensor", "dp"), scatter_dimension=0, tiled=True
     ).astype(jnp.float32)
+
+
+def grid_place():
+    me = lax.axis_index("dp")
+    return lax.axis_index("tensor"), me // 4, lax.rem(me // 2, 2), lax.rem(me, 2)
+
+
+def at_place(t, z, x, c):
+    return (z * 4 + x * 2 + c, t)
+
+
+def greet_neighbours():
+    t, z, x, c = grid_place()
+    barrier = pltpu.get_barrier_semaphore()
+    others = [at_place(t, lax.rem(z + gap, 4), x, c) for gap in range(1, 4)]
+    others += [at_place(1 - t, z, x, c), at_place(t, z, 1 - x, c), at_place(t, z, x, 1 - c)]
+    for other in others:
+        pl.semaphore_signal(barrier, inc=1, device_id=other, device_id_type=MESH)
+    pl.semaphore_wait(barrier, len(others))
+
+
+class Gather:
+    def __init__(self, own, buffer, sends, lands, local, index):
+        self.own, self.buffer, self.index = own, buffer, index
+        self.sends, self.lands, self.local = sends, lands, local
+        t, z, x, c = self.place = grid_place()
+        even = c == 0
+        self.mid = (jnp.where(even, t, 1 - t), jnp.where(even, 1 - x, x))
+        self.last = (jnp.where(even, 1 - t, t), jnp.where(even, x, 1 - x))
+        self.both = (1 - t, 1 - x)
+
+    def group(self, spot, c):
+        return self.buffer.at[spot[0], :, spot[1], c]
+
+    def slot(self, z):
+        t, _, x, c = self.place
+        return self.buffer.at[t, z, x, c]
+
+    def copy(self, source, target, which, device):
+        return pltpu.make_async_remote_copy(
+            src_ref=source,
+            dst_ref=target,
+            send_sem=self.sends.at[self.index, which],
+            recv_sem=self.lands.at[self.index, which],
+            device_id=device,
+            device_id_type=MESH,
+        )
+
+    def outgoing(self, which):
+        t, z, x, c = self.place
+        if which < 3:
+            device = at_place(t, lax.rem(z + which + 1, 4), x, c)
+            return self.copy(self.own, self.slot(z), which, device)
+        spot = {3: (t, x), 4: (t, x), 5: self.mid, 6: (t, x), 7: self.mid, 8: self.last, 9: self.both}[which]
+        group = self.group(spot, c)
+        if which == 3:
+            device = at_place(self.mid[0], z, self.mid[1], c)
+        elif which < 6:
+            device = at_place(self.last[0], z, self.last[1], c)
+        else:
+            device = at_place(t, z, x, 1 - c)
+        return self.copy(group, group, which, device)
+
+    def arrived(self, which):
+        t, z, x, c = self.place
+        if which < 3:
+            target = self.slot(lax.rem(z + 3 - which, 4))
+        elif which < 6:
+            target = self.group({3: self.mid, 4: self.last, 5: self.both}[which], c)
+        else:
+            spot = {6: (t, x), 7: self.last, 8: self.mid, 9: self.both}[which]
+            target = self.group(spot, 1 - c)
+        self.copy(target, target, which, at_place(t, z, x, 1 - c)).wait_recv()
+
+    def start(self):
+        _, z, _, _ = self.place
+        pltpu.make_async_copy(self.own, self.slot(z), self.local.at[self.index]).start()
+        for which in range(3):
+            self.outgoing(which).start()
+
+    def own_ready(self):
+        _, z, _, _ = self.place
+        pltpu.make_async_copy(self.own, self.slot(z), self.local.at[self.index]).wait()
+        for which in range(3):
+            self.arrived(which)
+        for which in (3, 4, 6):
+            self.outgoing(which).start()
+
+    def mid_ready(self):
+        self.arrived(3)
+        for which in (5, 7):
+            self.outgoing(which).start()
+
+    def last_ready(self):
+        self.arrived(4)
+        self.outgoing(8).start()
+        self.arrived(5)
+        self.outgoing(9).start()
+
+    def finish(self):
+        for which in range(6, 10):
+            self.arrived(which)
+
+    def drain(self):
+        for which in range(10):
+            self.outgoing(which).wait_send()
+
+
+def attend_gather_kernel(
+    piece, spans, mixing_ref, middle_ref, shrink_ref, offsets_ref, x_ref,
+    qkv_ref, ctx_ref, mixing_out, middle_out, shrink_out, offsets_out,
+    w_ref, both_ref, sends, lands, local, swap_send, swap_land, load_sem,
+):
+    step = pl.program_id(0)
+    t, z, x, c = grid_place()
+    mixing, middle, shrink = (
+        Gather(own, out, sends, lands, local, index)
+        for index, (own, out) in enumerate(
+            ((mixing_ref, mixing_out), (middle_ref, middle_out), (shrink_ref, shrink_out))
+        )
+    )
+
+    def swap(which):
+        return pltpu.make_async_remote_copy(
+            src_ref=both_ref.at[which],
+            dst_ref=both_ref.at[which],
+            send_sem=swap_send,
+            recv_sem=swap_land,
+            device_id=at_place(1 - t, z, x, c),
+            device_id_type=MESH,
+        )
+
+    @pl.when(step == 0)
+    def _():
+        both_ref[t] = offsets_ref[...]
+        greet_neighbours()
+        mixing.start()
+        swap(t).start()
+        middle.start()
+        mixing.own_ready()
+        mixing.mid_ready()
+        shrink.start()
+        middle.own_ready()
+        mixing.last_ready()
+        mixing.finish()
+        load = pltpu.make_async_copy(mixing_out, w_ref, load_sem)
+        load.start()
+        swap(1 - t).wait_recv()
+        offsets_out[...] = both_ref[...]
+        load.wait()
+
+    @pl.when(step == 2)
+    def _():
+        middle.mid_ready()
+        shrink.own_ready()
+
+    rows = x_ref.shape[0]
+    width = w_ref.shape[5] // 3
+    visible = visible_keys(spans, step, rows, piece, 1)
+    for half in range(w_ref.shape[0]):
+        weight = w_ref[half].reshape(D, 3 * width)
+        bias = both_ref[half]
+        bias = jnp.concatenate(
+            [bias[:, :width], jnp.zeros((1, width), jnp.float32), bias[:, width : 2 * width]], axis=1
+        )
+        attend_half(half, weight, bias, visible, x_ref, qkv_ref, ctx_ref)
+
+    @pl.when(step == pl.num_programs(0) - 1)
+    def _():
+        shrink.mid_ready()
+        middle.last_ready()
+        shrink.last_ready()
+        middle.finish()
+        shrink.finish()
+        swap(t).wait_send()
+        for each in (mixing, middle, shrink):
+            each.drain()
+
+
+def attend_gather(piece, spans, inputs, mixing_own, middle_own, shrink_own, offsets, chunk):
+    rows = inputs.shape[0]
+    halves = lax.axis_size("tensor")
+    columns = halves * mixing_own.shape[1]
+    anywhere = pl.BlockSpec(memory_space=pl.ANY)
+    bf16 = jnp.bfloat16
+
+    def buffer(own):
+        return jax.ShapeDtypeStruct((halves, 4, 2, 2) + own.shape, bf16)
+
+    owns = (mixing_own, middle_own, shrink_own)
+    both = jax.ShapeDtypeStruct((halves, 1, offsets.shape[0]), jnp.float32)
+    outs = pl.pallas_call(
+        functools.partial(attend_gather_kernel, piece),
+        grid=(rows // chunk,),
+        in_specs=[
+            pl.BlockSpec(memory_space=pltpu.SMEM),
+            anywhere,
+            anywhere,
+            anywhere,
+            full_spec((1, offsets.shape[0])),
+            row_spec(chunk, D),
+        ],
+        out_specs=[
+            row_spec(chunk, columns),
+            row_spec(chunk, D),
+            anywhere,
+            anywhere,
+            anywhere,
+            full_spec(both.shape),
+        ],
+        out_shape=[
+            jax.ShapeDtypeStruct((rows, columns), bf16),
+            jax.ShapeDtypeStruct((rows, D), bf16),
+            *(buffer(own) for own in owns),
+            both,
+        ],
+        scratch_shapes=[
+            pltpu.VMEM(buffer(mixing_own).shape, bf16),
+            pltpu.VMEM(both.shape, jnp.float32),
+            pltpu.SemaphoreType.DMA((3, 10)),
+            pltpu.SemaphoreType.DMA((3, 10)),
+            pltpu.SemaphoreType.DMA((3,)),
+            pltpu.SemaphoreType.DMA,
+            pltpu.SemaphoreType.DMA,
+            pltpu.SemaphoreType.DMA,
+        ],
+        compiler_params=pltpu.CompilerParams(
+            collective_id=3, has_side_effects=True, vmem_limit_bytes=big_vmem
+        ),
+        cost_estimate=pl.CostEstimate(
+            flops=2 * rows * D * columns,
+            bytes_accessed=64 * 1024 * 1024,
+            transcendentals=rows * chunk * 12,
+        ),
+        name="attend_gather",
+    )(spans, *owns, offsets.reshape(1, -1), inputs)
+    qkv, context, *fulls, offsets_both = outs
+    fulls = [full.reshape(halves, -1, full.shape[-1]) for full in fulls]
+    return qkv, context, *fulls, offsets_both.reshape(halves, -1)
+
+
+class Scatter:
+    def __init__(self, whole, acc, sib, one, two, line, out, sends, lands, local, index):
+        self.whole, self.acc, self.sib, self.out, self.index = whole, acc, sib, out, index
+        self.one, self.two, self.line = one, two, line
+        self.sends, self.lands, self.local = sends, lands, local
+        t, z, x, c = self.place = grid_place()
+        even = c == 0
+        self.first = (jnp.where(even, 1 - t, t), jnp.where(even, x, 1 - x))
+        self.second = (jnp.where(even, t, 1 - t), jnp.where(even, 1 - x, x))
+        self.spots = (self.first, (1 - t, 1 - x), self.second, (t, x))
+
+    def copy(self, source, target, which, device):
+        return pltpu.make_async_remote_copy(
+            src_ref=source,
+            dst_ref=target,
+            send_sem=self.sends.at[self.index, which],
+            recv_sem=self.lands.at[self.index, which],
+            device_id=device,
+            device_id_type=MESH,
+        )
+
+    def outgoing(self, which):
+        t, z, x, c = self.place
+        if which < 4:
+            spot = self.spots[{0: 2, 1: 1, 2: 0, 3: 3}[which]]
+            return self.copy(
+                self.whole.at[spot[0], :, spot[1], 1 - c],
+                self.sib.at[spot[0], :, spot[1]],
+                which,
+                at_place(t, z, x, 1 - c),
+            )
+        if which < 6:
+            spot = self.spots[which - 4]
+            device = at_place(self.first[0], z, self.first[1], c)
+            return self.copy(self.acc.at[spot[0], :, spot[1]], self.one.at[which - 4], which, device)
+        if which == 6:
+            spot = self.second
+            device = at_place(spot[0], z, spot[1], c)
+            return self.copy(self.acc.at[spot[0], :, spot[1]], self.two, which, device)
+        there = lax.rem(z + which - 6, 4)
+        return self.copy(
+            self.acc.at[t, there, x], self.line.at[which - 7], which, at_place(t, there, x, c)
+        )
+
+    def arrived(self, which):
+        t, z, x, c = self.place
+        if which < 4:
+            spot = self.spots[which]
+            target = self.sib.at[spot[0], :, spot[1]]
+        elif which < 6:
+            target = self.one.at[which - 4]
+        elif which == 6:
+            target = self.two
+        else:
+            target = self.line.at[which - 7]
+        self.copy(target, target, which, at_place(t, z, x, 1 - c)).wait_recv()
+
+    def load(self, which):
+        c = self.place[3]
+        spot = self.spots[which]
+        return pltpu.make_async_copy(
+            self.whole.at[spot[0], :, spot[1], c],
+            self.acc.at[spot[0], :, spot[1]],
+            self.local.at[self.index, which],
+        )
+
+    def add(self, spot, read):
+        @pl.loop(0, 4)
+        def _(z):
+            low = self.acc[spot[0], z, spot[1]].astype(jnp.float32)
+            low = low + read(z).astype(jnp.float32)
+            self.acc[spot[0], z, spot[1]] = low.astype(jnp.bfloat16)
+
+    def start(self):
+        for which in range(4):
+            self.outgoing(which).start()
+            self.load(which).start()
+
+    def cores_ready(self):
+        for which in range(4):
+            spot = self.spots[which]
+            self.arrived(which)
+            self.load(which).wait()
+            self.add(spot, lambda z: self.sib[spot[0], z, spot[1]])
+            if which < 2:
+                self.outgoing(4 + which).start()
+
+    def first_ready(self):
+        self.arrived(5)
+        self.add(self.second, lambda z: self.one[1, z])
+        self.outgoing(6).start()
+        self.arrived(4)
+        self.add(self.spots[3], lambda z: self.one[0, z])
+
+    def second_ready(self):
+        self.arrived(6)
+        self.add(self.spots[3], lambda z: self.two[z])
+        for which in range(7, 10):
+            self.outgoing(which).start()
+
+    def finish(self):
+        t, z, x, c = self.place
+        total = self.acc[t, z, x].astype(jnp.float32)
+        for which in range(7, 10):
+            self.arrived(which)
+            total = total + self.line[which - 7].astype(jnp.float32)
+        self.out[...] = total
+        return jnp.sum(total * total, axis=0, keepdims=True)
+
+    def drain(self):
+        for which in range(10):
+            self.outgoing(which).wait_send()
+
+
+class Total:
+    def __init__(self, slots, line, sends, lands):
+        self.slots, self.line, self.sends, self.lands = slots, line, sends, lands
+        t, z, x, c = self.place = grid_place()
+        self.partners = (at_place(t, z, x, 1 - c), at_place(t, z, 1 - x, c), at_place(1 - t, z, x, c))
+
+    def pair(self, stage):
+        return pltpu.make_async_remote_copy(
+            src_ref=self.slots.at[2 * stage],
+            dst_ref=self.slots.at[2 * stage + 1],
+            send_sem=self.sends.at[stage],
+            recv_sem=self.lands.at[stage],
+            device_id=self.partners[stage],
+            device_id_type=MESH,
+        )
+
+    def along(self, gap):
+        t, z, x, c = self.place
+        return pltpu.make_async_remote_copy(
+            src_ref=self.line.at[z],
+            dst_ref=self.line.at[z],
+            send_sem=self.sends.at[2 + gap],
+            recv_sem=self.lands.at[2 + gap],
+            device_id=at_place(t, lax.rem(z + gap, 4), x, c),
+            device_id_type=MESH,
+        )
+
+    def landed(self, gap):
+        t, z, x, c = self.place
+        spot = self.line.at[lax.rem(z + 4 - gap, 4)]
+        pltpu.make_async_remote_copy(
+            src_ref=spot,
+            dst_ref=spot,
+            send_sem=self.sends.at[2 + gap],
+            recv_sem=self.lands.at[2 + gap],
+            device_id=self.partners[0],
+            device_id_type=MESH,
+        ).wait_recv()
+
+    def start(self, value):
+        self.slots[0] = value
+        self.pair(0).start()
+
+    def advance(self, stage):
+        self.pair(stage).wait_recv()
+        summed = self.slots[2 * stage] + self.slots[2 * stage + 1]
+        if stage < 2:
+            self.slots[2 * stage + 2] = summed
+            self.pair(stage + 1).start()
+            return
+        z = self.place[1]
+        self.line[z] = summed
+        for gap in range(1, 4):
+            self.along(gap).start()
+
+    def finish(self):
+        for gap in range(1, 4):
+            self.landed(gap)
+        return (self.line[0] + self.line[1]) + (self.line[2] + self.line[3])
+
+    def drain(self):
+        for stage in range(3):
+            self.pair(stage).wait_send()
+        for gap in range(1, 4):
+            self.along(gap).wait_send()
+
+
+def scatter_kernel(count, *refs):
+    wholes, vector_ref = refs[:count], refs[count]
+    outs, total_ref, norm_ref = refs[count + 1 : 2 * count + 1], refs[2 * count + 1], refs[2 * count + 2]
+    rest = refs[2 * count + 3 :]
+    buffers = [rest[5 * index : 5 * index + 5] for index in range(count)]
+    sends, lands, local, vs, vl, vsend, vland, ns, nl, nsend, nland = rest[5 * count :]
+    parts = [
+        Scatter(wholes[i], *buffers[i], outs[i], sends, lands, local, i) for i in range(count)
+    ]
+    vector = Total(vs, vl, vsend, vland)
+    norm = Total(ns, nl, nsend, nland)
+    greet_neighbours()
+    parts[0].start()
+    vector.start(vector_ref[...])
+    parts[1].start()
+    parts[0].cores_ready()
+    vector.advance(0)
+    for part in parts[2:]:
+        part.start()
+    parts[1].cores_ready()
+    parts[0].first_ready()
+    vector.advance(1)
+    parts[2].cores_ready()
+    parts[1].first_ready()
+    parts[0].second_ready()
+    vector.advance(2)
+    parts[3].cores_ready()
+    parts[2].first_ready()
+    parts[1].second_ready()
+    squares = []
+    squares.append(jnp.sum(parts[0].finish()))
+    parts[3].first_ready()
+    parts[2].second_ready()
+    squares.append(jnp.sum(parts[1].finish()))
+    total_ref[...] = vector.finish()
+    parts[3].second_ready()
+    squares.append(jnp.sum(parts[2].finish()))
+    squares.append(jnp.sum(parts[3].finish()))
+    norm.start(jnp.full(norm_ref.shape, sum(squares[1:], squares[0])))
+    for stage in range(3):
+        norm.advance(stage)
+    norm_ref[...] = norm.finish()
+    for each in parts + [vector, norm]:
+        each.drain()
+
+
+def scatter_all(wholes, vector):
+    count = len(wholes)
+    anywhere = pl.BlockSpec(memory_space=pl.ANY)
+    vmem = pl.BlockSpec(memory_space=pltpu.VMEM)
+    halves = lax.axis_size("tensor")
+    bf16, f32 = jnp.bfloat16, jnp.float32
+    rows = wholes[0].shape[1] // lax.axis_size("dp")
+    scratch = []
+    for whole in wholes:
+        columns = whole.shape[2]
+        scratch += [
+            pltpu.VMEM((halves, 4, 2, rows, columns), bf16),
+            pltpu.VMEM((halves, 4, 2, rows, columns), bf16),
+            pltpu.VMEM((2, 4, rows, columns), bf16),
+            pltpu.VMEM((4, rows, columns), bf16),
+            pltpu.VMEM((3, rows, columns), bf16),
+        ]
+    small = (8, 128)
+    scratch += [
+        pltpu.SemaphoreType.DMA((count, 10)),
+        pltpu.SemaphoreType.DMA((count, 10)),
+        pltpu.SemaphoreType.DMA((count, 4)),
+    ]
+    for shape in (vector.shape, small):
+        scratch += [
+            pltpu.VMEM((6,) + shape, f32),
+            pltpu.VMEM((4,) + shape, f32),
+            pltpu.SemaphoreType.DMA((6,)),
+            pltpu.SemaphoreType.DMA((6,)),
+        ]
+    outs = pl.pallas_call(
+        functools.partial(scatter_kernel, count),
+        in_specs=[anywhere] * count + [vmem],
+        out_specs=[vmem] * (count + 2),
+        out_shape=[jax.ShapeDtypeStruct((rows, whole.shape[2]), f32) for whole in wholes]
+        + [jax.ShapeDtypeStruct(vector.shape, f32), jax.ShapeDtypeStruct(small, f32)],
+        scratch_shapes=scratch,
+        compiler_params=pltpu.CompilerParams(
+            collective_id=4, has_side_effects=True, vmem_limit_bytes=big_vmem
+        ),
+        name="scatter_all",
+    )(*(whole.reshape(halves, 4, 2, 2, rows, -1) for whole in wholes), vector)
+    return outs[:count], outs[count], outs[count + 1][0, 0]
 
 
 def row_spec(rows, columns):
@@ -581,25 +1098,10 @@
             jnp.concatenate([low[head:], high[head:]]).reshape(long_tokens.shape),
         )
 
-    mixing_full = gathered(mixing_weight.astype(jnp.bfloat16).reshape(-1, 3 * width))
-    merging_full = gathered(merging_weight.T.astype(jnp.bfloat16))
-    expand_full = gathered(expand_weight.astype(jnp.bfloat16))
-    shrink_full = gathered(shrink_weight.T.astype(jnp.bfloat16))
-    offsets_other = tensor_swap(offsets_weight)
-    offsets_both = jnp.where(
-        place == 0,
-        jnp.stack([offsets_weight, offsets_other]),
-        jnp.stack([offsets_other, offsets_weight]),
-    )
-    mixing_bias = jnp.concatenate(
-        [
-            offsets_both[:, :width],
-            jnp.zeros((halves, width), jnp.float32),
-            offsets_both[:, width : 2 * width],
-        ],
-        axis=1,
-    ).reshape(1, -1)
-    upward_bias = offsets_both[:, 2 * width :].reshape(1, -1)
+    fast = lax.axis_size("dp") == 16 and halves == 2
+    mixing_own = mixing_weight.astype(jnp.bfloat16).reshape(-1, 3 * width)
+    middle_own = jnp.concatenate([merging_weight.T, expand_weight], axis=1).astype(jnp.bfloat16)
+    shrink_own = shrink_weight.T.astype(jnp.bfloat16)
     short_limits = lax.dynamic_slice_in_dim(short_lengths, place * shorts, shorts)
     long_limits = lax.dynamic_slice_in_dim(long_lengths, place * longs, longs)
     spans = jnp.concatenate(
@@ -620,25 +1122,48 @@
     params = pltpu.CompilerParams(vmem_limit_bytes=big_vmem)
     mixing_columns = halves * 3 * width
     scores_flops = 2 * rows * chunk * PAIR * (halves * width // HEAD_DIM)
-    qkv, context = pl.pallas_call(
-        functools.partial(attend_forward_kernel, piece),
-        grid=(chunks,),
-        in_specs=[
-            smem,
-            row_spec(chunk, D),
-            full_spec(mixing_full.shape),
-            full_spec(mixing_bias.shape),
-        ],
-        out_specs=[row_spec(chunk, mixing_columns), row_spec(chunk, D)],
-        out_shape=[shaped(mixing_columns, bf16), shaped(D, bf16)],
-        compiler_params=params,
-        cost_estimate=pl.CostEstimate(
-            flops=2 * rows * D * mixing_columns + 6 * scores_flops,
-            bytes_accessed=16 * 1024 * 1024,
-            transcendentals=rows * chunk * 12,
-        ),
-        name="attend_forward",
-    )(spans, inputs, mixing_full, mixing_bias)
+    if fast:
+        qkv, context, mixing_full, middle_full, shrink_full, offsets_both = attend_gather(
+            piece, spans, inputs, mixing_own, middle_own, shrink_own, offsets_weight, chunk
+        )
+    else:
+        mixing_full, middle_full, shrink_full = (
+            gathered(own) for own in (mixing_own, middle_own, shrink_own)
+        )
+        offsets_other = tensor_swap(offsets_weight)
+        offsets_both = jnp.where(
+            place == 0,
+            jnp.stack([offsets_weight, offsets_other]),
+            jnp.stack([offsets_other, offsets_weight]),
+        )
+        mixing_bias = jnp.concatenate(
+            [
+                offsets_both[:, :width],
+                jnp.zeros((halves, width), jnp.float32),
+                offsets_both[:, width : 2 * width],
+            ],
+            axis=1,
+        ).reshape(1, -1)
+        qkv, context = pl.pallas_call(
+            functools.partial(attend_forward_kernel, piece),
+            grid=(chunks,),
+            in_specs=[
+                smem,
+                row_spec(chunk, D),
+                full_spec(mixing_full.shape),
+                full_spec(mixing_bias.shape),
+            ],
+            out_specs=[row_spec(chunk, mixing_columns), row_spec(chunk, D)],
+            out_shape=[shaped(mixing_columns, bf16), shaped(D, bf16)],
+            compiler_params=params,
+            cost_estimate=pl.CostEstimate(
+                flops=2 * rows * D * mixing_columns + 6 * scores_flops,
+                bytes_accessed=16 * 1024 * 1024,
+                transcendentals=rows * chunk * 12,
+            ),
+            name="attend_forward",
+        )(spans, inputs, mixing_full, mixing_bias)
+    upward_bias = offsets_both[:, 2 * width :].reshape(1, -1)
     output, hidden_low, activated, slope, normed_first, rstd_first, normed_second, rstd_second = (
         pl.pallas_call(
             feed_forward_kernel,
@@ -646,8 +1171,7 @@
             in_specs=[
                 row_spec(chunk, D),
                 row_spec(chunk, D),
-                full_spec(merging_full.shape),
-                full_spec(expand_full.shape),
+                full_spec(middle_full.shape),
                 full_spec(shrink_full.shape),
                 full_spec(scales_weight.shape),
                 full_spec(upward_bias.shape),
@@ -682,16 +1206,15 @@
         )(
             context,
             inputs,
-            merging_full,
-            expand_full,
+            middle_full,
             shrink_full,
             scales_weight,
             upward_bias,
         )
     )
-    output_other = tensor_swap(output)
     leading = jnp.concatenate([output[: shorts * piece : piece], output[chunk::chunk]], axis=0)
     query_gradient, lead_back, loss_part = contrast(leading, queries, positives)
+    output_other = tensor_swap(lax.optimization_barrier((output, lead_back))[0])
     lead_rows = jnp.zeros((chunks, 8, D), f32)
     lead_rows = lead_rows.at[0, :shorts].set(lead_back[:shorts])
     lead_rows = lead_rows.at[1:, 0].set(lead_back[shorts:])
@@ -707,8 +1230,7 @@
                 row_spec(chunk, D),
                 row_spec(chunk, 1),
                 row_spec(chunk, FF),
-                full_spec(merging_full.shape),
-                full_spec(expand_full.shape),
+                full_spec(middle_full.shape),
                 full_spec(shrink_full.shape),
                 full_spec(scales_weight.shape),
             ],
@@ -745,15 +1267,11 @@
             normed_second,
             rstd_second,
             slope,
-            merging_full,
-            expand_full,
+            middle_full,
             shrink_full,
             scales_weight,
         )
     )
-    shrink_sum = scattered(weight_grad(down_low, activated, halves, 512))
-    expand_sum = scattered(weight_grad(hidden_low, upward_low, halves, 512))
-    merging_sum = scattered(weight_grad(first_low, context, halves, 384))
     projected_back, input_back, input_low, bias_grad = pl.pallas_call(
         functools.partial(attend_back_kernel, piece),
         grid=(chunks,),
@@ -785,8 +1303,15 @@
         name="attend_back",
     )(spans, qkv, context_back, first_back, mixing_full)
     input_other = tensor_swap(input_low)
-    mixing_sum = scattered(weight_grad(inputs, projected_back, halves, 384))
-
+    down_low, hidden_low, first_low, inputs, output_other, input_back = lax.optimization_barrier(
+        (down_low, hidden_low, first_low, inputs, output_other, input_back)
+    )
+    shrink_grad = weight_grad(down_low, activated, halves, 512)
+    expand_grad = weight_grad(hidden_low, upward_low, halves, 512)
+    merging_grad = weight_grad(first_low, context, halves, 384)
+    mixing_grad = weight_grad(inputs, projected_back, halves, 384)
+
+    mixing_grad, input_other = lax.optimization_barrier((mixing_grad, input_other))
     short_output, long_output = both_halves(output, output_other)
     short_gradient, long_gradient = both_halves(input_back, input_other.astype(f32))
 
@@ -794,20 +1319,27 @@
     offsets_grad = jnp.concatenate(
         [bias_both[:, 0], bias_both[:, 2], upward_grad[0].reshape(halves, wide)], axis=1
     )
+    lane = lax.broadcasted_iota(jnp.int32, (1, D), 1)
+    grads = (shrink_grad, expand_grad, merging_grad, mixing_grad)
+
+    def stacked(scalars):
+        scalars = jnp.pad(scalars, ((0, 3), (0, 0)))
+        return jnp.concatenate([vector_grad[:6], offsets_grad.reshape(-1, D), scalars], axis=0)
+
+    losses = jnp.where(lane == 1, loss_part, 0.0)
+    if fast:
+        sums, summed, squares_all = scatter_all(grads, stacked(losses))
+    else:
+        sums = [scattered(grad) for grad in grads]
+        squares_part = sum(jnp.sum(each * each) for each in sums)
+        summed = all_total(stacked(jnp.where(lane == 0, squares_part, losses)))
+        squares_all = summed[12, 0]
+    shrink_sum, expand_sum, merging_sum, mixing_sum = sums
     reduced = (mixing_sum.reshape(mixing_weight.shape), merging_sum.T, expand_sum, shrink_sum.T)
-    squares_part = jnp.sum(mixing_sum * mixing_sum) + jnp.sum(merging_sum * merging_sum)
-    squares_part = squares_part + jnp.sum(expand_sum * expand_sum)
-    squares_part = squares_part + jnp.sum(shrink_sum * shrink_sum)
-    lane = lax.broadcasted_iota(jnp.int32, (1, D), 1)
-    scalars = jnp.where(lane == 0, squares_part, jnp.where(lane == 1, loss_part, 0.0))
-    stacked = jnp.concatenate(
-        [vector_grad[:6], offsets_grad.reshape(-1, D), scalars, jnp.zeros((3, D), f32)], axis=0
-    )
-    summed = all_total(stacked)
     scales_sum = summed[:6]
     offsets_all = summed[6:12].reshape(halves, -1)
     offsets_sum = jnp.where(place == 0, offsets_all[0], offsets_all[1])
-    squares_all = summed[12, 0] + jnp.sum(summed[:12] * summed[:12])
+    squares_all = squares_all + jnp.sum(summed[:12] * summed[:12])
     loss_all = summed[12, 1] / halves
     norm_value = jnp.sqrt(squares_all)
     factor = clip_limit / jnp.maximum(norm_value, clip_limit)

time: 837 us -> 424 us (0.51)
  waiting for transfers between devices: 557 us -> 17.3 us
  Pallas kernels: 189 us -> 336 us
  between operations: 22.3 us -> 6.32 us
  local copies, waits for them, and re-layouts: 17.2 us -> 27 us
  other arithmetic: 42.7 us -> 33.5 us
    reduce_scatter x4 -> x0, waiting for transfers between devices: 284 us -> none  [scattered(): lax.psum_scatter(whole.reshape(-1, whole.shape[2]), ('tensor', 'dp'), sca...]
    all_gather x4 -> x0, waiting for transfers between devices: 217 us -> none  [gathered(): lax.all_gather(own, ('tensor', 'dp'), axis=0, tiled=True)]
    pallas_call x2, Pallas kernels: 36.6 us -> 185 us  [the longest x1 97.1 us: scatter_all(): pl.pallas_call(functools.partial(scatter_kernel, count), in_specs=[anywhe...]
    ppermute x3 -> x2, waiting for transfers between devices: 55.6 us -> 17.3 us  [tensor_swap(): return lax.ppermute(value, 'tensor', [(0, 1), (1, 0)])]
  transfers between devices with their start and end apart: 11 -> 2, of which waited for: 10 -> 1; matrix products, arithmetic and copies ran while one was open for 4% -> 3% of each run, Pallas kernels for 11% -> 19%
where the time goes in v2:
time: 424 us; the launch traced here: 422 us
  Pallas kernels  336 us (79%)
  other arithmetic  33.5 us (8%)
  local copies, waits for them, and re-layouts  27 us (6%)
  waiting for transfers between devices  17.3 us (4%)
  between operations  6.32 us (1%)
    pallas_call x1, Pallas kernels, scatter_all(): pl.pallas_call(functools.partial(scatter_kernel, count), in_specs=[anywhe...  97.1 us
    pallas_call x1, Pallas kernels, attend_gather(): pl.pallas_call(functools.partial(attend_gather_kernel, piece), grid=(rows...  87.8 us
    pallas_call x4, Pallas kernels, weight_grad(): pl.pallas_call(weight_grad_kernel, grid=(columns // tile,), in_specs=[pl....  39.7 us
    pallas_call x1, Pallas kernels, shards(): pl.pallas_call(functools.partial(attend_back_kernel, piece), grid=(chunks...  35.5 us
    pallas_call x1, Pallas kernels, shards(): pl.pallas_call(functools.partial(feed_back_kernel, piece), grid=(chunks,)...  27.4 us
    pallas_call x1, Pallas kernels, shards(): pl.pallas_call(feed_forward_kernel, grid=(chunks,), in_specs=[row_spec(ch...  26.3 us
    pallas_call x1, Pallas kernels, contrast(): pl.pallas_call(functools.partial(contrast_kernel, count, own, halves), in...  22.2 us
    ppermute x2, waiting for transfers between devices, tensor_swap(): return lax.ppermute(value, 'tensor', [(0, 1), (1, 0)])  17.3 us
  transfers between devices with their start and end apart: 2, of which 1 were waited for; matrix products, arithmetic and copies ran while one was open for 3% of the time, Pallas kernels for 19%

profile of v2, /device:TPU:0, one launch (start us, length us, event | category | flops | bytes accessed | tf_op | source)
XLA Modules:
  0.0 422.3 jit_solution(11546704997510638161)
XLA Ops:
  2.3 1.3 reshape.248.offsets_ref
  7.1 1.6 convert_bitcast_fusion.shrink_ref
  11.3 1.7 constant_dynamic-slice_fusion
  12.9 1.4 pad_maximum_fusion.2.x_ref.left_ref
  14.3 87.8 %attend_gather.1 = (bf16[1280,2304]{1,0:T(8,128)(2,1)}, bf16[1280,768]{1,0:T(8,128)(2,1)}, bf16[2,4,2,2,48,1152]{5,4,3,2,1,0:T(8,128)(2,1)}, bf16[2,4,2,2,48,192...) custom-call(s32[5,4]{1,0:T(8,128)} %pad_add_fusion.spans, ...), custom_call_target="tpu_custom_call" | custom-call | flops 4529848320 | bytes 67108864 | tf_op jit(solution)/shard_map/attend_gather/pallas_call | solution.py:703
  103.5 26.3 %feed_forward.1 = (bf16[1280,768]{1,0:T(8,128)(2,1)}, bf16[1280,768]{1,0:T(8,128)(2,1)}, bf16[1280,3072]{1,0:T(8,128)(2,1)}, bf16[1280,3072]{1,0:T(8,128)(2,1)},...) custom-call(bf16[1280,768]{1,0:T(8,128)(2,1)} %get-tuple-element.98.ctx_ref.right_ref, ...), custom_call_target="tpu_custom_call" | custom-call | flops 13589544960 | bytes 50331648 | tf_op jit(solution)/shard_map/feed_forward/pallas_call | solution.py:1168
  129.9 1.4 slice.132
  133.6 22.2 %contrast.1 = (f32[16,768]{1,0:T(8,128)}, f32[8,768]{1,0:T(8,128)}, f32[8,128]{1,0:T(8,128)}) custom-call(bf16[8,768]{1,0:T(8,128)(2,1)} %pad_maximum_fusion.8.cls_ref, bf16[16,768]{1,0:T(8,128)(2,1)} %q_ref.1, s32[16,1]{1,0:T(8,128)} %copy.83.pos_ref), custom_call_target="tpu_custom_call" | custom-call | tf_op jit(solution)/shard_map/contrast/pallas_call | solution.py:409
  155.9 1.4 collective-permute-start
  158.1 1.4 pad_maximum_fusion.3.cot_ref
  160.5 27.4 %feed_back.1 = (bf16[1280,768]{1,0:T(8,128)(2,1)}, bf16[1280,3072]{1,0:T(8,128)(2,1)}, bf16[1280,768]{1,0:T(8,128)(2,1)}, f32[1280,768]{1,0:T(8,128)}, bf16[1280...) custom-call(bf16[1280,768]{1,0:T(8,128)(2,1)} %pad_maximum_fusion.3.cot_ref, f32[5,8,768]{2,1,0:T(8,128)} %copy-done.26, ...), custom_call_target="tpu_custom_call" | custom-call | flops 13589544960 | bytes 50331648 | tf_op jit(solution)/shard_map/feed_back/pallas_call | solution.py:1222
  188.0 35.5 %attend_back.1 = (bf16[1280,2304]{1,0:T(8,128)(2,1)}, f32[1280,768]{1,0:T(8,128)}, bf16[1280,768]{1,0:T(8,128)(2,1)}, f32[8,2304]{1,0:T(8,128)}) custom-call(s32[5,4]{1,0:T(8,128)} %pad_add_fusion.spans, bf16[1280,2304]{1,0:T(8,128)(2,1)} %get-tuple-element.113.qkv_ref, bf16[1280,768]{1,0:T(8,128)(2,1)} %get-tuple-element.114.dctx_ref, ...), custom_call_target="tpu_custom_call" | custom-call | flops 19629342720 | bytes 25165824 | tf_op jit(solution)/shard_map/attend_back/pallas_call | solution.py:1275
  224.8 1.2 slice.148
  229.3 1.8 broadcast_select_fusion.1
  231.1 1.3 slice.158
  233.2 1.2 slice.159
  234.4 5.6 %weight_grad.7 = bf16[2,768,384]{2,1,0:T(8,128)(2,1)} custom-call(bf16[1280,768]{1,0:T(8,128)(2,1)} %get-tuple-element.129.left_ref, bf16[1280,768]{1,0:T(8,128)(2,1)} %get-tuple-element.98.ctx_ref.right_ref), custom_call_target="tpu_custom_call" | custom-call | flops 1509949440 | bytes 5111808 | tf_op jit(solution)/shard_map/weight_grad/pallas_call | solution.py:255
  240.0 11.0 %weight_grad.4 = bf16[2,768,1152]{2,1,0:T(8,128)(2,1)} custom-call(bf16[1280,768]{1,0:T(8,128)(2,1)} %pad_maximum_fusion.2.x_ref.left_ref, bf16[1280,2304]{1,0:T(8,128)(2,1)} %get-tuple-element.121.right_ref), custom_call_target="tpu_custom_call" | custom-call | flops 4529848320 | bytes 11403264 | tf_op jit(solution)/shard_map/weight_grad/pallas_call | solution.py:255
  251.0 17.3 %collective-permute-done.1 = bf16[1280,768]{1,0:T(8,128)(2,1)} collective-permute-done((bf16[1280,768]{1,0:T(8,128)(2,1)}, bf16[1280,768]{1,0:T(8,128)(2,1)}, u32[]{:S(2)}, u32[]{:S(2)}) %collective-permute-start.1) | collective-permute-done | bytes 1966112 | tf_op jit(solution)/shard_map/ppermute | solution.py:499
  268.3 11.6 %weight_grad.6 = bf16[2,768,1536]{2,1,0:T(8,128)(2,1)} custom-call(bf16[1280,768]{1,0:T(8,128)(2,1)} %get-tuple-element.127.left_ref, bf16[1280,3072]{1,0:T(8,128)(2,1)} %get-tuple-element.128.right_ref), custom_call_target="tpu_custom_call" | custom-call | flops 6039797760 | bytes 14548992 | tf_op jit(solution)/shard_map/weight_grad/pallas_call | solution.py:255
  279.9 11.6 %weight_grad.5 = bf16[2,768,1536]{2,1,0:T(8,128)(2,1)} custom-call(bf16[1280,768]{1,0:T(8,128)(2,1)} %get-tuple-element.125.left_ref, bf16[1280,3072]{1,0:T(8,128)(2,1)} %get-tuple-element.126.right_ref), custom_call_target="tpu_custom_call" | custom-call | flops 6039797760 | bytes 14548992 | tf_op jit(solution)/shard_map/weight_grad/pallas_call | solution.py:255
  291.4 97.1 %scatter_all.1 = (f32[48,1536]{1,0:T(8,128)}, f32[48,1536]{1,0:T(8,128)}, f32[48,384]{1,0:T(8,128)}, f32[48,1152]{1,0:T(8,128)}, f32[16,768]{1,0:T(8,128)}, /*index=5*/f32[8,128]{1,0:T(8,128)}) custom-call(bf16[2,4,2,2,48,1536]{5,4,3,2,1,0:T(8,128)(2,1)} %bitcast.73, bf16[2,4,2,2,48,1536]{5,4,3,2,1,0:T(8,128)(2,1)} %bitcast.72, ...), custom_call_target="tpu_custom_call" | custom-call | tf_op jit(solution)/shard_map/scatter_all/pallas_call | solution.py:1010
  388.5 1.4 multiply_reduce_fusion
  389.9 1.3 slice.149
  391.2 2.1 convert_select_fusion.1
  395.5 1.9 slice.163
  397.3 1.2 slice.150
  399.9 1.4 select_multiply_fusion
  401.3 1.6 broadcast_multiply_fusion
  403.7 3.9 pad_maximum_fusion.1
  409.2 3.1 pad_maximum_fusion
  412.6 1.2 pad_maximum_fusion.4
  (132 shorter events, 27.6 us)
Async XLA Ops:
  1.3 9.9 %copy-start.12 = (bf16[8,256,768]{2,1,0:T(8,128)(2,1)S(1)}, bf16[8,256,768]{2,1,0:T(8,128)(2,1)}, u32[]{:S(2)}) copy-start(bf16[8,256,768]{2,1,0:T(8,128)(2,1)} %param.40) | copy-start | bytes 9437188
  103.5 28.8 %copy-start.41 = (s32[16]{0:T(128)S(1)}, s32[16]{0:T(128)}, u32[]{:S(2)}) copy-start(s32[16]{0:T(128)} %param.44) | copy-start | bytes 196
  155.9 73.4 %collective-permute-start = (bf16[1280,768]{1,0:T(8,128)(2,1)}, bf16[1280,768]{1,0:T(8,128)(2,1)}, u32[]{:S(2)}, u32[]{:S(2)}) collective-permute-start(bf16[1280,768]{1,0:T(8,128)(2,1)} %get-tuple-element.112), channel_id=1, source_target_pairs={{0,1},{1,0},{2,3},{3,2},{4,5},{5,4},{6,7},{7,6},{8,9},{9,8},{10,11... | collective-permute-start | bytes 5898248 | tf_op jit(solution)/shard_map/ppermute | solution.py:499
  187.9 40.7 %copy-start.37 = (f32[8,768]{1,0:T(8,128)S(1)}, f32[8,768]{1,0:T(8,128)}, u32[]{:S(2)}) copy-start(f32[8,768]{1,0:T(8,128)} %get-tuple-element.131) | copy-start | bytes 73732
  187.9 41.4 %copy-start.6 = (bf16[1280,768]{1,0:T(8,128)(2,1)S(1)}, bf16[1280,768]{1,0:T(8,128)(2,1)}, u32[]{:S(2)}) copy-start(bf16[1280,768]{1,0:T(8,128)(2,1)} %get-tuple-element.112) | copy-start | bytes 5898244
  223.4 44.9 %collective-permute-start.1 = (bf16[1280,768]{1,0:T(8,128)(2,1)}, bf16[1280,768]{1,0:T(8,128)(2,1)}, u32[]{:S(2)}, u32[]{:S(2)}) collective-permute-start(bf16[1280,768]{1,0:T(8,128)(2,1)} %get-tuple-element.122), channel_id=1, source_target_pairs={{0,1},{1,0},{2,3},{3,2},{4,5},{5,4},{6,7},{7,6},{8,9},{9,8},{10,11... | collective-permute-start | bytes 5898248 | tf_op jit(solution)/shard_map/ppermute | solution.py:499
  291.4 99.8 %copy-start.3 = (f32[1280,768]{1,0:T(8,128)S(1)}, f32[1280,768]{1,0:T(8,128)}, u32[]{:S(2)}) copy-start(f32[1280,768]{1,0:T(8,128)} %get-tuple-element.119) | copy-start | bytes 11796484
  403.7 3.9 copy-start.7
  403.7 5.5 %copy-start.2 = (f32[1024,768]{1,0:T(8,128)S(1)}, f32[1024,768]{1,0:T(8,128)}, u32[]{:S(2)}) copy-start(f32[1024,768]{1,0:T(8,128)} %slice.163) | copy-start | bytes 9437188
  409.2 3.1 copy-start.4
  409.2 3.1 copy-start.5
  412.4 2.8 copy-start.13
  412.4 2.8 copy-start.27
  412.4 2.8 copy-start.28
  412.4 2.8 copy-start.29
  412.4 2.8 copy-start.30
  412.5 3.5 copy-start.10
  412.5 3.5 copy-start.11
  412.5 3.5 copy-start.22
  412.5 3.5 copy-start.23
  412.5 3.5 copy-start.24
  412.5 4.5 %copy-start.8 = (f32[48,1536]{1,0:T(8,128)S(1)}, f32[48,1536]{1,0:T(8,128)}, u32[]{:S(2)}) copy-start(f32[48,1536]{1,0:T(8,128)} %param.54) | copy-start | bytes 884740
  412.5 4.5 %copy-start.14 = (f32[48,1536]{1,0:T(8,128)S(1)}, f32[48,1536]{1,0:T(8,128)}, u32[]{:S(2)}) copy-start(f32[48,1536]{1,0:T(8,128)} %param.57) | copy-start | bytes 884740
  412.5 4.5 %copy-start.15 = (f32[48,1536]{1,0:T(8,128)S(1)}, f32[48,1536]{1,0:T(8,128)}, u32[]{:S(2)}) copy-start(f32[48,1536]{1,0:T(8,128)} %param.56) | copy-start | bytes 884740
  412.6 4.5 %copy-start.16 = (f32[48,1536]{1,0:T(8,128)S(1)}, f32[48,1536]{1,0:T(8,128)}, u32[]{:S(2)}) copy-start(f32[48,1536]{1,0:T(8,128)} %param.55) | copy-start | bytes 884740
  412.6 4.5 %copy-start.21 = (f32[48,1536]{1,0:T(8,128)S(1)}, f32[48,1536]{1,0:T(8,128)}, u32[]{:S(2)}) copy-start(f32[48,1536]{1,0:T(8,128)} %get-tuple-element.139) | copy-start | bytes 884740
  413.8 4.4 %copy-start.9 = (f32[1536,48]{0,1:T(8,128)S(1)}, f32[1536,48]{0,1:T(8,128)}, u32[]{:S(2)}) copy-start(f32[1536,48]{0,1:T(8,128)} %param.58) | copy-start | bytes 884740
  413.8 4.4 %copy-start.17 = (f32[1536,48]{0,1:T(8,128)S(1)}, f32[1536,48]{0,1:T(8,128)}, u32[]{:S(2)}) copy-start(f32[1536,48]{0,1:T(8,128)} %param.61) | copy-start | bytes 884740
  413.8 4.4 %copy-start.18 = (f32[1536,48]{0,1:T(8,128)S(1)}, f32[1536,48]{0,1:T(8,128)}, u32[]{:S(2)}) copy-start(f32[1536,48]{0,1:T(8,128)} %param.60) | copy-start | bytes 884740
  413.8 4.4 %copy-start.19 = (f32[1536,48]{0,1:T(8,128)S(1)}, f32[1536,48]{0,1:T(8,128)}, u32[]{:S(2)}) copy-start(f32[1536,48]{0,1:T(8,128)} %param.59) | copy-start | bytes 884740
  413.8 4.4 %copy-start.20 = (f32[48,1536]{1,0:T(8,128)S(1)}, f32[48,1536]{1,0:T(8,128)}, u32[]{:S(2)}) copy-start(f32[48,1536]{1,0:T(8,128)} %get-tuple-element.140) | copy-start | bytes 884740
  416.0 4.1 copy-start.1
  (12 other events, 20.2 us)

commit v3 on v2

--- a/solution.py
+++ b/solution.py
@@ -108,89 +108,162 @@
         attend_half(half, w_ref[half], bias, visible, x_ref, qkv_ref, ctx_ref)
 
 
-def feed_forward_kernel(
-    ctx_ref, x_ref, me_ref, st_ref, scales_ref, bu_ref,
-    out_ref, hb_ref, g_ref, slope_ref, n1_ref, r1_ref, n2_ref, r2_ref,
-):
-    wide = st_ref.shape[2]
-    width = me_ref.shape[2] - wide
+def feed_up(context, inputs, me_ref, scales_ref, bu_ref, outs):
+    hb_ref, g_ref, slope_ref, n1_ref, r1_ref = outs
+    wide = bu_ref.shape[1] // 2
+    width = me_ref.shape[-1] - wide
     attention = scales_ref[4:5, :]
-    for half in range(me_ref.shape[0]):
+
+    def weight(half, columns):
+        place = (half,) + (slice(None),) * (len(me_ref.shape) - 2) + (columns,)
+        return me_ref[place].reshape(D, -1)
+
+    for half in range(2):
         attention = attention + dot_nt(
-            ctx_ref[:, half * width : (half + 1) * width], me_ref[half, :, :width]
-        )
-    normed, rstd = layer_stats(x_ref[...].astype(jnp.float32) + attention)
+            context[:, half * width : (half + 1) * width], weight(half, slice(0, width))
+        )
+    normed, rstd = layer_stats(inputs.astype(jnp.float32) + attention)
     n1_ref[...] = normed
     r1_ref[...] = rstd
     hidden = normed * scales_ref[0:1, :] + scales_ref[1:2, :]
     hidden_low = hidden.astype(jnp.bfloat16)
     hb_ref[...] = hidden_low
-    downward = scales_ref[5:6, :]
-    for half in range(st_ref.shape[0]):
+    activated = []
+    for half in range(2):
         at = half * wide
-        upward = dot_nn(hidden_low, me_ref[half, :, width:]) + bu_ref[:, at : at + wide]
+        upward = dot_nn(hidden_low, weight(half, slice(width, width + wide))) + bu_ref[:, at : at + wide]
         cumulative = 0.5 * (1.0 + lax.erf(upward * inverse_root_two))
         density = jnp.exp(-0.5 * upward * upward) * inverse_root_tau
-        activated = (upward * cumulative).astype(jnp.bfloat16)
-        g_ref[:, at : at + wide] = activated
+        activated.append((upward * cumulative).astype(jnp.bfloat16))
+        g_ref[:, at : at + wide] = activated[half]
         slope_ref[:, at : at + wide] = (cumulative + upward * density).astype(jnp.bfloat16)
-        downward = downward + dot_nt(activated, st_ref[half])
+    return hidden, activated
+
+
+def feed_down(piece, hidden, activated, st_ref, scales_ref, outs):
+    out_ref, n2_ref, r2_ref, lead_ref = outs
+    downward = scales_ref[5:6, :]
+    for half in range(2):
+        wide = st_ref.shape[-1]
+        downward = downward + dot_nt(activated[half], st_ref[half].reshape(D, wide))
     normed, rstd = layer_stats(hidden + downward)
     n2_ref[...] = normed
     r2_ref[...] = rstd
-    out_ref[...] = (normed * scales_ref[2:3, :] + scales_ref[3:4, :]).astype(jnp.bfloat16)
+    result = (normed * scales_ref[2:3, :] + scales_ref[3:4, :]).astype(jnp.bfloat16)
+    out_ref[...] = result
+    for index in range(result.shape[0] // piece):
+        row = result[index * piece : index * piece + 8].astype(jnp.float32)
+        lead_ref[0, index : index + 1, :] = row[:1]
+
+
+def feed_forward_kernel(
+    piece, ctx_ref, x_ref, me_ref, st_ref, scales_ref, bu_ref,
+    hb_ref, g_ref, slope_ref, n1_ref, r1_ref, out_ref, n2_ref, r2_ref, lead_ref,
+):
+    hidden, activated = feed_up(
+        ctx_ref[...], x_ref[...], me_ref, scales_ref, bu_ref, (hb_ref, g_ref, slope_ref, n1_ref, r1_ref)
+    )
+    feed_down(piece, hidden, activated, st_ref, scales_ref, (out_ref, n2_ref, r2_ref, lead_ref))
 
 
 def add_row(ref, index, value):
     ref[index : index + 1, :] += jnp.sum(value, axis=0, keepdims=True)
 
 
+def out_back_kernel(
+    piece, chunks, cot_ref, lead_ref, n2_ref, r2_ref, scales_ref, g_ref, dr2_ref, vec_ref, grad_ref, turned_ref
+):
+    step = pl.program_id(0)
+
+    @pl.when(step == 0)
+    def _():
+        vec_ref[...] = jnp.zeros_like(vec_ref)
+
+    @pl.when(step < chunks)
+    def _():
+        dout = cot_ref[...].astype(jnp.float32)
+        rows = dout.shape[0]
+        row = lax.broadcasted_iota(jnp.int32, dout.shape, 0)
+        for index in range(rows // piece):
+            dout = dout + jnp.where(row == index * piece, lead_ref[0, index : index + 1, :], 0.0)
+        normed = n2_ref[...]
+        add_row(vec_ref, 0, dout * normed)
+        add_row(vec_ref, 1, dout)
+        second = layer_back(dout, normed, r2_ref[...], scales_ref[2:3, :])
+        add_row(vec_ref, 2, second)
+        dr2_ref[...] = second
+        turned_ref[:, pl.ds(pl.multiple_of(step * rows, rows), rows)] = second.astype(jnp.bfloat16).T
+
+    @pl.when(step >= chunks)
+    def _():
+        grad_ref[0] = dot_nn(turned_ref[...], g_ref[...]).astype(jnp.bfloat16)
+
+
+def no_progress(point):
+    pass
+
+
 def feed_back_kernel(
-    piece, cot_ref, lead_ref, n1_ref, r1_ref, n2_ref, r2_ref, slope_ref, me_ref, st_ref, scales_ref,
-    dz_ref, dub_ref, da_ref, dr1_ref, dctx_ref, vec_ref, up_ref,
+    chunks, dr2_ref, n1_ref, r1_ref, slope_ref, hb_ref, ctx_ref, me_ref, st_ref, scales_ref,
+    dr1_ref, dctx_ref, vec_ref, up_ref, merging_ref, expand_ref,
+    dub_ref, turned_h, turned_a, progress=no_progress,
 ):
-    @pl.when(pl.program_id(0) == 0)
+    step = pl.program_id(0)
+    rows = dr2_ref.shape[0]
+    wide = st_ref.shape[2]
+    width = me_ref.shape[2] - wide
+    tiles = ctx_ref.shape[1]
+    tile = expand_ref.shape[2]
+    merging_steps = D // tiles
+
+    @pl.when(step == 0)
     def _():
         vec_ref[...] = jnp.zeros_like(vec_ref)
         up_ref[...] = jnp.zeros_like(up_ref)
 
-    wide = st_ref.shape[2]
-    width = me_ref.shape[2] - wide
-    dout = cot_ref[...].astype(jnp.float32)
-    row = lax.broadcasted_iota(jnp.int32, dout.shape, 0)
-    for index in range(dout.shape[0] // piece):
-        dout = dout + jnp.where(row == index * piece, lead_ref[0, index : index + 1, :], 0.0)
-    normed = n2_ref[...]
-    add_row(vec_ref, 2, dout * normed)
-    add_row(vec_ref, 3, dout)
-    second = layer_back(dout, normed, r2_ref[...], scales_ref[2:3, :])
-    add_row(vec_ref, 5, second)
-    low = second.astype(jnp.bfloat16)
-    dz_ref[...] = low
-    hidden_back = second
-    for half in range(st_ref.shape[0]):
-        at = half * wide
-        upward = dot_nn(low, st_ref[half]) * slope_ref[:, at : at + wide].astype(jnp.float32)
-        up_ref[0:1, at : at + wide] += jnp.sum(upward, axis=0, keepdims=True)
-        upward_low = upward.astype(jnp.bfloat16)
-        dub_ref[:, at : at + wide] = upward_low
-        hidden_back = hidden_back + dot_nt(upward_low, me_ref[half, :, width:])
-    normed = n1_ref[...]
-    add_row(vec_ref, 0, hidden_back * normed)
-    add_row(vec_ref, 1, hidden_back)
-    first = layer_back(hidden_back, normed, r1_ref[...], scales_ref[0:1, :])
-    add_row(vec_ref, 4, first)
-    dr1_ref[...] = first
-    low = first.astype(jnp.bfloat16)
-    da_ref[...] = low
-    for half in range(me_ref.shape[0]):
-        dctx_ref[:, half * width : (half + 1) * width] = dot_nn(low, me_ref[half, :, :width]).astype(
-            jnp.bfloat16
-        )
+    progress(0)
+
+    @pl.when(step < chunks)
+    def _():
+        place = pl.ds(pl.multiple_of(step * rows, rows), rows)
+        hidden_back = dr2_ref[...]
+        low = hidden_back.astype(jnp.bfloat16)
+        turned_h[:, place] = hb_ref[...].T
+        for half in range(st_ref.shape[0]):
+            at = half * wide
+            upward = dot_nn(low, st_ref[half]) * slope_ref[:, at : at + wide].astype(jnp.float32)
+            up_ref[0:1, at : at + wide] += jnp.sum(upward, axis=0, keepdims=True)
+            upward_low = upward.astype(jnp.bfloat16)
+            dub_ref[place, at : at + wide] = upward_low
+            hidden_back = hidden_back + dot_nt(upward_low, me_ref[half, :, width:])
+            progress(1 + half)
+        normed = n1_ref[...]
+        add_row(vec_ref, 0, hidden_back * normed)
+        add_row(vec_ref, 1, hidden_back)
+        first = layer_back(hidden_back, normed, r1_ref[...], scales_ref[0:1, :])
+        add_row(vec_ref, 2, first)
+        dr1_ref[...] = first
+        low = first.astype(jnp.bfloat16)
+        turned_a[:, place] = low.T
+        for half in range(me_ref.shape[0]):
+            dctx_ref[:, half * width : (half + 1) * width] = dot_nn(
+                low, me_ref[half, :, :width]
+            ).astype(jnp.bfloat16)
+
+    @pl.when(jnp.logical_and(step >= chunks, step < chunks + merging_steps))
+    def _():
+        merging_ref[0] = dot_nn(turned_a[...], ctx_ref[...]).astype(jnp.bfloat16)
+
+    @pl.when(step >= chunks + merging_steps)
+    def _():
+        start = (step - chunks - merging_steps) * tile
+        right = dub_ref[:, pl.ds(pl.multiple_of(start, tile), tile)]
+        expand_ref[0] = dot_nn(turned_h[...], right).astype(jnp.bfloat16)
 
 
 def attend_back_kernel(
-    piece, spans, qkv_ref, dctx_ref, dr1_ref, w_ref, dproj_ref, dx_ref, low_ref, bias_ref
+    piece, spans, qkv_ref, dctx_ref, dr1_ref, w_ref, dproj_ref, dx_ref, bias_ref, low_ref,
+    progress=no_progress,
 ):
     step = pl.program_id(0)
 
@@ -201,6 +274,7 @@
     rows = qkv_ref.shape[0]
     width = w_ref.shape[2] // 3
     visible = visible_keys(spans, step, rows, piece, 0)
+    point = 0
     total = dr1_ref[...]
     for half in range(w_ref.shape[0]):
         base = half * 3 * width
@@ -235,9 +309,11 @@
                 if part != 1:
                     bias_ref[0:1, spot : spot + PAIR] += jnp.sum(value, axis=0, keepdims=True)
                 dproj_ref[:, spot : spot + PAIR] = value.astype(jnp.bfloat16)
+            point += 1
+            progress(point)
         total = total + dot_nt(dproj_ref[:, base : base + 3 * width], w_ref[half])
     dx_ref[...] = total
-    low_ref[...] = total.astype(jnp.bfloat16)
+    low_ref[step if low_ref.shape[0] > 1 else 0] = total.astype(jnp.bfloat16)
 
 
 def weight_grad_kernel(left_ref, right_ref, out_ref, turned_ref):
@@ -274,12 +350,15 @@
 
 def contrast_kernel(
     count, own, halves, cls_ref, q_ref, pos_ref, qg_ref, lead_ref, loss_ref,
-    all_ref, part_ref, got_ref, stat_ref, term_ref,
+    mine_ref, all_ref, part_ref, got_ref, stat_ref, term_ref,
     sem_a, sem_b, sem_c, sem_d, sem_e, sem_f, sem_g, sem_h,
 ):
     me = lax.axis_index("dp")
     half = lax.axis_index("tensor")
     other = 1 - half
+    kind = own // 2
+    firsts = [cls_ref[0, :kind, :]] + [cls_ref[1 + index, :1, :] for index in range(kind)]
+    mine_ref[...] = jnp.concatenate(firsts, axis=0).astype(jnp.bfloat16)
     barrier = pltpu.get_barrier_semaphore()
 
     @pl.loop(1, count)
@@ -314,13 +393,13 @@
         )
 
     def whole(peer):
-        return cls_ref
+        return mine_ref
 
     @pl.loop(1, count)
     def _(gap):
         push(whole, all_ref, sem_a, sem_b, gap).start()
 
-    all_ref[me] = cls_ref[...]
+    all_ref[me] = mine_ref[...]
 
     @pl.loop(1, count)
     def _(gap):
@@ -331,10 +410,13 @@
     logits = dot_nt(queries, passages)
     column = lax.broadcasted_iota(jnp.int32, logits.shape, 1)
     near = column % own
-    kind = own // 2
     index = (column // own) * (own * halves) + (near // kind) * (kind * halves)
     index = index + half * kind + near % kind
-    chosen = jnp.where(index == pos_ref[...], 1.0, 0.0)
+    query = lax.broadcasted_iota(jnp.int32, logits.shape, 0)
+    positive = jnp.zeros(logits.shape, jnp.int32)
+    for each in range(logits.shape[0]):
+        positive = jnp.where(query == each, pos_ref[each], positive)
+    chosen = jnp.where(index == positive, 1.0, 0.0)
     highest = jnp.max(logits, axis=1, keepdims=True)
     summed = jnp.sum(jnp.exp(logits - highest), axis=1, keepdims=True)
     picked = jnp.sum(logits * chosen, axis=1, keepdims=True)
@@ -389,7 +471,11 @@
     def _(gap):
         landed(piece, got_ref, sem_c, sem_d, gap).wait_recv()
 
-    lead_ref[...] = jnp.sum(got_ref[...].astype(jnp.float32), axis=0)
+    lead = jnp.sum(got_ref[...].astype(jnp.float32), axis=0)
+    lead_ref[...] = jnp.zeros_like(lead_ref)
+    lead_ref[0, :kind, :] = lead[:kind]
+    for index in range(kind):
+        lead_ref[1 + index, :1, :] = lead[kind + index : kind + index + 1]
 
     @pl.loop(1, count)
     def _(gap):
@@ -403,19 +489,20 @@
 def contrast(leading, queries, positives):
     count = lax.axis_size("dp")
     halves = lax.axis_size("tensor")
-    own = leading.shape[0]
+    own = 2 * (leading.shape[0] - 1)
     here = queries.shape[0]
     whole = pl.BlockSpec(memory_space=pltpu.VMEM)
     query_gradient, lead_back, loss = pl.pallas_call(
         functools.partial(contrast_kernel, count, own, halves),
-        in_specs=[whole] * 3,
+        in_specs=[whole] * 2 + [pl.BlockSpec(memory_space=pltpu.SMEM)],
         out_specs=[whole] * 3,
         out_shape=[
             jax.ShapeDtypeStruct((here, D), jnp.float32),
-            jax.ShapeDtypeStruct((own, D), jnp.float32),
+            jax.ShapeDtypeStruct(leading.shape, jnp.float32),
             jax.ShapeDtypeStruct((8, 128), jnp.float32),
         ],
         scratch_shapes=[
+            pltpu.VMEM((own, D), jnp.bfloat16),
             pltpu.VMEM((count, own, D), jnp.bfloat16),
             pltpu.VMEM((count, own, D), jnp.bfloat16),
             pltpu.VMEM((count, own, D), jnp.bfloat16),
@@ -434,8 +521,8 @@
             collective_id=1, has_side_effects=True, vmem_limit_bytes=big_vmem
         ),
         name="contrast",
-    )(leading, queries, positives.reshape(here, 1))
-    return query_gradient, lead_back, loss[0, 0]
+    )(leading, queries, positives)
+    return query_gradient, lead_back, loss
 
 
 def total_kernel(bits, value_ref, out_ref, slots, send_sem, recv_sem):
@@ -520,17 +607,22 @@
     return (z * 4 + x * 2 + c, t)
 
 
-def greet_neighbours():
+def greet_neighbours(cube=False):
     t, z, x, c = grid_place()
     barrier = pltpu.get_barrier_semaphore()
     others = [at_place(t, lax.rem(z + gap, 4), x, c) for gap in range(1, 4)]
     others += [at_place(1 - t, z, x, c), at_place(t, z, 1 - x, c), at_place(t, z, x, 1 - c)]
+    if cube:
+        others += [at_place(1 - t, z, 1 - x, c), at_place(1 - t, z, x, 1 - c)]
+        others += [at_place(t, z, 1 - x, 1 - c), at_place(1 - t, z, 1 - x, 1 - c)]
     for other in others:
         pl.semaphore_signal(barrier, inc=1, device_id=other, device_id_type=MESH)
     pl.semaphore_wait(barrier, len(others))
 
 
 class Gather:
+    count = 19
+
     def __init__(self, own, buffer, sends, lands, local, index):
         self.own, self.buffer, self.index = own, buffer, index
         self.sends, self.lands, self.local = sends, lands, local
@@ -543,9 +635,9 @@
     def group(self, spot, c):
         return self.buffer.at[spot[0], :, spot[1], c]
 
-    def slot(self, z):
-        t, _, x, c = self.place
-        return self.buffer.at[t, z, x, c]
+    def slot(self, spot, gap):
+        _, z, _, c = self.place
+        return self.buffer.at[spot[0], lax.rem(z + 4 - gap, 4), spot[1], c]
 
     def copy(self, source, target, which, device):
         return pltpu.make_async_remote_copy(
@@ -559,75 +651,100 @@
 
     def outgoing(self, which):
         t, z, x, c = self.place
+        here = (t, x)
+        middle = at_place(self.mid[0], z, self.mid[1], c)
+        last = at_place(self.last[0], z, self.last[1], c)
         if which < 3:
             device = at_place(t, lax.rem(z + which + 1, 4), x, c)
-            return self.copy(self.own, self.slot(z), which, device)
-        spot = {3: (t, x), 4: (t, x), 5: self.mid, 6: (t, x), 7: self.mid, 8: self.last, 9: self.both}[which]
-        group = self.group(spot, c)
-        if which == 3:
-            device = at_place(self.mid[0], z, self.mid[1], c)
-        elif which < 6:
-            device = at_place(self.last[0], z, self.last[1], c)
-        else:
-            device = at_place(t, z, x, 1 - c)
-        return self.copy(group, group, which, device)
+            return self.copy(self.own, self.slot(here, 0), which, device)
+        if which < 5:
+            return self.copy(self.own, self.slot(here, 0), which, (middle, last)[which - 3])
+        if which < 11:
+            slot = self.slot(here, (which - 5) % 3 + 1)
+            return self.copy(slot, slot, which, middle if which < 8 else last)
+        if which < 15:
+            slot = self.slot(self.mid, which - 11)
+            return self.copy(slot, slot, which, last)
+        group = self.group((here, self.mid, self.last, self.both)[which - 15], c)
+        return self.copy(group, group, which, at_place(t, z, x, 1 - c))
 
     def arrived(self, which):
         t, z, x, c = self.place
         if which < 3:
-            target = self.slot(lax.rem(z + 3 - which, 4))
-        elif which < 6:
-            target = self.group({3: self.mid, 4: self.last, 5: self.both}[which], c)
+            target = self.slot((t, x), which + 1)
+        elif which < 5:
+            target = self.slot((self.mid, self.last)[which - 3], 0)
+        elif which < 11:
+            target = self.slot(self.mid if which < 8 else self.last, (which - 5) % 3 + 1)
+        elif which < 15:
+            target = self.slot(self.both, which - 11)
         else:
-            spot = {6: (t, x), 7: self.last, 8: self.mid, 9: self.both}[which]
-            target = self.group(spot, 1 - c)
+            target = self.group(((t, x), self.last, self.mid, self.both)[which - 15], 1 - c)
         self.copy(target, target, which, at_place(t, z, x, 1 - c)).wait_recv()
 
+    def keep(self):
+        t, z, x, c = self.place
+        return pltpu.make_async_copy(self.own, self.slot((t, x), 0), self.local.at[self.index])
+
     def start(self):
-        _, z, _, _ = self.place
-        pltpu.make_async_copy(self.own, self.slot(z), self.local.at[self.index]).start()
-        for which in range(3):
+        self.keep().start()
+        for which in (0, 2, 1, 3, 4):
             self.outgoing(which).start()
 
-    def own_ready(self):
-        _, z, _, _ = self.place
-        pltpu.make_async_copy(self.own, self.slot(z), self.local.at[self.index]).wait()
-        for which in range(3):
+    def line_part(self, gap):
+        self.arrived(gap)
+        self.outgoing(5 + gap).start()
+        self.outgoing(8 + gap).start()
+
+    def line_kept(self):
+        self.keep().wait()
+        self.outgoing(15).start()
+
+    def line_ready(self):
+        for gap in (0, 2, 1):
+            self.line_part(gap)
+        self.line_kept()
+
+    def middle_ready(self):
+        self.arrived(3)
+        self.outgoing(11).start()
+        for gap in (0, 2, 1):
+            self.arrived(5 + gap)
+            self.outgoing(12 + gap).start()
+        self.outgoing(16).start()
+
+    def last_ready(self):
+        for which in (4, 8, 10, 9):
             self.arrived(which)
-        for which in (3, 4, 6):
-            self.outgoing(which).start()
-
-    def mid_ready(self):
-        self.arrived(3)
-        for which in (5, 7):
-            self.outgoing(which).start()
-
-    def last_ready(self):
-        self.arrived(4)
-        self.outgoing(8).start()
-        self.arrived(5)
-        self.outgoing(9).start()
+        self.outgoing(17).start()
+
+    def both_ready(self):
+        for which in range(11, 15):
+            self.arrived(which)
+        self.outgoing(18).start()
 
     def finish(self):
-        for which in range(6, 10):
+        for which in range(15, 19):
             self.arrived(which)
 
     def drain(self):
-        for which in range(10):
+        for which in range(self.count):
             self.outgoing(which).wait_send()
 
 
-def attend_gather_kernel(
-    piece, spans, mixing_ref, middle_ref, shrink_ref, offsets_ref, x_ref,
-    qkv_ref, ctx_ref, mixing_out, middle_out, shrink_out, offsets_out,
-    w_ref, both_ref, sends, lands, local, swap_send, swap_land, load_sem,
+def forward_gather_kernel(
+    piece, chunks, spans, mixing_ref, middle_ref, shrink_ref, offsets_ref, scales_ref, x_ref,
+    qkv_ref, ctx_ref, hb_ref, g_ref, slope_ref, n1_ref, r1_ref, out_ref, n2_ref, r2_ref, lead_ref,
+    mixing_out, middle_out, shrink_out,
+    w_ref, me_ref, st_ref, both_ref, flat_ref, up_ref, ctx_all, g_all, hidden_all,
+    sends, lands, local, swap_send, swap_land, stores,
 ):
     step = pl.program_id(0)
     t, z, x, c = grid_place()
     mixing, middle, shrink = (
-        Gather(own, out, sends, lands, local, index)
-        for index, (own, out) in enumerate(
-            ((mixing_ref, mixing_out), (middle_ref, middle_out), (shrink_ref, shrink_out))
+        Gather(own, full, sends, lands, local, index)
+        for index, (own, full) in enumerate(
+            ((mixing_ref, w_ref), (middle_ref, me_ref), (shrink_ref, st_ref))
         )
     )
 
@@ -641,6 +758,13 @@
             device_id_type=MESH,
         )
 
+    def store(index):
+        target = (mixing_out, middle_out, shrink_out)[index]
+        return pltpu.make_async_copy((w_ref, me_ref, st_ref)[index], target, stores.at[index])
+
+    rows = x_ref.shape[0]
+    width = w_ref.shape[5] // 3
+
     @pl.when(step == 0)
     def _():
         both_ref[t] = offsets_ref[...]
@@ -648,106 +772,152 @@
         mixing.start()
         swap(t).start()
         middle.start()
-        mixing.own_ready()
-        mixing.mid_ready()
         shrink.start()
-        middle.own_ready()
+        mixing.line_ready()
+        mixing.middle_ready()
         mixing.last_ready()
+        middle.line_part(0)
+        mixing.both_ready()
         mixing.finish()
-        load = pltpu.make_async_copy(mixing_out, w_ref, load_sem)
-        load.start()
+        store(0).start()
+        middle.line_part(2)
+        middle.line_part(1)
+        middle.line_kept()
         swap(1 - t).wait_recv()
-        offsets_out[...] = both_ref[...]
-        load.wait()
+        for half in range(2):
+            flat_ref[half] = jnp.concatenate(
+                [both_ref[half, index : index + 1, :] for index in range(both_ref.shape[1])], axis=1
+            )
+            wide = up_ref.shape[1] // 2
+            up_ref[:, half * wide : (half + 1) * wide] = flat_ref[half][:, 2 * width :]
 
     @pl.when(step == 2)
     def _():
-        middle.mid_ready()
-        shrink.own_ready()
-
-    rows = x_ref.shape[0]
-    width = w_ref.shape[5] // 3
-    visible = visible_keys(spans, step, rows, piece, 1)
-    for half in range(w_ref.shape[0]):
-        weight = w_ref[half].reshape(D, 3 * width)
-        bias = both_ref[half]
-        bias = jnp.concatenate(
-            [bias[:, :width], jnp.zeros((1, width), jnp.float32), bias[:, width : 2 * width]], axis=1
-        )
-        attend_half(half, weight, bias, visible, x_ref, qkv_ref, ctx_ref)
+        middle.middle_ready()
+
+    @pl.when(step == chunks - 1)
+    def _():
+        shrink.line_ready()
+        middle.last_ready()
+
+    @pl.when(step == chunks)
+    def _():
+        middle.both_ready()
+        middle.finish()
+        store(1).start()
+
+    @pl.when(step == chunks + 1)
+    def _():
+        shrink.middle_ready()
+
+    @pl.when(step == 2 * chunks - 2)
+    def _():
+        shrink.last_ready()
+
+    @pl.when(step == 2 * chunks)
+    def _():
+        shrink.both_ready()
+        shrink.finish()
+        store(2).start()
+
+    def here(first):
+        return pl.ds(pl.multiple_of((step - first) * rows, rows), rows)
+
+    @pl.when(step < chunks)
+    def _():
+        visible = visible_keys(spans, step, rows, piece, 1)
+        for half in range(2):
+            weight = w_ref[half].reshape(D, 3 * width)
+            bias = flat_ref[half]
+            bias = jnp.concatenate(
+                [bias[:, :width], jnp.zeros((1, width), jnp.float32), bias[:, width : 2 * width]],
+                axis=1,
+            )
+            attend_half(half, weight, bias, visible, x_ref, qkv_ref, ctx_ref)
+        ctx_all[here(0), :] = ctx_ref[...]
+
+    @pl.when(jnp.logical_and(step >= chunks, step < 2 * chunks))
+    def _():
+        outs = (hb_ref, g_ref, slope_ref, n1_ref, r1_ref)
+        place = here(chunks)
+        hidden, activated = feed_up(ctx_all[place, :], x_ref[...], me_ref, scales_ref, up_ref, outs)
+        hidden_all[place, :] = hidden
+        for half in range(2):
+            wide = st_ref.shape[5]
+            g_all[place, half * wide : (half + 1) * wide] = activated[half]
+
+    @pl.when(step >= 2 * chunks)
+    def _():
+        place = here(2 * chunks)
+        wide = st_ref.shape[5]
+        activated = [g_all[place, half * wide : (half + 1) * wide] for half in range(2)]
+        outs = (out_ref, n2_ref, r2_ref, lead_ref)
+        feed_down(piece, hidden_all[place, :], activated, st_ref, scales_ref, outs)
 
     @pl.when(step == pl.num_programs(0) - 1)
     def _():
-        shrink.mid_ready()
-        middle.last_ready()
-        shrink.last_ready()
-        middle.finish()
-        shrink.finish()
         swap(t).wait_send()
         for each in (mixing, middle, shrink):
             each.drain()
-
-
-def attend_gather(piece, spans, inputs, mixing_own, middle_own, shrink_own, offsets, chunk):
+        for index in range(3):
+            store(index).wait()
+
+
+def forward_gather(piece, spans, inputs, owns, offsets, scales, chunk):
     rows = inputs.shape[0]
+    chunks = rows // chunk
     halves = lax.axis_size("tensor")
-    columns = halves * mixing_own.shape[1]
+    columns = halves * owns[0].shape[1]
     anywhere = pl.BlockSpec(memory_space=pl.ANY)
-    bf16 = jnp.bfloat16
+    bf16, f32 = jnp.bfloat16, jnp.float32
 
     def buffer(own):
-        return jax.ShapeDtypeStruct((halves, 4, 2, 2) + own.shape, bf16)
-
-    owns = (mixing_own, middle_own, shrink_own)
-    both = jax.ShapeDtypeStruct((halves, 1, offsets.shape[0]), jnp.float32)
+        return (halves, 4, 2, 2) + own.shape
+
+    def spec(width, first):
+        return pl.BlockSpec((chunk, width), lambda i: (jnp.clip(i - first * chunks, 0, chunks - 1), 0))
+
+    shapes = [(columns, bf16, 0), (D, bf16, 0)]
+    shapes += [(D, bf16, 1), (FF, bf16, 1), (FF, bf16, 1), (D, f32, 1), (1, f32, 1)]
+    shapes += [(D, bf16, 2), (D, f32, 2), (1, f32, 2)]
     outs = pl.pallas_call(
-        functools.partial(attend_gather_kernel, piece),
-        grid=(rows // chunk,),
+        functools.partial(forward_gather_kernel, piece, chunks),
+        grid=(3 * chunks,),
         in_specs=[
             pl.BlockSpec(memory_space=pltpu.SMEM),
-            anywhere,
-            anywhere,
-            anywhere,
-            full_spec((1, offsets.shape[0])),
-            row_spec(chunk, D),
+            *(full_spec(own.shape) for own in owns),
+            full_spec((offsets.shape[0] // 128, 128)),
+            full_spec(scales.shape),
+            pl.BlockSpec((chunk, D), lambda i: (jnp.minimum(i, 2 * chunks - 1) % chunks, 0)),
         ],
-        out_specs=[
-            row_spec(chunk, columns),
-            row_spec(chunk, D),
-            anywhere,
-            anywhere,
-            anywhere,
-            full_spec(both.shape),
-        ],
-        out_shape=[
-            jax.ShapeDtypeStruct((rows, columns), bf16),
-            jax.ShapeDtypeStruct((rows, D), bf16),
-            *(buffer(own) for own in owns),
-            both,
-        ],
-        scratch_shapes=[
-            pltpu.VMEM(buffer(mixing_own).shape, bf16),
-            pltpu.VMEM(both.shape, jnp.float32),
-            pltpu.SemaphoreType.DMA((3, 10)),
-            pltpu.SemaphoreType.DMA((3, 10)),
+        out_specs=[spec(width, first) for width, _, first in shapes]
+        + [pl.BlockSpec((1, 8, D), lambda i: (jnp.maximum(i - 2 * chunks, 0), 0, 0))]
+        + [anywhere] * 3,
+        out_shape=[jax.ShapeDtypeStruct((rows, width), dtype) for width, dtype, _ in shapes]
+        + [jax.ShapeDtypeStruct((chunks, 8, D), f32)]
+        + [jax.ShapeDtypeStruct(buffer(own), bf16) for own in owns],
+        scratch_shapes=[pltpu.VMEM(buffer(own), bf16) for own in owns]
+        + [
+            pltpu.VMEM((halves, offsets.shape[0] // 128, 128), f32),
+            pltpu.VMEM((halves, 1, offsets.shape[0]), f32),
+            pltpu.VMEM((1, FF), f32),
+            pltpu.VMEM((rows, D), bf16),
+            pltpu.VMEM((rows, FF), bf16),
+            pltpu.VMEM((rows, D), f32),
+            pltpu.SemaphoreType.DMA((3, Gather.count)),
+            pltpu.SemaphoreType.DMA((3, Gather.count)),
             pltpu.SemaphoreType.DMA((3,)),
             pltpu.SemaphoreType.DMA,
             pltpu.SemaphoreType.DMA,
-            pltpu.SemaphoreType.DMA,
+            pltpu.SemaphoreType.DMA((3,)),
         ],
         compiler_params=pltpu.CompilerParams(
             collective_id=3, has_side_effects=True, vmem_limit_bytes=big_vmem
         ),
-        cost_estimate=pl.CostEstimate(
-            flops=2 * rows * D * columns,
-            bytes_accessed=64 * 1024 * 1024,
-            transcendentals=rows * chunk * 12,
-        ),
-        name="attend_gather",
-    )(spans, *owns, offsets.reshape(1, -1), inputs)
-    qkv, context, *fulls, offsets_both = outs
-    fulls = [full.reshape(halves, -1, full.shape[-1]) for full in fulls]
-    return qkv, context, *fulls, offsets_both.reshape(halves, -1)
+        name="forward_gather",
+    )(spans, *owns, offsets.reshape(-1, 128), scales, inputs)
+    fulls = [full.reshape(halves, -1, full.shape[-1]) for full in outs[-3:]]
+    return outs[:2], outs[2:-3], fulls
 
 
 class Scatter:
@@ -759,6 +929,7 @@
         even = c == 0
         self.first = (jnp.where(even, 1 - t, t), jnp.where(even, x, 1 - x))
         self.second = (jnp.where(even, t, 1 - t), jnp.where(even, 1 - x, x))
+        self.order = (2, 1, 0, 3)
         self.spots = (self.first, (1 - t, 1 - x), self.second, (t, x))
 
     def copy(self, source, target, which, device):
@@ -774,7 +945,7 @@
     def outgoing(self, which):
         t, z, x, c = self.place
         if which < 4:
-            spot = self.spots[{0: 2, 1: 1, 2: 0, 3: 3}[which]]
+            spot = self.spots[self.order[which]]
             return self.copy(
                 self.whole.at[spot[0], :, spot[1], 1 - c],
                 self.sib.at[spot[0], :, spot[1]],
@@ -864,6 +1035,58 @@
             self.outgoing(which).wait_send()
 
 
+class LateScatter(Scatter):
+    def __init__(self, *args):
+        super().__init__(*args)
+        _, _, x, _ = self.place
+        self.order = (0, 1, 2, 3)
+        self.spots = ((0, 1 - x), (1, 1 - x), (0, x), (1, x))
+
+    def outgoing(self, which):
+        t, z, x, c = self.place
+        if which < 4:
+            return super().outgoing(which)
+        if which < 6:
+            side = which - 4
+            return self.copy(
+                self.acc.at[side, :, 1 - x], self.one.at[side], which, at_place(t, z, 1 - x, c)
+            )
+        if which == 6:
+            return self.copy(self.acc.at[1 - t, z, x], self.two, which, at_place(1 - t, z, x, c))
+        there = lax.rem(z + which - 6, 4)
+        return self.copy(
+            self.acc.at[:, there, x], self.line.at[which - 7], which, at_place(t, there, x, c)
+        )
+
+    def first_ready(self):
+        for side in range(2):
+            self.arrived(4 + side)
+            self.add((side, self.place[2]), lambda z: self.one[side, z])
+        for which in range(7, 10):
+            self.outgoing(which).start()
+
+    def second_ready(self):
+        t, z, x, _ = self.place
+        for which in range(7, 10):
+            self.arrived(which)
+
+        def total(side):
+            value = self.acc[side, z, x].astype(jnp.float32)
+            for which in range(3):
+                value = value + self.line[which, side].astype(jnp.float32)
+            return value
+
+        self.acc[1 - t, z, x] = total(1 - t).astype(jnp.bfloat16)
+        self.outgoing(6).start()
+        self.out[...] = total(t)
+
+    def finish(self):
+        self.arrived(6)
+        total = self.out[...] + self.two[...].astype(jnp.float32)
+        self.out[...] = total
+        return jnp.sum(total * total, axis=0, keepdims=True)
+
+
 class Total:
     def __init__(self, slots, line, sends, lands):
         self.slots, self.line, self.sends, self.lands = slots, line, sends, lands
@@ -931,95 +1154,448 @@
             self.along(gap).wait_send()
 
 
-def scatter_kernel(count, *refs):
-    wholes, vector_ref = refs[:count], refs[count]
-    outs, total_ref, norm_ref = refs[count + 1 : 2 * count + 1], refs[2 * count + 1], refs[2 * count + 2]
-    rest = refs[2 * count + 3 :]
-    buffers = [rest[5 * index : 5 * index + 5] for index in range(count)]
-    sends, lands, local, vs, vl, vsend, vland, ns, nl, nsend, nland = rest[5 * count :]
-    parts = [
-        Scatter(wholes[i], *buffers[i], outs[i], sends, lands, local, i) for i in range(count)
+class Cube:
+    def __init__(self, slots, line, sends, lands):
+        self.slots, self.line, self.sends, self.lands = slots, line, sends, lands
+        self.place = grid_place()
+
+    def turned(self, flip):
+        t, _, x, c = self.place
+        return (1 - t if flip & 4 else t), (1 - x if flip & 2 else x), (1 - c if flip & 1 else c)
+
+    def copy(self, slot, which, device):
+        return pltpu.make_async_remote_copy(
+            src_ref=slot,
+            dst_ref=slot,
+            send_sem=self.sends.at[which],
+            recv_sem=self.lands.at[which],
+            device_id=device,
+            device_id_type=MESH,
+        )
+
+    def slot(self, flip):
+        t, x, c = self.turned(flip)
+        return self.slots.at[t * 4 + x * 2 + c]
+
+    def push(self, flip):
+        t, x, c = self.turned(flip)
+        return self.copy(self.slot(0), flip - 1, at_place(t, self.place[1], x, c))
+
+    def along(self, gap, back=False):
+        t, z, x, c = self.place
+        slot = self.line.at[lax.rem(z + 4 - gap, 4) if back else z]
+        return self.copy(slot, 6 + gap, at_place(t, lax.rem(z + gap, 4), x, c))
+
+    def total(self, value):
+        t, z, x, c = self.place
+        self.slots[t * 4 + x * 2 + c] = value
+        for flip in range(1, 8):
+            self.push(flip).start()
+        for flip in range(1, 8):
+            self.copy(self.slot(flip), flip - 1, self.place_of(flip)).wait_recv()
+        self.line[z] = jnp.sum(self.slots[...], axis=0)
+        for gap in range(1, 4):
+            self.along(gap).start()
+        for gap in range(1, 4):
+            self.along(gap, True).wait_recv()
+        return (self.line[0] + self.line[1]) + (self.line[2] + self.line[3])
+
+    def place_of(self, flip):
+        t, x, c = self.turned(flip)
+        return at_place(t, self.place[1], x, c)
+
+    def drain(self):
+        for flip in range(1, 8):
+            self.push(flip).wait_send()
+        for gap in range(1, 4):
+            self.along(gap).wait_send()
+
+
+def scatter_buffers(whole, columns, late=False):
+    halves = lax.axis_size("tensor")
+    rows = whole.shape[1] // lax.axis_size("dp")
+    two, line = ((), (3, halves)) if late else ((4,), (3,))
+    shapes = ((halves, 4, 2), (halves, 4, 2), (2, 4), two, line)
+    return [pltpu.VMEM(shape + (rows, columns), jnp.bfloat16) for shape in shapes]
+
+
+def scatter_parts(pieces, buffers, sems, kind=Scatter):
+    return [
+        kind(
+            whole.at[:, :, :, :, :, first : first + columns],
+            *buffers[5 * index : 5 * index + 5],
+            out.at[:, first : first + columns],
+            *sems,
+            index,
+        )
+        for index, (whole, out, first, columns) in enumerate(pieces)
     ]
-    vector = Total(vs, vl, vsend, vland)
-    norm = Total(ns, nl, nsend, nland)
-    greet_neighbours()
-    parts[0].start()
-    vector.start(vector_ref[...])
-    parts[1].start()
-    parts[0].cores_ready()
-    vector.advance(0)
-    for part in parts[2:]:
-        part.start()
-    parts[1].cores_ready()
-    parts[0].first_ready()
-    vector.advance(1)
-    parts[2].cores_ready()
-    parts[1].first_ready()
-    parts[0].second_ready()
-    vector.advance(2)
-    parts[3].cores_ready()
-    parts[2].first_ready()
-    parts[1].second_ready()
-    squares = []
-    squares.append(jnp.sum(parts[0].finish()))
-    parts[3].first_ready()
-    parts[2].second_ready()
-    squares.append(jnp.sum(parts[1].finish()))
-    total_ref[...] = vector.finish()
-    parts[3].second_ready()
-    squares.append(jnp.sum(parts[2].finish()))
-    squares.append(jnp.sum(parts[3].finish()))
-    norm.start(jnp.full(norm_ref.shape, sum(squares[1:], squares[0])))
-    for stage in range(3):
-        norm.advance(stage)
-    norm_ref[...] = norm.finish()
-    for each in parts + [vector, norm]:
-        each.drain()
-
-
-def scatter_all(wholes, vector):
-    count = len(wholes)
-    anywhere = pl.BlockSpec(memory_space=pl.ANY)
-    vmem = pl.BlockSpec(memory_space=pltpu.VMEM)
-    halves = lax.axis_size("tensor")
-    bf16, f32 = jnp.bfloat16, jnp.float32
-    rows = wholes[0].shape[1] // lax.axis_size("dp")
-    scratch = []
-    for whole in wholes:
-        columns = whole.shape[2]
-        scratch += [
-            pltpu.VMEM((halves, 4, 2, rows, columns), bf16),
-            pltpu.VMEM((halves, 4, 2, rows, columns), bf16),
-            pltpu.VMEM((2, 4, rows, columns), bf16),
-            pltpu.VMEM((4, rows, columns), bf16),
-            pltpu.VMEM((3, rows, columns), bf16),
-        ]
-    small = (8, 128)
-    scratch += [
+
+
+def scatter_sems(count):
+    return [
         pltpu.SemaphoreType.DMA((count, 10)),
         pltpu.SemaphoreType.DMA((count, 10)),
         pltpu.SemaphoreType.DMA((count, 4)),
     ]
-    for shape in (vector.shape, small):
-        scratch += [
-            pltpu.VMEM((6,) + shape, f32),
-            pltpu.VMEM((4,) + shape, f32),
+
+
+def scatter_input(whole):
+    return whole.reshape(lax.axis_size("tensor"), 4, 2, 2, -1, whole.shape[2])
+
+
+def scatter_shape(whole):
+    return jax.ShapeDtypeStruct((whole.shape[1] // lax.axis_size("dp"), whole.shape[2]), jnp.float32)
+
+
+def push_partner(source, target, index, sends, lands):
+    t, z, x, c = grid_place()
+    return pltpu.make_async_remote_copy(
+        src_ref=source.at[index],
+        dst_ref=target.at[index],
+        send_sem=sends.at[index],
+        recv_sem=lands.at[index],
+        device_id=at_place(1 - t, z, x, c),
+        device_id_type=MESH,
+    )
+
+
+class Plan:
+    def __init__(self, actions, times):
+        self.at, self.rest = {}, []
+        points = sorted(times.items(), key=lambda item: item[1])
+        at = 0
+        for due, action in sorted(actions, key=lambda item: item[0]):
+            while at < len(points) and points[at][1] < due:
+                at += 1
+            if at < len(points):
+                self.at.setdefault(points[at][0], []).append(action)
+            else:
+                self.rest.append(action)
+
+    def run(self, point):
+        for (step, where), actions in self.at.items():
+            if where == point:
+
+                @pl.when(pl.program_id(0) == step)
+                def _():
+                    for action in actions:
+                        action()
+
+    def finish(self):
+        for action in self.rest:
+            action()
+
+
+def scatter_actions(parts, ready, link, ended=lambda part: part.finish):
+    actions = []
+    for index, part in enumerate(parts):
+        due = ready + link * index
+        actions += [
+            (due, part.cores_ready),
+            (due + link + 2, part.first_ready),
+            (due + 2 * link + 4, part.second_ready),
+            (due + 2 * link + 7, ended(part)),
+        ]
+    return actions
+
+
+def feed_back_scatter_kernel(chunks, early, columns, whole_ref, tail_ref, *refs):
+    ins, outs, (tail_out, out_ref) = refs[:9], refs[9:15], refs[15:17]
+    scratch, rest = refs[17:20], refs[20:]
+    count = whole_ref.shape[5] // columns
+    buffers, sems, (sends, lands) = rest[: 5 * count], rest[5 * count : 5 * count + 3], rest[5 * count + 3 :]
+    parts = scatter_parts(
+        [(whole_ref, out_ref, index * columns, columns) for index in range(count)], buffers, sems, LateScatter
+    )
+
+    def begin():
+        greet_neighbours()
+        for part in parts:
+            part.start()
+        for index in range(early):
+            push_partner(tail_ref.at[chunks - early :], tail_out, index, sends, lands).start()
+
+    actions = [(0, begin)] + scatter_actions(parts, 8, 6.6)
+    steps = chunks + D // ins[5].shape[1] + 2 * (ins[7].shape[2] // outs[5].shape[2])
+    times = {(step, 0): 4 + 5.3 * step for step in range(chunks)}
+    times |= {(step, 0): 30.5 + 1.7 * (step - chunks) for step in range(chunks, steps)}
+    times |= {(step, 1 + half): 6 + 5.3 * step + 2 * half for step in range(chunks) for half in range(2)}
+    times[(0, 0)] = 0
+    plan = Plan(actions, times)
+    feed_back_kernel(chunks, *ins, *outs, *scratch, plan.run)
+
+    @pl.when(pl.program_id(0) == pl.num_programs(0) - 1)
+    def _():
+        plan.finish()
+        for part in parts:
+            part.drain()
+        for index in range(early):
+            push_partner(tail_ref.at[chunks - early :], tail_out, index, sends, lands).wait()
+
+
+def attend_last_kernel(piece, chunks, columns, spans, one_ref, two_ref, *refs):
+    ins, left_ref, done_ref, first_ref, second_ref, upward_ref, loss_ref = refs[:4], *refs[4:10]
+    dx_ref, low_out, one_out, two_out, last_out, total_ref, norm_ref = refs[10:17]
+    dproj_ref, bias_ref, turned_ref, grad_ref, square_ref, low_ref, sends, lands = refs[17:25]
+    rest = refs[25:]
+    count = one_ref.shape[5] // columns + 1
+    late = scatter_parts(
+        [(one_ref, one_out, index * columns, columns) for index in range(count - 1)]
+        + [(two_ref, two_out, 0, columns)],
+        rest[: 5 * count],
+        rest[5 * count : 5 * count + 3],
+        LateScatter,
+    )
+    rest = rest[5 * count + 3 :]
+    tail = grad_ref.shape[5] // columns
+    last = scatter_parts(
+        [(grad_ref, last_out, index * columns, columns) for index in range(tail)],
+        rest[: 5 * tail],
+        rest[5 * tail : 5 * tail + 3],
+    )
+    rest = rest[5 * tail + 3 :]
+    vector, norm = Total(*rest[:4]), Cube(*rest[4:])
+    step = pl.program_id(0)
+
+    def begin():
+        greet_neighbours(True)
+        for part in late:
+            part.start()
+        square_ref[...] = jnp.zeros_like(square_ref)
+        turned_ref[...] = left_ref[...].T
+
+    def ended(part):
+        def action():
+            square_ref[0:1, :] += part.finish()
+
+        return action
+
+    actions = [(0, begin)] + scatter_actions(late, 8, 6.6, ended)
+    actions += scatter_actions(last, 46, 5, ended)
+    actions += [(46.5, lambda: vector.advance(0)), (50, lambda: vector.advance(1)), (57, lambda: vector.advance(2))]
+    times = {(step, point): 4 + 7.3 * step + 1.15 * point for step in range(chunks) for point in range(7)}
+    times |= {(chunks + tile, 0): 41 + 2.0 * tile for tile in range(2 * tail)}
+    times[(0, 0)] = 0
+    plan = Plan(actions, times)
+    plan.run(0)
+
+    @pl.when(step < chunks)
+    def _():
+        rows = dx_ref.shape[0]
+        here = dproj_ref.at[pl.ds(pl.multiple_of(step * rows, rows), rows), :]
+        attend_back_kernel(piece, spans, *ins, here, dx_ref, bias_ref, low_ref, plan.run)
+
+    for index in range(chunks):
+
+        @pl.when(step == index)
+        def _():
+            if index == chunks - 1:
+                base = bias_ref.shape[1] // 2
+                wide = upward_ref.shape[1] // 2
+                lines = [first_ref[0:2, :], second_ref[0:2, :], first_ref[2:3, :], second_ref[2:3, :]]
+                for half in range(2):
+                    at = half * base
+                    pair = [bias_ref[0:1, at : at + columns]]
+                    pair += [bias_ref[0:1, at + 2 * columns : at + 3 * columns]]
+                    lines.append(jnp.concatenate(pair, axis=1))
+                    lines += [
+                        upward_ref[0:1, half * wide + first : half * wide + first + D]
+                        for first in range(0, wide, D)
+                    ]
+                column = lax.broadcasted_iota(jnp.int32, (1, D), 1)
+                lines.append(jnp.where(column == 1, loss_ref[0:1, 0:1], 0.0))
+                lines.append(jnp.zeros((3, D), jnp.float32))
+                pack = jnp.concatenate(lines, axis=0)
+                vector.start(pack)
+            push_partner(low_ref, low_out, index, sends, lands).start()
+
+    @pl.when(step >= chunks)
+    def _():
+        tile = step - chunks
+        half, piece_index = lax.rem(tile, 2), lax.div(tile, 2)
+        start = pl.multiple_of((half * tail + piece_index) * columns, columns)
+        grad = dot_nn(turned_ref[...], dproj_ref[:, pl.ds(start, columns)]).astype(jnp.bfloat16)
+        start = pl.multiple_of(piece_index * columns, columns)
+        grad_ref[half, :, :, :, :, pl.ds(start, columns)] = grad.reshape(
+            grad_ref.shape[1:5] + (columns,)
+        )
+
+    for index, part in enumerate(last):
+
+        @pl.when(step == chunks + 2 * index + 1)
+        def _():
+            part.start()
+
+    @pl.when(step == pl.num_programs(0) - 1)
+    def _():
+        plan.finish()
+        total_ref[...] = vector.finish()
+        squares = jnp.sum(square_ref[...]) + jnp.sum(done_ref[...] * done_ref[...])
+        norm_ref[...] = norm.total(jnp.full(norm_ref.shape, squares))
+        for each in late + last + [vector, norm]:
+            each.drain()
+        for index in range(chunks):
+            push_partner(low_ref, low_out, index, sends, lands).wait()
+
+
+def adam(weight, moment, square, average, gradient, rate, scalars):
+    factor, first_fix, second_fix = scalars
+    clipped = gradient * factor
+    first = first_decay * moment + (1.0 - first_decay) * clipped
+    second = second_decay * square + (1.0 - second_decay) * clipped * clipped
+    master = weight - rate * (
+        first / first_fix / (jnp.sqrt(second / second_fix) + adam_eps) + decay_weight * weight
+    )
+    smooth = smooth_decay * average + (1.0 - smooth_decay) * master
+    return master, first, second, smooth
+
+
+def finish_kernel(chunk, chunks, rates, passages, halves, *refs):
+    out_own, out_head, out_tail, dx_own, dx_other = refs[:5]
+    large, grads = refs[5:21], refs[21:25]
+    scales_refs, offsets_refs, total_ref, norm_ref, step_ref = refs[25:29], refs[29:33], *refs[33:36]
+    short_out, long_out, short_dx, long_dx = refs[36:40]
+    large_outs, scales_outs, offsets_outs, figures_ref = refs[40:56], refs[56:60], refs[60:64], refs[64]
+    scratch = refs[65:]
+    ins, outs = scratch[:16], scratch[16:32]
+    rows_ref, own_ref, low_ref, wide_ref, in_sems, out_sems, block_sems, wide_sems, load_sems = scratch[32:]
+    place = lax.axis_index("tensor")
+    longs = chunks - 1
+
+    def rows(first, count):
+        return pl.ds(pl.multiple_of(first * chunk, chunk), count * chunk)
+
+    ahead = out_head.shape[0] // chunk
+    other = 1 - place
+    brought = [
+        pltpu.make_async_copy(source, target, load_sems.at[k])
+        for k, (source, target) in enumerate(
+            (
+                (dx_other, low_ref),
+                (out_own, rows_ref.at[rows(0, chunks)]),
+                (out_head, rows_ref.at[rows(chunks, ahead)]),
+                (out_tail, rows_ref.at[rows(chunks + ahead, chunks - ahead)]),
+                (dx_own, own_ref),
+            )
+        )
+    ]
+    for load in brought:
+        load.start()
+    loads = [pltpu.make_async_copy(large[k], ins[k], in_sems.at[k]) for k in range(16)]
+    for load in loads:
+        load.start()
+    blocks = [
+        (rows_ref.at[rows(0, 1)], short_out.at[rows(place, 1)]),
+        (rows_ref.at[rows(1, longs)], long_out.at[rows(place * longs, longs)]),
+        (rows_ref.at[rows(chunks, 1)], short_out.at[rows(other, 1)]),
+        (rows_ref.at[rows(chunks + 1, longs)], long_out.at[rows(other * longs, longs)]),
+        (own_ref.at[rows(0, 1)], short_dx.at[rows(place, 1)]),
+        (own_ref.at[rows(1, longs)], long_dx.at[rows(place * longs, longs)]),
+    ]
+    copies = [
+        pltpu.make_async_copy(source, target, block_sems.at[k])
+        for k, (source, target) in enumerate(blocks)
+    ]
+    brought[0].wait()
+    for index in range(chunks):
+        wide_ref[index] = low_ref[rows(index, 1), :].astype(jnp.float32)
+        target = short_dx.at[rows(other, 1)]
+        if index > 0:
+            target = long_dx.at[rows(other * longs + index - 1, 1)]
+        copy = pltpu.make_async_copy(wide_ref.at[index], target, wide_sems.at[index])
+        copy.start()
+        copies.append(copy)
+    for load in brought[1:]:
+        load.wait()
+    for copy in copies[:6]:
+        copy.start()
+
+    sums = total_ref[...]
+    row = lax.broadcasted_iota(jnp.int32, sums.shape, 0)
+    column = lax.broadcasted_iota(jnp.int32, sums.shape, 1)
+
+    def whole_sum(value):
+        return jnp.sum(jnp.sum(value, axis=1, keepdims=True), axis=0, keepdims=True)
+
+    squares = norm_ref[0:1, 0:1] + whole_sum(jnp.where(row < 12, sums * sums, 0.0))
+    loss = whole_sum(jnp.where(jnp.logical_and(row == 12, column == 1), sums, 0.0))
+    norm = jnp.sqrt(squares)
+    factor = clip_limit / jnp.maximum(norm, clip_limit)
+    steps = jnp.full((1, 1), step_ref[0], jnp.int32).astype(jnp.float32)
+    first_fix = 1.0 - jnp.exp(steps * math.log(first_decay))
+    second_fix = 1.0 - jnp.exp(steps * math.log(second_decay))
+    scalars = (factor, first_fix, second_fix)
+    figure = lax.broadcasted_iota(jnp.int32, figures_ref.shape, 0)
+    figures_ref[...] = jnp.where(figure == 0, norm, loss / (halves * passages))
+    for each in range(4):
+        values = []
+        for k in range(4 * each, 4 * each + 4):
+            loads[k].wait()
+            values.append(ins[k][...])
+        gradient = grads[each][...]
+        if values[0].ndim == 3:
+            width = values[0].shape[2]
+            gradient = jnp.stack([gradient[:, k * width : (k + 1) * width] for k in range(3)])
+        fixed = [one.reshape((1,) * values[0].ndim) for one in scalars]
+        new = adam(*values, gradient, rates[each], fixed)
+        for part in range(4):
+            k = 4 * each + part
+            outs[k][...] = new[part]
+            copy = pltpu.make_async_copy(outs[k], large_outs[k], out_sems.at[k])
+            copy.start()
+            copies.append(copy)
+    new = adam(*(ref[...] for ref in scales_refs), sums[:6], rates[4], scalars)
+    for ref, value in zip(scales_outs, new):
+        ref[...] = value
+    mine = jnp.where(place == 0, sums[6:9], sums[9:12])
+    width = offsets_refs[0].shape[1]
+    mine = jnp.concatenate(
+        [mine[r : r + 1, c : c + width] for r in range(3) for c in range(0, D, width)], axis=0
+    )
+    new = adam(*(ref[...] for ref in offsets_refs), mine, rates[5], scalars)
+    for ref, value in zip(offsets_outs, new):
+        ref[...] = value
+    for copy in copies:
+        copy.wait()
+
+
+def finish(chunk, halves_of_rows, large, grads, scales, offsets, total, norm, step_count, passages):
+    chunks = halves_of_rows[0].shape[0] // chunk
+    halves = lax.axis_size("tensor")
+    anywhere = pl.BlockSpec(memory_space=pl.ANY)
+    vmem = pl.BlockSpec(memory_space=pltpu.VMEM)
+    smem = pl.BlockSpec(memory_space=pltpu.SMEM)
+    f32, bf16 = jnp.float32, jnp.bfloat16
+    rates = (1.0 / math.sqrt(D), 8.0 / math.sqrt(D), 1.0 / math.sqrt(D), 1.0 / math.sqrt(FF), 0.3, 0.3)
+    offsets = [each.reshape(-1, 128) for each in offsets]
+    shaped = [jax.ShapeDtypeStruct(each.shape, f32) for each in (*large, *scales, *offsets)]
+    both = [
+        jax.ShapeDtypeStruct((halves * count * chunk, D), dtype)
+        for dtype in (bf16, f32)
+        for count in (1, chunks - 1)
+    ]
+    outs = pl.pallas_call(
+        functools.partial(finish_kernel, chunk, chunks, rates, passages, halves),
+        in_specs=[anywhere] * 21 + [vmem] * 14 + [smem],
+        out_specs=[anywhere] * 20 + [vmem] * 9,
+        out_shape=both + shaped + [jax.ShapeDtypeStruct((8, 128), f32)],
+        scratch_shapes=[pltpu.VMEM(each.shape, f32) for each in large] * 2
+        + [
+            pltpu.VMEM((halves * chunks * chunk, D), bf16),
+            pltpu.VMEM((chunks * chunk, D), f32),
+            pltpu.VMEM((chunks * chunk, D), bf16),
+            pltpu.VMEM((chunks, chunk, D), f32),
+            pltpu.SemaphoreType.DMA((16,)),
+            pltpu.SemaphoreType.DMA((16,)),
             pltpu.SemaphoreType.DMA((6,)),
-            pltpu.SemaphoreType.DMA((6,)),
-        ]
-    outs = pl.pallas_call(
-        functools.partial(scatter_kernel, count),
-        in_specs=[anywhere] * count + [vmem],
-        out_specs=[vmem] * (count + 2),
-        out_shape=[jax.ShapeDtypeStruct((rows, whole.shape[2]), f32) for whole in wholes]
-        + [jax.ShapeDtypeStruct(vector.shape, f32), jax.ShapeDtypeStruct(small, f32)],
-        scratch_shapes=scratch,
-        compiler_params=pltpu.CompilerParams(
-            collective_id=4, has_side_effects=True, vmem_limit_bytes=big_vmem
-        ),
-        name="scatter_all",
-    )(*(whole.reshape(halves, 4, 2, 2, rows, -1) for whole in wholes), vector)
-    return outs[:count], outs[count], outs[count + 1][0, 0]
+            pltpu.SemaphoreType.DMA((chunks,)),
+            pltpu.SemaphoreType.DMA((5,)),
+        ],
+        compiler_params=pltpu.CompilerParams(vmem_limit_bytes=big_vmem),
+        name="finish",
+    )(*halves_of_rows, *large, *grads, *scales, *offsets, total, norm, step_count)
+    return outs[:4], outs[4:20], outs[20:24], [each.reshape(-1) for each in outs[24:28]], outs[28]
 
 
 def row_spec(rows, columns):
@@ -1088,16 +1664,6 @@
             axis=0,
         )
 
-    def both_halves(own, other):
-        own_first = place == 0
-        low = jnp.where(own_first, own, other)
-        high = jnp.where(own_first, other, own)
-        head = shorts * short_span
-        return (
-            jnp.concatenate([low[:head], high[:head]]).reshape(short_tokens.shape),
-            jnp.concatenate([low[head:], high[head:]]).reshape(long_tokens.shape),
-        )
-
     fast = lax.axis_size("dp") == 16 and halves == 2
     mixing_own = mixing_weight.astype(jnp.bfloat16).reshape(-1, 3 * width)
     middle_own = jnp.concatenate([merging_weight.T, expand_weight], axis=1).astype(jnp.bfloat16)
@@ -1123,8 +1689,14 @@
     mixing_columns = halves * 3 * width
     scores_flops = 2 * rows * chunk * PAIR * (halves * width // HEAD_DIM)
     if fast:
-        qkv, context, mixing_full, middle_full, shrink_full, offsets_both = attend_gather(
-            piece, spans, inputs, mixing_own, middle_own, shrink_own, offsets_weight, chunk
+        (qkv, context), feed, (mixing_full, middle_full, shrink_full) = forward_gather(
+            piece,
+            spans,
+            inputs,
+            (mixing_own, middle_own, shrink_own),
+            offsets_weight,
+            scales_weight,
+            chunk,
         )
     else:
         mixing_full, middle_full, shrink_full = (
@@ -1163,241 +1735,362 @@
             ),
             name="attend_forward",
         )(spans, inputs, mixing_full, mixing_bias)
-    upward_bias = offsets_both[:, 2 * width :].reshape(1, -1)
-    output, hidden_low, activated, slope, normed_first, rstd_first, normed_second, rstd_second = (
-        pl.pallas_call(
-            feed_forward_kernel,
+        upward_bias = offsets_both[:, 2 * width :].reshape(1, -1)
+        feed_ins = [context, inputs, middle_full, shrink_full, scales_weight, upward_bias]
+        feed_in_specs = [
+            row_spec(chunk, D),
+            row_spec(chunk, D),
+            full_spec(middle_full.shape),
+            full_spec(shrink_full.shape),
+            full_spec(scales_weight.shape),
+            full_spec(upward_bias.shape),
+        ]
+        feed_out_specs = [
+            row_spec(chunk, D),
+            row_spec(chunk, FF),
+            row_spec(chunk, FF),
+            row_spec(chunk, D),
+            row_spec(chunk, 1),
+            row_spec(chunk, D),
+            row_spec(chunk, D),
+            row_spec(chunk, 1),
+            pl.BlockSpec((1, 8, D), lambda i: (i, 0, 0)),
+        ]
+        feed_outs = [
+            shaped(D, bf16),
+            shaped(FF, bf16),
+            shaped(FF, bf16),
+            shaped(D, f32),
+            shaped(1, f32),
+            shaped(D, bf16),
+            shaped(D, f32),
+            shaped(1, f32),
+            jax.ShapeDtypeStruct((chunks, 8, D), f32),
+        ]
+        feed_cost = pl.CostEstimate(
+            flops=2 * rows * D * (D + 2 * FF),
+            bytes_accessed=48 * 1024 * 1024,
+            transcendentals=2 * rows * FF,
+        )
+        feed = pl.pallas_call(
+            functools.partial(feed_forward_kernel, piece),
             grid=(chunks,),
-            in_specs=[
+            in_specs=feed_in_specs,
+            out_specs=feed_out_specs,
+            out_shape=feed_outs,
+            compiler_params=params,
+            cost_estimate=feed_cost,
+            name="feed_forward",
+        )(*feed_ins)
+    anywhere = pl.BlockSpec(memory_space=pl.ANY)
+    (
+        hidden_low,
+        activated,
+        slope,
+        normed_first,
+        rstd_first,
+        output,
+        normed_second,
+        rstd_second,
+        leading,
+    ) = feed
+    query_gradient, lead_rows, loss_rows = contrast(leading, queries, positives)
+    ahead = 2
+    if fast:
+        output_head = lax.optimization_barrier((output[: ahead * chunk], lead_rows))[0]
+        output_head = tensor_swap(output_head)
+    tile = 512
+    per = wide // tile
+
+    def chunk_spec(columns):
+        return pl.BlockSpec((chunk, columns), lambda i: (jnp.minimum(i, chunks - 1), 0))
+
+    second_back, second_grad, shrink_grad = pl.pallas_call(
+        functools.partial(out_back_kernel, piece, chunks),
+        grid=(chunks + FF // tile,),
+        in_specs=[
+            chunk_spec(D),
+            pl.BlockSpec((1, 8, D), lambda i: (jnp.minimum(i, chunks - 1), 0, 0)),
+            chunk_spec(D),
+            chunk_spec(1),
+            full_spec(scales_weight.shape),
+            pl.BlockSpec((rows, tile), lambda i: (0, jnp.maximum(i - chunks, 0))),
+        ],
+        out_specs=[
+            chunk_spec(D),
+            pl.BlockSpec((8, D), lambda i: (0, 0)),
+            pl.BlockSpec(
+                (1, D, tile),
+                lambda i: (jnp.maximum(i - chunks, 0) // per, 0, jnp.maximum(i - chunks, 0) % per),
+            ),
+        ],
+        out_shape=[
+            shaped(D, f32),
+            jax.ShapeDtypeStruct((8, D), f32),
+            jax.ShapeDtypeStruct((halves, D, wide), bf16),
+        ],
+        scratch_shapes=[pltpu.VMEM((D, rows), bf16)],
+        compiler_params=params,
+        cost_estimate=pl.CostEstimate(
+            flops=2 * rows * D * FF, bytes_accessed=32 * 1024 * 1024, transcendentals=0
+        ),
+        name="out_back",
+    )(cotangent, lead_rows, normed_second, rstd_second, scales_weight, activated)
+    back_ins = [
+        second_back,
+        normed_first,
+        rstd_first,
+        slope,
+        hidden_low,
+        context,
+        middle_full,
+        shrink_full,
+        scales_weight,
+    ]
+    merging_tiles = D // width
+    back_steps = chunks + merging_tiles + FF // tile
+
+    def merging_at(i):
+        return jnp.clip(i - chunks, 0, merging_tiles - 1)
+
+    def expand_at(i):
+        return jnp.maximum(i - chunks - merging_tiles, 0)
+
+    back_in_specs = [
+        chunk_spec(D),
+        chunk_spec(D),
+        chunk_spec(1),
+        chunk_spec(FF),
+        chunk_spec(D),
+        pl.BlockSpec((rows, width), lambda i: (0, merging_at(i))),
+        full_spec(middle_full.shape),
+        full_spec(shrink_full.shape),
+        full_spec(scales_weight.shape),
+    ]
+    back_out_specs = [
+        chunk_spec(D),
+        chunk_spec(D),
+        pl.BlockSpec((8, D), lambda i: (0, 0)),
+        pl.BlockSpec((8, FF), lambda i: (0, 0)),
+        pl.BlockSpec((1, D, width), lambda i: (merging_at(i), 0, 0)),
+        pl.BlockSpec((1, D, tile), lambda i: (expand_at(i) // per, 0, expand_at(i) % per)),
+    ]
+    back_outs = [
+        shaped(D, f32),
+        shaped(D, bf16),
+        jax.ShapeDtypeStruct((8, D), f32),
+        jax.ShapeDtypeStruct((8, FF), f32),
+        jax.ShapeDtypeStruct((halves, D, width), bf16),
+        jax.ShapeDtypeStruct((halves, D, wide), bf16),
+    ]
+    back_scratch = [
+        pltpu.VMEM((rows, FF), bf16),
+        pltpu.VMEM((D, rows), bf16),
+        pltpu.VMEM((D, rows), bf16),
+    ]
+    back_cost = pl.CostEstimate(
+        flops=2 * rows * D * (2 * D + 3 * FF), bytes_accessed=48 * 1024 * 1024, transcendentals=0
+    )
+    if fast:
+        shrink_grad, output_head = lax.optimization_barrier((shrink_grad, output_head))
+        tail = output.reshape(chunks, chunk, D)
+        *back, output_tail, shrink_sum = pl.pallas_call(
+            functools.partial(feed_back_scatter_kernel, chunks, chunks - ahead, width),
+            grid=(back_steps,),
+            in_specs=[anywhere, full_spec(tail.shape)] + back_in_specs,
+            out_specs=back_out_specs + [anywhere, full_spec(scatter_shape(shrink_grad).shape)],
+            out_shape=back_outs
+            + [jax.ShapeDtypeStruct((chunks - ahead, chunk, D), bf16), scatter_shape(shrink_grad)],
+            scratch_shapes=back_scratch
+            + scatter_buffers(shrink_grad, width, True) * (wide // width)
+            + scatter_sems(wide // width)
+            + [pltpu.SemaphoreType.DMA((chunks - ahead,))] * 2,
+            compiler_params=pltpu.CompilerParams(
+                collective_id=5, has_side_effects=True, vmem_limit_bytes=big_vmem
+            ),
+            cost_estimate=back_cost,
+            name="feed_back_scatter",
+        )(scatter_input(shrink_grad), tail, *back_ins)
+    else:
+        back = pl.pallas_call(
+            functools.partial(feed_back_kernel, chunks),
+            grid=(back_steps,),
+            in_specs=back_in_specs,
+            out_specs=back_out_specs,
+            out_shape=back_outs,
+            scratch_shapes=back_scratch,
+            compiler_params=params,
+            cost_estimate=back_cost,
+            name="feed_back",
+        )(*back_ins)
+        shrink_sum = scattered(shrink_grad)
+        output_head = tensor_swap(output[: ahead * chunk])
+        output_tail = tensor_swap(output[ahead * chunk :])
+    first_back, context_back, first_grad, upward_grad, merging_grad, expand_grad = back
+    pair_ins = [qkv, context_back, first_back, mixing_full]
+    pair_in_specs = [
+        chunk_spec(mixing_columns),
+        chunk_spec(D),
+        chunk_spec(D),
+        full_spec(mixing_full.shape),
+    ]
+    pair_cost = pl.CostEstimate(
+        flops=2 * rows * D * mixing_columns + 15 * scores_flops,
+        bytes_accessed=24 * 1024 * 1024,
+        transcendentals=rows * chunk * 12,
+    )
+    lane = lax.broadcasted_iota(jnp.int32, (1, D), 1)
+    losses = jnp.where(lane == 1, loss_rows[0, 0], 0.0)
+
+    def stacked(bias_both, scalars):
+        scalars = jnp.pad(scalars, ((0, 3), (0, 0)))
+        offsets_grad = jnp.concatenate([bias_both, upward_grad[0].reshape(halves, wide)], axis=1)
+        vectors = [first_grad[:2], second_grad[:2], first_grad[2:3], second_grad[2:3]]
+        return jnp.concatenate(vectors + [offsets_grad.reshape(-1, D), scalars], axis=0)
+
+    if fast:
+        parts = (expand_grad, merging_grad)
+        late_count, last_count = wide // width + 1, 3
+        last_whole = jax.ShapeDtypeStruct((halves, D, 3 * width), bf16)
+        vector = jax.ShapeDtypeStruct((16, D), f32)
+        more = (inputs, shrink_sum, first_grad, second_grad, upward_grad, loss_rows)
+        small = (8, 128)
+        out_shape = [
+            shaped(D, f32),
+            jax.ShapeDtypeStruct((chunks, chunk, D), bf16),
+            scatter_shape(expand_grad),
+            scatter_shape(merging_grad),
+            scatter_shape(last_whole),
+            jax.ShapeDtypeStruct(vector.shape, f32),
+            jax.ShapeDtypeStruct(small, f32),
+        ]
+        input_back, input_other, expand_sum, merging_sum, mixing_sum, summed, squares_all = (
+            pl.pallas_call(
+                functools.partial(attend_last_kernel, piece, chunks, width),
+                grid=(chunks + 2 * last_count,),
+                in_specs=[smem, anywhere, anywhere]
+                + pair_in_specs
+                + [full_spec(each.shape) for each in more],
+                out_specs=[chunk_spec(D), anywhere]
+                + [full_spec(each.shape) for each in out_shape[2:]],
+                out_shape=out_shape,
+                scratch_shapes=[
+                    pltpu.VMEM((rows, mixing_columns), bf16),
+                    pltpu.VMEM((8, mixing_columns), f32),
+                    pltpu.VMEM((D, rows), bf16),
+                    pltpu.VMEM((halves, 4, 2, 2, D // 16, 3 * width), bf16),
+                    pltpu.VMEM((8, width), f32),
+                    pltpu.VMEM((chunks, chunk, D), bf16),
+                    pltpu.SemaphoreType.DMA((chunks,)),
+                    pltpu.SemaphoreType.DMA((chunks,)),
+                ]
+                + scatter_buffers(expand_grad, width, True) * late_count
+                + scatter_sems(late_count)
+                + scatter_buffers(last_whole, width) * last_count
+                + scatter_sems(last_count)
+                + [
+                    pltpu.VMEM((6,) + vector.shape, f32),
+                    pltpu.VMEM((4,) + vector.shape, f32),
+                    pltpu.SemaphoreType.DMA((6,)),
+                    pltpu.SemaphoreType.DMA((6,)),
+                    pltpu.VMEM((8,) + small, f32),
+                    pltpu.VMEM((4,) + small, f32),
+                    pltpu.SemaphoreType.DMA((10,)),
+                    pltpu.SemaphoreType.DMA((10,)),
+                ],
+                compiler_params=pltpu.CompilerParams(
+                    collective_id=6, has_side_effects=True, vmem_limit_bytes=big_vmem
+                ),
+                cost_estimate=pair_cost,
+                name="attend_last",
+            )(
+                spans,
+                *(scatter_input(part) for part in parts),
+                *pair_ins,
+                *more,
+            )
+        )
+    else:
+        projected_back, input_back, bias_grad, input_low = pl.pallas_call(
+            functools.partial(attend_back_kernel, piece),
+            grid=(chunks,),
+            in_specs=[smem] + pair_in_specs,
+            out_specs=[
+                row_spec(chunk, mixing_columns),
                 row_spec(chunk, D),
-                row_spec(chunk, D),
-                full_spec(middle_full.shape),
-                full_spec(shrink_full.shape),
-                full_spec(scales_weight.shape),
-                full_spec(upward_bias.shape),
-            ],
-            out_specs=[
-                row_spec(chunk, D),
-                row_spec(chunk, D),
-                row_spec(chunk, FF),
-                row_spec(chunk, FF),
-                row_spec(chunk, D),
-                row_spec(chunk, 1),
-                row_spec(chunk, D),
-                row_spec(chunk, 1),
+                pl.BlockSpec((8, mixing_columns), lambda i: (0, 0)),
+                pl.BlockSpec((1, chunk, D), lambda i: (i, 0, 0)),
             ],
             out_shape=[
-                shaped(D, bf16),
-                shaped(D, bf16),
-                shaped(FF, bf16),
-                shaped(FF, bf16),
+                shaped(mixing_columns, bf16),
                 shaped(D, f32),
-                shaped(1, f32),
-                shaped(D, f32),
-                shaped(1, f32),
+                jax.ShapeDtypeStruct((8, mixing_columns), f32),
+                jax.ShapeDtypeStruct((chunks, chunk, D), bf16),
             ],
             compiler_params=params,
-            cost_estimate=pl.CostEstimate(
-                flops=2 * rows * D * (D + 2 * FF),
-                bytes_accessed=48 * 1024 * 1024,
-                transcendentals=2 * rows * FF,
-            ),
-            name="feed_forward",
-        )(
-            context,
-            inputs,
-            middle_full,
-            shrink_full,
-            scales_weight,
-            upward_bias,
-        )
+            cost_estimate=pair_cost,
+            name="attend_back",
+        )(spans, *pair_ins)
+        expand_sum, merging_sum = scattered(expand_grad), scattered(merging_grad)
+        input_other = tensor_swap(input_low)
+        mixing_sum = scattered(weight_grad(inputs, projected_back, halves, 384))
+        sums = (shrink_sum, expand_sum, merging_sum, mixing_sum)
+        squares_part = sum(jnp.sum(each * each) for each in sums)
+        bias_both = bias_grad[0].reshape(halves, 3, width)
+        bias_both = jnp.concatenate([bias_both[:, 0], bias_both[:, 2]], axis=1)
+        summed = all_total(stacked(bias_both, jnp.where(lane == 0, squares_part, losses)))
+        squares_all = jnp.full((8, 128), summed[12, 0])
+    grads = (mixing_sum, merging_sum, expand_sum, shrink_sum)
+
+    def turn(value):
+        return value.transpose(1, 0, 2)
+
+    large = (
+        turn(mixing_weight),
+        turn(mixing_moment),
+        turn(mixing_square),
+        turn(mixing_average),
+        merging_weight.T,
+        merging_moment.T,
+        merging_square.T,
+        merging_average.T,
+        expand_weight,
+        expand_moment,
+        expand_square,
+        expand_average,
+        shrink_weight.T,
+        shrink_moment.T,
+        shrink_square.T,
+        shrink_average.T,
     )
-    leading = jnp.concatenate([output[: shorts * piece : piece], output[chunk::chunk]], axis=0)
-    query_gradient, lead_back, loss_part = contrast(leading, queries, positives)
-    output_other = tensor_swap(lax.optimization_barrier((output, lead_back))[0])
-    lead_rows = jnp.zeros((chunks, 8, D), f32)
-    lead_rows = lead_rows.at[0, :shorts].set(lead_back[:shorts])
-    lead_rows = lead_rows.at[1:, 0].set(lead_back[shorts:])
-    down_low, upward_low, first_low, first_back, context_back, vector_grad, upward_grad = (
-        pl.pallas_call(
-            functools.partial(feed_back_kernel, piece),
-            grid=(chunks,),
-            in_specs=[
-                row_spec(chunk, D),
-                pl.BlockSpec((1, 8, D), lambda i: (i, 0, 0)),
-                row_spec(chunk, D),
-                row_spec(chunk, 1),
-                row_spec(chunk, D),
-                row_spec(chunk, 1),
-                row_spec(chunk, FF),
-                full_spec(middle_full.shape),
-                full_spec(shrink_full.shape),
-                full_spec(scales_weight.shape),
-            ],
-            out_specs=[
-                row_spec(chunk, D),
-                row_spec(chunk, FF),
-                row_spec(chunk, D),
-                row_spec(chunk, D),
-                row_spec(chunk, D),
-                pl.BlockSpec((8, D), lambda i: (0, 0)),
-                pl.BlockSpec((8, FF), lambda i: (0, 0)),
-            ],
-            out_shape=[
-                shaped(D, bf16),
-                shaped(FF, bf16),
-                shaped(D, bf16),
-                shaped(D, f32),
-                shaped(D, bf16),
-                jax.ShapeDtypeStruct((8, D), f32),
-                jax.ShapeDtypeStruct((8, FF), f32),
-            ],
-            compiler_params=params,
-            cost_estimate=pl.CostEstimate(
-                flops=2 * rows * D * (D + 2 * FF),
-                bytes_accessed=48 * 1024 * 1024,
-                transcendentals=0,
-            ),
-            name="feed_back",
-        )(
-            cotangent,
-            lead_rows,
-            normed_first,
-            rstd_first,
-            normed_second,
-            rstd_second,
-            slope,
-            middle_full,
-            shrink_full,
-            scales_weight,
-        )
+    both, large_new, scales_new, offsets_new, figures = finish(
+        chunk,
+        (output, output_head, output_tail.reshape(-1, D), input_back, input_other.reshape(rows, D)),
+        large,
+        grads,
+        (scales_weight, scales_moment, scales_square, scales_average),
+        (offsets_weight, offsets_moment, offsets_square, offsets_average),
+        summed,
+        squares_all,
+        step_count,
+        queries.shape[0] * lax.axis_size("dp"),
     )
-    projected_back, input_back, input_low, bias_grad = pl.pallas_call(
-        functools.partial(attend_back_kernel, piece),
-        grid=(chunks,),
-        in_specs=[
-            smem,
-            row_spec(chunk, mixing_columns),
-            row_spec(chunk, D),
-            row_spec(chunk, D),
-            full_spec(mixing_full.shape),
-        ],
-        out_specs=[
-            row_spec(chunk, mixing_columns),
-            row_spec(chunk, D),
-            row_spec(chunk, D),
-            pl.BlockSpec((8, mixing_columns), lambda i: (0, 0)),
-        ],
-        out_shape=[
-            shaped(mixing_columns, bf16),
-            shaped(D, f32),
-            shaped(D, bf16),
-            jax.ShapeDtypeStruct((8, mixing_columns), f32),
-        ],
-        compiler_params=params,
-        cost_estimate=pl.CostEstimate(
-            flops=2 * rows * D * mixing_columns + 15 * scores_flops,
-            bytes_accessed=24 * 1024 * 1024,
-            transcendentals=rows * chunk * 12,
-        ),
-        name="attend_back",
-    )(spans, qkv, context_back, first_back, mixing_full)
-    input_other = tensor_swap(input_low)
-    down_low, hidden_low, first_low, inputs, output_other, input_back = lax.optimization_barrier(
-        (down_low, hidden_low, first_low, inputs, output_other, input_back)
-    )
-    shrink_grad = weight_grad(down_low, activated, halves, 512)
-    expand_grad = weight_grad(hidden_low, upward_low, halves, 512)
-    merging_grad = weight_grad(first_low, context, halves, 384)
-    mixing_grad = weight_grad(inputs, projected_back, halves, 384)
-
-    mixing_grad, input_other = lax.optimization_barrier((mixing_grad, input_other))
-    short_output, long_output = both_halves(output, output_other)
-    short_gradient, long_gradient = both_halves(input_back, input_other.astype(f32))
-
-    bias_both = bias_grad[0].reshape(halves, 3, width)
-    offsets_grad = jnp.concatenate(
-        [bias_both[:, 0], bias_both[:, 2], upward_grad[0].reshape(halves, wide)], axis=1
-    )
-    lane = lax.broadcasted_iota(jnp.int32, (1, D), 1)
-    grads = (shrink_grad, expand_grad, merging_grad, mixing_grad)
-
-    def stacked(scalars):
-        scalars = jnp.pad(scalars, ((0, 3), (0, 0)))
-        return jnp.concatenate([vector_grad[:6], offsets_grad.reshape(-1, D), scalars], axis=0)
-
-    losses = jnp.where(lane == 1, loss_part, 0.0)
-    if fast:
-        sums, summed, squares_all = scatter_all(grads, stacked(losses))
-    else:
-        sums = [scattered(grad) for grad in grads]
-        squares_part = sum(jnp.sum(each * each) for each in sums)
-        summed = all_total(stacked(jnp.where(lane == 0, squares_part, losses)))
-        squares_all = summed[12, 0]
-    shrink_sum, expand_sum, merging_sum, mixing_sum = sums
-    reduced = (mixing_sum.reshape(mixing_weight.shape), merging_sum.T, expand_sum, shrink_sum.T)
-    scales_sum = summed[:6]
-    offsets_all = summed[6:12].reshape(halves, -1)
-    offsets_sum = jnp.where(place == 0, offsets_all[0], offsets_all[1])
-    squares_all = squares_all + jnp.sum(summed[:12] * summed[:12])
-    loss_all = summed[12, 1] / halves
-    norm_value = jnp.sqrt(squares_all)
-    factor = clip_limit / jnp.maximum(norm_value, clip_limit)
-    steps_float = step_count[0].astype(jnp.float32)
-    first_fix = 1.0 - jnp.power(first_decay, steps_float)
-    second_fix = 1.0 - jnp.power(second_decay, steps_float)
-
-    def update(weight, moment, square, average, gradient, rate):
-        clipped = gradient * factor
-        first = first_decay * moment + (1.0 - first_decay) * clipped
-        second = second_decay * square + (1.0 - second_decay) * clipped * clipped
-        master = weight - rate * (
-            first / first_fix / (jnp.sqrt(second / second_fix) + adam_eps) + decay_weight * weight
-        )
-        smooth = smooth_decay * average + (1.0 - smooth_decay) * master
-        return (master, first, second, smooth)
-
-    mixing_new = update(
-        mixing_weight, mixing_moment, mixing_square, mixing_average, reduced[0], 1.0 / math.sqrt(D)
-    )
-    merging_new = update(
-        merging_weight,
-        merging_moment,
-        merging_square,
-        merging_average,
-        reduced[1],
-        8.0 / math.sqrt(D),
-    )
-    expand_new = update(
-        expand_weight, expand_moment, expand_square, expand_average, reduced[2], 1.0 / math.sqrt(D)
-    )
-    shrink_new = update(
-        shrink_weight, shrink_moment, shrink_square, shrink_average, reduced[3], 1.0 / math.sqrt(FF)
-    )
-    scales_new = update(
-        scales_weight, scales_moment, scales_square, scales_average, scales_sum, 0.3
-    )
-    offsets_new = update(
-        offsets_weight, offsets_moment, offsets_square, offsets_average, offsets_sum, 0.3
-    )
-    contrast_loss = (loss_all / (queries.shape[0] * lax.axis_size("dp"))).reshape(1)
-    gradient_norm = norm_value.reshape(1)
     return (
         (
-            short_output,
-            long_output,
-            short_gradient,
-            long_gradient,
+            both[0].reshape(short_tokens.shape),
+            both[1].reshape(long_tokens.shape),
+            both[2].reshape(short_tokens.shape),
+            both[3].reshape(long_tokens.shape),
             query_gradient,
-            contrast_loss,
-            gradient_norm,
-        )
-        + mixing_new
-        + merging_new
-        + expand_new
-        + shrink_new
-        + scales_new
-        + offsets_new
+            figures[1, :1],
+            figures[0, :1],
+        )
+        + tuple(turn(each) for each in large_new[:4])
+        + tuple(each.T for each in large_new[4:8])
+        + tuple(large_new[8:12])
+        + tuple(each.T for each in large_new[12:])
+        + tuple(scales_new)
+        + tuple(offsets_new)
     )
 
 

time: 424 us -> 323 us (0.76)
  Pallas kernels: 336 us -> 304 us
  other arithmetic: 33.5 us -> 8.65 us
  local copies, waits for them, and re-layouts: 27 us -> 6.93 us
  waiting for transfers between devices: 17.3 us -> 0.01 us
  between operations: 6.32 us -> 1.45 us
    pallas_call x9 -> x5, Pallas kernels: 314 us -> 284 us  [the longest x1 101 us: shards(): pl.pallas_call(functools.partial(attend_last_kernel, piece, chunks, width...]
    ppermute x2 -> x1, waiting for transfers between devices: 17.3 us -> 0.01 us  [tensor_swap(): return lax.ppermute(value, 'tensor', [(0, 1), (1, 0)])]
    slice x17 -> x2, local copies, waits for them, and re-layouts: 16 us -> 2.46 us  [the longest x1 1.28 us: shards(): figures[0, :1]]
    concatenate x7 -> x0, other arithmetic: 10.4 us -> none  [the longest x2 7.01 us: both_halves(): jnp.concatenate([low[head:], high[head:]]).reshape(long_tokens.shape)]
    add x6 -> x0, other arithmetic: 5.37 us -> none  [update(): smooth = smooth_decay * average + (1.0 - smooth_decay) * master]
    select_n x3 -> x0, other arithmetic: 4.6 us -> none  [the longest x2 3.95 us: both_halves(): low = jnp.where(own_first, own, other)]
  transfers between devices with their start and end apart: 2 -> 1, of which waited for: 1 -> 0; matrix products, arithmetic and copies ran while one was open for 3% -> 0% of each run, Pallas kernels for 19% -> 5%
where the time goes in v3:
time: 323 us; the launch traced here: 322 us
  Pallas kernels  304 us (94%)
  other arithmetic  8.65 us (3%)
  local copies, waits for them, and re-layouts  6.93 us (2%)
    pallas_call x1, Pallas kernels, shards(): pl.pallas_call(functools.partial(attend_last_kernel, piece, chunks, width...  101 us
    pallas_call x1, Pallas kernels, forward_gather(): pl.pallas_call(functools.partial(forward_gather_kernel, piece, chunks), g...  97.3 us
    pallas_call x1, Pallas kernels, shards(): pl.pallas_call(functools.partial(feed_back_scatter_kernel, chunks, chunks...  56.2 us
    pallas_call x1, Pallas kernels, contrast(): pl.pallas_call(functools.partial(contrast_kernel, count, own, halves), in...  19.8 us
    pallas_call x1, Pallas kernels, shards(): pl.pallas_call(functools.partial(out_back_kernel, piece, chunks), grid=(c...  16.4 us
    pallas_call x1, Pallas kernels, finish(): pl.pallas_call(functools.partial(finish_kernel, chunk, chunks, rates, pas...  13.1 us
  transfers between devices with their start and end apart: 1, of which 0 were waited for; matrix products, arithmetic and copies ran while one was open for 0% of the time, Pallas kernels for 5%

profile of v3, /device:TPU:0, one launch (start us, length us, event | category | flops | bytes accessed | tf_op | source)
XLA Modules:
  0.0 322.1 jit_solution(15955835417434786701)
XLA Ops:
  0.7 0.0 copy-start
  0.7 0.7 dynamic_slice.19
  1.4 0.0 copy-done
  1.4 0.1 dynamic-slice_bitcast_fusion
  1.5 1.0 convert.7
  2.5 0.9 bitcast_convert_fusion.1
  3.4 0.9 convert_bitcast_fusion
  4.3 0.7 copy.66
  5.0 1.6 bitcast_convert_fusion.shrink_ref
  6.6 2.2 constant_dynamic-slice_fusion
  8.8 0.0 copy-done.3
  8.9 0.1 copy-done.4
  9.0 0.1 constant_dynamic-slice_fusion.1
  9.0 1.4 pad_maximum_fusion.x_ref.refs_4_
  10.4 0.1 broadcast_subtract_fusion
  10.5 0.6 pad_add_fusion.spans
  11.1 0.7 pad_maximum_fusion.2.middle_ref
  11.8 97.3 %forward_gather.1 = (bf16[1280,2304]{1,0:T(8,128)(2,1)}, bf16[1280,768]{1,0:T(8,128)(2,1)}, bf16[1280,768]{1,0:T(8,128)(2,1)}, bf16[1280,3072]{1,0:T(8,128)(2,1)...) custom-call(s32[5,4]{1,0:T(8,128)} %pad_add_fusion.spans, ...), custom_call_target="tpu_custom_call" | custom-call | tf_op jit(solution)/shard_map/forward_gather/pallas_call | solution.py:883
  109.1 1.2 slice.9
  110.3 19.8 %contrast.1 = (f32[16,768]{1,0:T(8,128)}, f32[5,8,768]{2,1,0:T(8,128)}, f32[8,128]{1,0:T(8,128)}) custom-call(f32[5,8,768]{2,1,0:T(8,128)} %get-tuple-element.99.cls_ref, bf16[16,768]{1,0:T(8,128)(2,1)} %q_ref.1, s32[16]{0:T(128)} %pos_ref.1), custom_call_target="tpu_custom_call" | custom-call | tf_op jit(solution)/shard_map/contrast/pallas_call | solution.py:495
  130.1 1.6 collective-permute-start
  132.3 1.4 pad_maximum_fusion.1.cot_ref
  133.7 16.4 %out_back.1 = (f32[1280,768]{1,0:T(8,128)}, f32[8,768]{1,0:T(8,128)}, bf16[2,768,1536]{2,1,0:T(8,128)(2,1)}) custom-call(bf16[1280,768]{1,0:T(8,128)(2,1)} %pad_maximum_fusion.1.cot_ref, f32[5,8,768]{2,1,0:T(8,128)} %get-tuple-element.100.lead_ref, f32[1280,768]{1,0:T(8,128)} %get-tuple-element.101.n2_ref, f32[1280,1]{1,0:T(8,128)} %get-tuple-element.102.r2_ref, ...), custom_call_target="tpu_custom_call" | custom-call | flops 6039797760 | bytes 33554432 | tf_op jit(solution)/shard_map/out_back/pallas_call | solution.py:1808
  150.1 0.0 collective-permute-done.refs_1_
  150.1 0.0 copy-start.2
  150.1 56.2 %feed_back_scatter.1 = (f32[1280,768]{1,0:T(8,128)}, bf16[1280,768]{1,0:T(8,128)(2,1)}, f32[8,768]{1,0:T(8,128)}, f32[8,3072]{1,0:T(8,128)}, bf16[2,768,384]{2,1...) custom-call(bf16[2,4,2,2,48,1536]{5,4,3,2,1,0:T(8,128)(2,1)} %bitcast.107, ...), custom_call_target="tpu_custom_call" | custom-call | flops 21139292160 | bytes 50331648 | tf_op jit(solution)/shard_map/feed_back_scatter/pallas_call | solution.py:1897
  206.3 0.0 copy-done.2
  206.3 100.8 %attend_last.1 = (f32[1280,768]{1,0:T(8,128)}, bf16[5,256,768]{2,1,0:T(8,128)(2,1)}, f32[48,1536]{1,0:T(8,128)}, f32[48,384]{1,0:T(8,128)}, f32[48,1152]{1,0:T(8...) custom-call(s32[5,4]{1,0:T(8,128)} %pad_add_fusion.spans, bf16[2,4,2,2,48,1536]{5,4,3,2,1,0:T(8,128)(2,1)} %bitcast.106, ...), custom_call_target="tpu_custom_call" | custom-call | flops 19629342720 | bytes 25165824 | tf_op jit(solution)/shard_map/attend_last/pallas_call | solution.py:1968
  307.1 0.0 copy-start.1
  307.1 13.1 %finish.1 = (bf16[512,768]{1,0:T(8,128)(2,1)}, bf16[2048,768]{1,0:T(8,128)(2,1)}, f32[512,768]{1,0:T(8,128)}, f32[2048,768]{1,0:T(8,128)}, f32[3,48,384]{2,1,0:T...) custom-call(bf16[1280,768]{1,0:T(8,128)(2,1)} %get-tuple-element.98., ...), custom_call_target="tpu_custom_call" | custom-call | tf_op jit(solution)/shard_map/finish/pallas_call | solution.py:1578
  320.2 1.3 fusion
  321.5 0.6 copy.69
  (6 shorter events, 0.0 us)
Async XLA Ops:
  0.7 0.8 copy-start
  6.6 2.2 copy-start.3
  6.6 2.3 copy-start.4
  130.1 20.0 %collective-permute-start = (bf16[512,768]{1,0:T(8,128)(2,1)S(1)}, bf16[512,768]{1,0:T(8,128)(2,1)S(1)}, u32[]{:S(2)}, u32[]{:S(2)}) collective-permute-start(bf16[512,768]{1,0:T(8,128)(2,1)S(1)} %slice.9), channel_id=1, source_target_pairs={{0,1},{1,0},{2,3},{3,2},{4,5},{5,4},{6,7},{7,6},{8,9},{9,8},{10,11... | collective-permute-start | bytes 2359304 | tf_op jit(solution)/shard_map/ppermute | solution.py:586
  150.1 56.2 %copy-start.2 = (bf16[512,768]{1,0:T(8,128)(2,1)}, bf16[512,768]{1,0:T(8,128)(2,1)S(1)}, u32[]{:S(2)}) copy-start(bf16[512,768]{1,0:T(8,128)(2,1)S(1)} %collective-permute-done.refs_1_) | copy-start | bytes 2359300
  307.1 14.4 %copy-start.5 = (f32[16,768]{1,0:T(8,128)S(1)}, f32[16,768]{1,0:T(8,128)}, u32[]{:S(2)}) copy-start(f32[16,768]{1,0:T(8,128)} %get-tuple-element.206) | copy-start | bytes 147460
  307.1 15.0 %copy-start.1 = (s32[8]{0:T(128)S(1)}, s32[8]{0:T(128)}, u32[]{:S(2)}) copy-start(s32[8]{0:T(128)} %param.37) | copy-start | bytes 100

commit v4 on v3

--- a/solution.py
+++ b/solution.py
@@ -78,10 +78,10 @@
     return jnp.where(lane < HEAD_DIM, low, high)
 
 
-def attend_half(half, weight, bias, visible, x_ref, qkv_ref, ctx_ref):
+def attend_half(half, weight, bias, visible, x, qkv_ref, ctx_ref):
     width = weight.shape[1] // 3
     base = half * 3 * width
-    projected = dot_nn(x_ref[...], weight) + bias
+    projected = dot_nn(x, weight) + bias
     qkv_ref[:, base : base + 3 * width] = projected.astype(jnp.bfloat16)
     for pair in range(width // PAIR):
         at = base + pair * PAIR
@@ -105,7 +105,7 @@
     visible = visible_keys(spans, step, rows, piece, 1)
     for half in range(w_ref.shape[0]):
         bias = bias_ref[:, half * 3 * width : (half + 1) * 3 * width]
-        attend_half(half, w_ref[half], bias, visible, x_ref, qkv_ref, ctx_ref)
+        attend_half(half, w_ref[half], bias, visible, x_ref[...], qkv_ref, ctx_ref)
 
 
 def feed_up(context, inputs, me_ref, scales_ref, bu_ref, outs):
@@ -171,7 +171,7 @@
 
 
 def out_back_kernel(
-    piece, chunks, cot_ref, lead_ref, n2_ref, r2_ref, scales_ref, g_ref, dr2_ref, vec_ref, grad_ref, turned_ref
+    piece, chunks, short_ref, long_ref, lead_ref, n2_ref, r2_ref, scales_ref, g_ref, dr2_ref, vec_ref, grad_ref, turned_ref
 ):
     step = pl.program_id(0)
 
@@ -181,7 +181,7 @@
 
     @pl.when(step < chunks)
     def _():
-        dout = cot_ref[...].astype(jnp.float32)
+        dout = jnp.where(step == 0, short_ref[...], long_ref[...]).astype(jnp.float32)
         rows = dout.shape[0]
         row = lax.broadcasted_iota(jnp.int32, dout.shape, 0)
         for index in range(rows // piece):
@@ -733,7 +733,7 @@
 
 
 def forward_gather_kernel(
-    piece, chunks, spans, mixing_ref, middle_ref, shrink_ref, offsets_ref, scales_ref, x_ref,
+    piece, chunks, spans, mixing_ref, middle_ref, shrink_ref, offsets_ref, scales_ref, short_ref, long_ref,
     qkv_ref, ctx_ref, hb_ref, g_ref, slope_ref, n1_ref, r1_ref, out_ref, n2_ref, r2_ref, lead_ref,
     mixing_out, middle_out, shrink_out,
     w_ref, me_ref, st_ref, both_ref, flat_ref, up_ref, ctx_all, g_all, hidden_all,
@@ -762,8 +762,12 @@
         target = (mixing_out, middle_out, shrink_out)[index]
         return pltpu.make_async_copy((w_ref, me_ref, st_ref)[index], target, stores.at[index])
 
-    rows = x_ref.shape[0]
+    rows = long_ref.shape[0]
     width = w_ref.shape[5] // 3
+
+    def tokens(first):
+        return jnp.where(step == first, short_ref[...], long_ref[...])
+
 
     @pl.when(step == 0)
     def _():
@@ -833,14 +837,14 @@
                 [bias[:, :width], jnp.zeros((1, width), jnp.float32), bias[:, width : 2 * width]],
                 axis=1,
             )
-            attend_half(half, weight, bias, visible, x_ref, qkv_ref, ctx_ref)
+            attend_half(half, weight, bias, visible, tokens(0), qkv_ref, ctx_ref)
         ctx_all[here(0), :] = ctx_ref[...]
 
     @pl.when(jnp.logical_and(step >= chunks, step < 2 * chunks))
     def _():
         outs = (hb_ref, g_ref, slope_ref, n1_ref, r1_ref)
         place = here(chunks)
-        hidden, activated = feed_up(ctx_all[place, :], x_ref[...], me_ref, scales_ref, up_ref, outs)
+        hidden, activated = feed_up(ctx_all[place, :], tokens(chunks), me_ref, scales_ref, up_ref, outs)
         hidden_all[place, :] = hidden
         for half in range(2):
             wide = st_ref.shape[5]
@@ -863,9 +867,8 @@
             store(index).wait()
 
 
-def forward_gather(piece, spans, inputs, owns, offsets, scales, chunk):
-    rows = inputs.shape[0]
-    chunks = rows // chunk
+def forward_gather(piece, spans, short_rows, long_rows, owns, offsets, scales, chunk, chunks):
+    rows = chunks * chunk
     halves = lax.axis_size("tensor")
     columns = halves * owns[0].shape[1]
     anywhere = pl.BlockSpec(memory_space=pl.ANY)
@@ -888,7 +891,7 @@
             *(full_spec(own.shape) for own in owns),
             full_spec((offsets.shape[0] // 128, 128)),
             full_spec(scales.shape),
-            pl.BlockSpec((chunk, D), lambda i: (jnp.minimum(i, 2 * chunks - 1) % chunks, 0)),
+            *half_specs(chunk, chunks, lambda i: jnp.minimum(i, 2 * chunks - 1) % chunks),
         ],
         out_specs=[spec(width, first) for width, _, first in shapes]
         + [pl.BlockSpec((1, 8, D), lambda i: (jnp.maximum(i - 2 * chunks, 0), 0, 0))]
@@ -915,7 +918,7 @@
             collective_id=3, has_side_effects=True, vmem_limit_bytes=big_vmem
         ),
         name="forward_gather",
-    )(spans, *owns, offsets.reshape(-1, 128), scales, inputs)
+    )(spans, *owns, offsets.reshape(-1, 128), scales, short_rows, long_rows)
     fulls = [full.reshape(halves, -1, full.shape[-1]) for full in outs[-3:]]
     return outs[:2], outs[2:-3], fulls
 
@@ -1335,7 +1338,9 @@
 
 
 def attend_last_kernel(piece, chunks, columns, spans, one_ref, two_ref, *refs):
-    ins, left_ref, done_ref, first_ref, second_ref, upward_ref, loss_ref = refs[:4], *refs[4:10]
+    ins, short_ref, long_ref, done_ref = refs[:4], *refs[4:7]
+    first_ref, second_ref, upward_ref, loss_ref = refs[7:11]
+    refs = refs[1:]
     dx_ref, low_out, one_out, two_out, last_out, total_ref, norm_ref = refs[10:17]
     dproj_ref, bias_ref, turned_ref, grad_ref, square_ref, low_ref, sends, lands = refs[17:25]
     rest = refs[25:]
@@ -1363,7 +1368,8 @@
         for part in late:
             part.start()
         square_ref[...] = jnp.zeros_like(square_ref)
-        turned_ref[...] = left_ref[...].T
+        turned_ref[:, : short_ref.shape[0]] = short_ref[...].T
+        turned_ref[:, short_ref.shape[0] :] = long_ref[...].T
 
     def ended(part):
         def action():
@@ -1596,6 +1602,16 @@
         name="finish",
     )(*halves_of_rows, *large, *grads, *scales, *offsets, total, norm, step_count)
     return outs[:4], outs[4:20], outs[20:24], [each.reshape(-1) for each in outs[24:28]], outs[28]
+
+
+def half_specs(chunk, chunks, at):
+    def long_at(i):
+        return (lax.axis_index("tensor") * (chunks - 1) + jnp.maximum(at(i) - 1, 0), 0)
+
+    return [
+        pl.BlockSpec((chunk, D), lambda i: (lax.axis_index("tensor"), 0)),
+        pl.BlockSpec((chunk, D), long_at),
+    ]
 
 
 def row_spec(rows, columns):
@@ -1678,7 +1694,6 @@
         axis=0,
     )
     inputs = own_half(short_tokens, long_tokens)
-    cotangent = own_half(short_cotangent, long_cotangent)
     bf16, f32 = jnp.bfloat16, jnp.float32
 
     def shaped(columns, dtype):
@@ -1692,11 +1707,13 @@
         (qkv, context), feed, (mixing_full, middle_full, shrink_full) = forward_gather(
             piece,
             spans,
-            inputs,
+            short_tokens.reshape(-1, D),
+            long_tokens.reshape(-1, D),
             (mixing_own, middle_own, shrink_own),
             offsets_weight,
             scales_weight,
             chunk,
+            chunks,
         )
     else:
         mixing_full, middle_full, shrink_full = (
@@ -1809,7 +1826,7 @@
         functools.partial(out_back_kernel, piece, chunks),
         grid=(chunks + FF // tile,),
         in_specs=[
-            chunk_spec(D),
+            *half_specs(chunk, chunks, lambda i: jnp.minimum(i, chunks - 1)),
             pl.BlockSpec((1, 8, D), lambda i: (jnp.minimum(i, chunks - 1), 0, 0)),
             chunk_spec(D),
             chunk_spec(1),
@@ -1835,7 +1852,10 @@
             flops=2 * rows * D * FF, bytes_accessed=32 * 1024 * 1024, transcendentals=0
         ),
         name="out_back",
-    )(cotangent, lead_rows, normed_second, rstd_second, scales_weight, activated)
+    )(
+        short_cotangent.reshape(-1, D),
+        long_cotangent.reshape(-1, D),
+        lead_rows, normed_second, rstd_second, scales_weight, activated)
     back_ins = [
         second_back,
         normed_first,
@@ -1953,7 +1973,7 @@
         late_count, last_count = wide // width + 1, 3
         last_whole = jax.ShapeDtypeStruct((halves, D, 3 * width), bf16)
         vector = jax.ShapeDtypeStruct((16, D), f32)
-        more = (inputs, shrink_sum, first_grad, second_grad, upward_grad, loss_rows)
+        more = (shrink_sum, first_grad, second_grad, upward_grad, loss_rows)
         small = (8, 128)
         out_shape = [
             shaped(D, f32),
@@ -1970,6 +1990,10 @@
                 grid=(chunks + 2 * last_count,),
                 in_specs=[smem, anywhere, anywhere]
                 + pair_in_specs
+                + [
+                    pl.BlockSpec((count * chunk, D), lambda i: (lax.axis_index("tensor"), 0), pipeline_mode=pl.Buffered(1))
+                    for count in (1, chunks - 1)
+                ]
                 + [full_spec(each.shape) for each in more],
                 out_specs=[chunk_spec(D), anywhere]
                 + [full_spec(each.shape) for each in out_shape[2:]],
@@ -2007,6 +2031,8 @@
                 spans,
                 *(scatter_input(part) for part in parts),
                 *pair_ins,
+                short_tokens.reshape(-1, D),
+                long_tokens.reshape(-1, D),
                 *more,
             )
         )

time: 323 us -> 318 us (0.985)
  transfers between devices with their start and end apart: 1 -> 1, of which waited for: 0 -> 1; matrix products, arithmetic and copies ran while one was open for 0% -> 0% of each run, Pallas kernels for 5% -> 5%
where the time goes in v4:
time: 318 us
  Pallas kernels  303 us (95%)
  other arithmetic  5.82 us (2%)
  local copies, waits for them, and re-layouts  4.57 us (1%)
    pallas_call x1, Pallas kernels, shards(): pl.pallas_call(functools.partial(attend_last_kernel, piece, chunks, width...  100 us
    pallas_call x1, Pallas kernels, forward_gather(): pl.pallas_call(functools.partial(forward_gather_kernel, piece, chunks), g...  97.7 us
    pallas_call x1, Pallas kernels, shards(): pl.pallas_call(functools.partial(feed_back_scatter_kernel, chunks, chunks...  55.8 us
    pallas_call x1, Pallas kernels, contrast(): pl.pallas_call(functools.partial(contrast_kernel, count, own, halves), in...  19.8 us
    pallas_call x1, Pallas kernels, shards(): pl.pallas_call(functools.partial(out_back_kernel, piece, chunks), grid=(c...  16.5 us
    pallas_call x1, Pallas kernels, finish(): pl.pallas_call(functools.partial(finish_kernel, chunk, chunks, rates, pas...  13.1 us
  transfers between devices with their start and end apart: 1, of which 1 were waited for; matrix products, arithmetic and copies ran while one was open for 0% of the time, Pallas kernels for 5%

profile of v4, /device:TPU:0, one launch (start us, length us, event | category | flops | bytes accessed | tf_op | source)
XLA Modules:
  0.0 317.7 jit_solution(5724468626422017056)
XLA Ops:
  0.7 0.0 copy-start
  0.7 0.7 dynamic_slice.7
  1.4 0.0 copy-done
  1.4 0.1 dynamic-slice_bitcast_fusion
  1.5 0.9 convert_bitcast_fusion
  2.5 0.7 copy.66
  3.1 1.0 convert.7
  4.1 0.9 bitcast_convert_fusion.1
  5.0 1.6 bitcast_convert_fusion.shrink_ref
  6.6 0.1 broadcast_subtract_fusion
  6.7 0.6 pad_add_fusion.spans
  7.3 0.7 pad_maximum_fusion.middle_ref
  8.0 97.7 %forward_gather.1 = (bf16[1280,2304]{1,0:T(8,128)(2,1)}, bf16[1280,768]{1,0:T(8,128)(2,1)}, bf16[1280,768]{1,0:T(8,128)(2,1)}, bf16[1280,3072]{1,0:T(8,128)(2,1)...) custom-call(s32[5,4]{1,0:T(8,128)} %pad_add_fusion.spans, ...), custom_call_target="tpu_custom_call" | custom-call | tf_op jit(solution)/shard_map/forward_gather/pallas_call | solution.py:886
  105.7 1.2 slice.9
  106.9 19.8 %contrast.1 = (f32[16,768]{1,0:T(8,128)}, f32[5,8,768]{2,1,0:T(8,128)}, f32[8,128]{1,0:T(8,128)}) custom-call(f32[5,8,768]{2,1,0:T(8,128)} %get-tuple-element.99.cls_ref, bf16[16,768]{1,0:T(8,128)(2,1)} %q_ref.1, s32[16]{0:T(128)} %pos_ref.1), custom_call_target="tpu_custom_call" | custom-call | tf_op jit(solution)/shard_map/contrast/pallas_call | solution.py:495
  126.7 1.6 collective-permute-start
  129.0 16.5 %out_back.1 = (f32[1280,768]{1,0:T(8,128)}, f32[8,768]{1,0:T(8,128)}, bf16[2,768,1536]{2,1,0:T(8,128)(2,1)}) custom-call(bf16[512,768]{1,0:T(8,128)(2,1)} %bitcast.90, bf16[2048,768]{1,0:T(8,128)(2,1)} %bitcast.87, f32[5,8,768]{2,1,0:T(8,128)} %get-tuple-element.100.lead_ref, f32[1280,768]{1,0:T(8,128)} %get-tuple-element.101.n2_ref, ...), custom_call_target="tpu_custom_call" | custom-call | flops 6039797760 | bytes 33554432 | tf_op jit(solution)/shard_map/out_back/pallas_call | solution.py:1825
  145.5 0.9 collective-permute-done.refs_1_
  146.3 0.0 copy-start.2
  146.3 55.8 %feed_back_scatter.1 = (f32[1280,768]{1,0:T(8,128)}, bf16[1280,768]{1,0:T(8,128)(2,1)}, f32[8,768]{1,0:T(8,128)}, f32[8,3072]{1,0:T(8,128)}, bf16[2,768,384]{2,1...) custom-call(bf16[2,4,2,2,48,1536]{5,4,3,2,1,0:T(8,128)(2,1)} %bitcast.109, ...), custom_call_target="tpu_custom_call" | custom-call | flops 21139292160 | bytes 50331648 | tf_op jit(solution)/shard_map/feed_back_scatter/pallas_call | solution.py:1917
  202.1 0.0 copy-done.2
  202.2 100.5 %attend_last.1 = (f32[1280,768]{1,0:T(8,128)}, bf16[5,256,768]{2,1,0:T(8,128)(2,1)}, f32[48,1536]{1,0:T(8,128)}, f32[48,384]{1,0:T(8,128)}, f32[48,1152]{1,0:T(8...) custom-call(s32[5,4]{1,0:T(8,128)} %pad_add_fusion.spans, bf16[2,4,2,2,48,1536]{5,4,3,2,1,0:T(8,128)(2,1)} %bitcast.108, ...), custom_call_target="tpu_custom_call" | custom-call | flops 19629342720 | bytes 25165824 | tf_op jit(solution)/shard_map/attend_last/pallas_call | solution.py:1988
  302.7 0.0 copy-start.1
  302.7 0.0 copy-start.3
  302.7 13.1 %finish.1 = (bf16[512,768]{1,0:T(8,128)(2,1)}, bf16[2048,768]{1,0:T(8,128)(2,1)}, f32[512,768]{1,0:T(8,128)}, f32[2048,768]{1,0:T(8,128)}, f32[3,48,384]{2,1,0:T...) custom-call(bf16[1280,768]{1,0:T(8,128)(2,1)} %get-tuple-element.98., ...), custom_call_target="tpu_custom_call" | custom-call | tf_op jit(solution)/shard_map/finish/pallas_call | solution.py:1584
  315.8 1.3 fusion
  317.1 0.0 copy-done.3
  317.1 0.6 copy.69
  317.7 0.0 copy-done.1
  (1 shorter events, 0.0 us)
Async XLA Ops:
  0.7 0.8 copy-start
  126.7 19.6 %collective-permute-start = (bf16[512,768]{1,0:T(8,128)(2,1)S(1)}, bf16[512,768]{1,0:T(8,128)(2,1)S(1)}, u32[]{:S(2)}, u32[]{:S(2)}) collective-permute-start(bf16[512,768]{1,0:T(8,128)(2,1)S(1)} %slice.9), channel_id=1, source_target_pairs={{0,1},{1,0},{2,3},{3,2},{4,5},{5,4},{6,7},{7,6},{8,9},{9,8},{10,11... | collective-permute-start | bytes 2359304 | tf_op jit(solution)/shard_map/ppermute | solution.py:586
  146.3 55.8 %copy-start.2 = (bf16[512,768]{1,0:T(8,128)(2,1)}, bf16[512,768]{1,0:T(8,128)(2,1)S(1)}, u32[]{:S(2)}) copy-start(bf16[512,768]{1,0:T(8,128)(2,1)S(1)} %collective-permute-done.refs_1_) | copy-start | bytes 2359300
  302.7 15.0 %copy-start.1 = (s32[8]{0:T(128)S(1)}, s32[8]{0:T(128)}, u32[]{:S(2)}) copy-start(s32[8]{0:T(128)} %param.37) | copy-start | bytes 100
  302.7 14.4 %copy-start.3 = (f32[16,768]{1,0:T(8,128)S(1)}, f32[16,768]{1,0:T(8,128)}, u32[]{:S(2)}) copy-start(f32[16,768]{1,0:T(8,128)} %get-tuple-element.202) | copy-start | bytes 147460

commit v5 on v4

--- a/solution.py
+++ b/solution.py
@@ -1298,7 +1298,7 @@
             (due, part.cores_ready),
             (due + link + 2, part.first_ready),
             (due + 2 * link + 4, part.second_ready),
-            (due + 2 * link + 7, ended(part)),
+            (due + 2 * link + 47, ended(part)),
         ]
     return actions
 

time: 318 us -> 310 us (0.975)
  Pallas kernels: 303 us -> 295 us
    pallas_call x1, Pallas kernels: 100 us -> 96.1 us  [shards(): pl.pallas_call(functools.partial(attend_last_kernel, piece, chunks, width...]
    pallas_call x1, Pallas kernels: 55.8 us -> 51.5 us  [shards(): pl.pallas_call(functools.partial(feed_back_scatter_kernel, chunks, chunks...]
where the time goes in v5:
time: 310 us; the launch traced here: 309 us
  Pallas kernels  295 us (95%)
  other arithmetic  5.82 us (2%)
  local copies, waits for them, and re-layouts  4.57 us (1%)
    pallas_call x1, Pallas kernels, forward_gather(): pl.pallas_call(functools.partial(forward_gather_kernel, piece, chunks), g...  97.7 us
    pallas_call x1, Pallas kernels, shards(): pl.pallas_call(functools.partial(attend_last_kernel, piece, chunks, width...  96.1 us
    pallas_call x1, Pallas kernels, shards(): pl.pallas_call(functools.partial(feed_back_scatter_kernel, chunks, chunks...  51.5 us
    pallas_call x1, Pallas kernels, contrast(): pl.pallas_call(functools.partial(contrast_kernel, count, own, halves), in...  19.8 us
    pallas_call x1, Pallas kernels, shards(): pl.pallas_call(functools.partial(out_back_kernel, piece, chunks), grid=(c...  16.5 us
    pallas_call x1, Pallas kernels, finish(): pl.pallas_call(functools.partial(finish_kernel, chunk, chunks, rates, pas...  13.1 us
  transfers between devices with their start and end apart: 1, of which 1 were waited for; matrix products, arithmetic and copies ran while one was open for 0% of the time, Pallas kernels for 5%

profile of v5, /device:TPU:0, one launch (start us, length us, event | category | flops | bytes accessed | tf_op | source)
XLA Modules:
  0.0 308.9 jit_solution(663187219452673224)
XLA Ops:
  0.7 0.0 copy-start
  0.7 0.7 dynamic_slice.7
  1.4 0.0 copy-done
  1.4 0.1 dynamic-slice_bitcast_fusion
  1.5 0.9 convert_bitcast_fusion
  2.5 0.7 copy.66
  3.1 1.0 convert.7
  4.1 0.9 bitcast_convert_fusion.1
  5.0 1.6 bitcast_convert_fusion.shrink_ref
  6.6 0.1 broadcast_subtract_fusion
  6.7 0.6 pad_add_fusion.spans
  7.3 0.7 pad_maximum_fusion.middle_ref
  8.0 97.7 %forward_gather.1 = (bf16[1280,2304]{1,0:T(8,128)(2,1)}, bf16[1280,768]{1,0:T(8,128)(2,1)}, bf16[1280,768]{1,0:T(8,128)(2,1)}, bf16[1280,3072]{1,0:T(8,128)(2,1)...) custom-call(s32[5,4]{1,0:T(8,128)} %pad_add_fusion.spans, ...), custom_call_target="tpu_custom_call" | custom-call | tf_op jit(solution)/shard_map/forward_gather/pallas_call | solution.py:886
  105.7 1.2 slice.9
  106.9 19.8 %contrast.1 = (f32[16,768]{1,0:T(8,128)}, f32[5,8,768]{2,1,0:T(8,128)}, f32[8,128]{1,0:T(8,128)}) custom-call(f32[5,8,768]{2,1,0:T(8,128)} %get-tuple-element.99.cls_ref, bf16[16,768]{1,0:T(8,128)(2,1)} %q_ref.1, s32[16]{0:T(128)} %pos_ref.1), custom_call_target="tpu_custom_call" | custom-call | tf_op jit(solution)/shard_map/contrast/pallas_call | solution.py:495
  126.7 1.6 collective-permute-start
  129.0 16.5 %out_back.1 = (f32[1280,768]{1,0:T(8,128)}, f32[8,768]{1,0:T(8,128)}, bf16[2,768,1536]{2,1,0:T(8,128)(2,1)}) custom-call(bf16[512,768]{1,0:T(8,128)(2,1)} %bitcast.90, bf16[2048,768]{1,0:T(8,128)(2,1)} %bitcast.87, f32[5,8,768]{2,1,0:T(8,128)} %get-tuple-element.100.lead_ref, f32[1280,768]{1,0:T(8,128)} %get-tuple-element.101.n2_ref, ...), custom_call_target="tpu_custom_call" | custom-call | flops 6039797760 | bytes 33554432 | tf_op jit(solution)/shard_map/out_back/pallas_call | solution.py:1825
  145.5 0.9 collective-permute-done.refs_1_
  146.3 0.0 copy-start.2
  146.3 51.5 %feed_back_scatter.1 = (f32[1280,768]{1,0:T(8,128)}, bf16[1280,768]{1,0:T(8,128)(2,1)}, f32[8,768]{1,0:T(8,128)}, f32[8,3072]{1,0:T(8,128)}, bf16[2,768,384]{2,1...) custom-call(bf16[2,4,2,2,48,1536]{5,4,3,2,1,0:T(8,128)(2,1)} %bitcast.109, ...), custom_call_target="tpu_custom_call" | custom-call | flops 21139292160 | bytes 50331648 | tf_op jit(solution)/shard_map/feed_back_scatter/pallas_call | solution.py:1917
  197.8 0.0 copy-done.2
  197.8 96.1 %attend_last.1 = (f32[1280,768]{1,0:T(8,128)}, bf16[5,256,768]{2,1,0:T(8,128)(2,1)}, f32[48,1536]{1,0:T(8,128)}, f32[48,384]{1,0:T(8,128)}, f32[48,1152]{1,0:T(8...) custom-call(s32[5,4]{1,0:T(8,128)} %pad_add_fusion.spans, bf16[2,4,2,2,48,1536]{5,4,3,2,1,0:T(8,128)(2,1)} %bitcast.108, ...), custom_call_target="tpu_custom_call" | custom-call | flops 19629342720 | bytes 25165824 | tf_op jit(solution)/shard_map/attend_last/pallas_call | solution.py:1988
  293.9 0.0 copy-start.1
  293.9 0.0 copy-start.3
  293.9 13.1 %finish.1 = (bf16[512,768]{1,0:T(8,128)(2,1)}, bf16[2048,768]{1,0:T(8,128)(2,1)}, f32[512,768]{1,0:T(8,128)}, f32[2048,768]{1,0:T(8,128)}, f32[3,48,384]{2,1,0:T...) custom-call(bf16[1280,768]{1,0:T(8,128)(2,1)} %get-tuple-element.98., ...), custom_call_target="tpu_custom_call" | custom-call | tf_op jit(solution)/shard_map/finish/pallas_call | solution.py:1584
  307.0 1.3 fusion
  308.3 0.0 copy-done.3
  308.3 0.6 copy.69
  308.9 0.0 copy-done.1
  (1 shorter events, 0.0 us)
Async XLA Ops:
  0.7 0.8 copy-start
  126.7 19.6 %collective-permute-start = (bf16[512,768]{1,0:T(8,128)(2,1)S(1)}, bf16[512,768]{1,0:T(8,128)(2,1)S(1)}, u32[]{:S(2)}, u32[]{:S(2)}) collective-permute-start(bf16[512,768]{1,0:T(8,128)(2,1)S(1)} %slice.9), channel_id=1, source_target_pairs={{0,1},{1,0},{2,3},{3,2},{4,5},{5,4},{6,7},{7,6},{8,9},{9,8},{10,11... | collective-permute-start | bytes 2359304 | tf_op jit(solution)/shard_map/ppermute | solution.py:586
  146.3 51.5 %copy-start.2 = (bf16[512,768]{1,0:T(8,128)(2,1)}, bf16[512,768]{1,0:T(8,128)(2,1)S(1)}, u32[]{:S(2)}) copy-start(bf16[512,768]{1,0:T(8,128)(2,1)S(1)} %collective-permute-done.refs_1_) | copy-start | bytes 2359300
  293.9 15.0 %copy-start.1 = (s32[8]{0:T(128)S(1)}, s32[8]{0:T(128)}, u32[]{:S(2)}) copy-start(s32[8]{0:T(128)} %param.37) | copy-start | bytes 100
  293.9 14.4 %copy-start.3 = (f32[16,768]{1,0:T(8,128)S(1)}, f32[16,768]{1,0:T(8,128)}, u32[]{:S(2)}) copy-start(f32[16,768]{1,0:T(8,128)} %get-tuple-element.202) | copy-start | bytes 147460
